TPU v7x, 32 devices: a whole 2x2x4 slice. The times are simulated.
32 devices in a mesh: ctx: 16 (over z, y, x), fsdp: 2 (over core).
Axes of the slice: x: 2, y: 2, z: 4, core: 2. Of those that a mesh axis runs over, the one named last changes fastest.
Arguments:
- hidden_in: bfloat16 [2, 2048, 2048], P('fsdp', 'ctx'), may hold values from -6 to 6
- gain_attn: bfloat16 [2048], P(('ctx', 'fsdp')), may hold values from 0.099609375 to 1.8984375
- w_query: bfloat16 [2048, 3072], P(('ctx', 'fsdp')), may hold values from -0.25 to 0.25
- w_kv_down: bfloat16 [2048, 576], P(('ctx', 'fsdp')), may hold values from -0.125 to 0.125
- gain_kv: bfloat16 [512], P(('ctx', 'fsdp')), may hold values from 0.099609375 to 1.8984375
- w_kv_up: bfloat16 [512, 4096], P(('ctx', 'fsdp')), may hold values from -0.25 to 0.25
- w_out: bfloat16 [2048, 2048], P(('ctx', 'fsdp')), may hold values from -0.5 to 0.5
- gain_ffn: bfloat16 [2048], P(('ctx', 'fsdp')), may hold values from 0.099609375 to 1.8984375
- w_router: bfloat16 [2048, 16], P(('ctx', 'fsdp')), may hold values from -0.0625 to 0.0625
- shared_gate: bfloat16 [2048, 2816], P(('ctx', 'fsdp')), may hold values from -0.125 to 0.125
- shared_up: bfloat16 [2048, 2816], P(('ctx', 'fsdp')), may hold values from -0.125 to 0.125
- shared_down: bfloat16 [2816, 2048], P(('ctx', 'fsdp')), may hold values from -0.109375 to 0.109375
- expert_gate: bfloat16 [16, 2048, 1408], P('ctx', None, 'fsdp'), may hold values from -0.125 to 0.125
- expert_up: bfloat16 [16, 2048, 1408], P('ctx', None, 'fsdp'), may hold values from -0.125 to 0.125
- expert_down: bfloat16 [16, 2048, 1408], P('ctx', None, 'fsdp'), may hold values from -0.3125 to 0.3125
- routes: int32 [2, 2048, 6], P('fsdp', 'ctx'), may hold values from 0 to 15, all different within a row; in each aligned block of 128 rows (0 to 127, 128 to 255, ..., all dimensions but the last counted through in order) at most 64 rows name the same one
- cotangent: bfloat16 [2, 2048, 2048], P('fsdp', 'ctx'), may hold values from -6 to 6
Outputs:
- hidden_out: bfloat16 [2, 2048, 2048], P('fsdp', 'ctx')
- grad_hidden_in: float32 [2, 2048, 2048], P('fsdp', 'ctx')
- grad_gain_attn: float32 [2048], P(('ctx', 'fsdp'))
- grad_w_query: float32 [2048, 3072], P(('ctx', 'fsdp'))
- grad_w_kv_down: float32 [2048, 576], P(('ctx', 'fsdp'))
- grad_gain_kv: float32 [512], P(('ctx', 'fsdp'))
- grad_w_kv_up: float32 [512, 4096], P(('ctx', 'fsdp'))
- grad_w_out: float32 [2048, 2048], P(('ctx', 'fsdp'))
- grad_gain_ffn: float32 [2048], P(('ctx', 'fsdp'))
- grad_w_router: float32 [2048, 16], P(('ctx', 'fsdp'))
- grad_shared_gate: float32 [2048, 2816], P(('ctx', 'fsdp'))
- grad_shared_up: float32 [2048, 2816], P(('ctx', 'fsdp'))
- grad_shared_down: float32 [2816, 2048], P(('ctx', 'fsdp'))
- grad_expert_gate: float32 [16, 2048, 1408], P('ctx', None, 'fsdp')
- grad_expert_up: float32 [16, 2048, 1408], P('ctx', None, 'fsdp')
- grad_expert_down: float32 [16, 2048, 1408], P('ctx', None, 'fsdp')
Inputs may be any that keep to these rules, and one draw needn't show every extreme that they name: `routes`: each token names 6 different experts. In each aligned block of 128 tokens of a sequence (the tokens of one device), no expert is named by more than 64 tokens.
All inputs are finite; a program needn't handle non-finite values.
Results may differ from a plain program's by a relative error of at most 0.023.
Values may be sent and summed in bfloat16 or wider, within the bound.
No kernel may reach another device: no remote copies, remote signals or barrier semaphores. Data moves between devices by JAX's collectives and lax.ppermute only.
A program may use at most 448 MiB of HBM per device.

v0:
```python
import functools
import math

import jax
import jax.numpy as jnp
from jax import lax
from jax.experimental import pallas as pl
from jax.experimental.pallas import tpu as pltpu
from jax.sharding import PartitionSpec as P

HEADS = 16
NOPE = 128
ROPE = 64
VHEAD = 128
KVR = 512
TOP = 6
QK = NOPE + ROPE

epsilon = 1e-06
rope_base = 10000.0
masked_score = -1e30
score_scale = 1.0 / math.sqrt(QK)

bf16 = jnp.bfloat16
f32 = jnp.float32


def mm(left, right):
    return jnp.dot(left, right, preferred_element_type=f32)


def mm_nt(left, right):
    return lax.dot_general(left, right, (((1,), (1,)), ((), ())), preferred_element_type=f32)


def mm_tn(left, right):
    return lax.dot_general(left, right, (((0,), (0,)), ((), ())), preferred_element_type=f32)


def rms_factor(values):
    return lax.rsqrt(jnp.mean(values * values, axis=-1, keepdims=True) + epsilon)


def rms_backward(values, factor, gain, upstream):
    weighted = upstream * gain
    inner_mean = jnp.mean(weighted * values, axis=-1, keepdims=True)
    grad_in = factor * weighted - values * (factor * factor * factor) * inner_mean
    grad_gain = jnp.sum(upstream * values * factor, axis=0)
    return (grad_in, grad_gain)


def rope_tables(positions):
    half_width = ROPE // 2
    frequency = jnp.exp(jnp.arange(half_width, dtype=f32) * (-math.log(rope_base) / half_width))
    angles = positions.astype(f32)[:, None] * frequency[None, :]
    angles = jnp.concatenate([angles, angles], axis=-1)
    return (jnp.cos(angles), jnp.sin(angles))


def rotate(values, cosine, sine):
    half_width = values.shape[-1] // 2
    turned = jnp.concatenate([-values[..., half_width:], values[..., :half_width]], axis=-1)
    return values * cosine + turned * sine


def unrotate(upstream, cosine, sine):
    half_width = upstream.shape[-1] // 2
    rotated = upstream * sine
    turned = jnp.concatenate([rotated[..., half_width:], -rotated[..., :half_width]], axis=-1)
    return upstream * cosine + turned


def swiglu(gate_pre, up_pre):
    return (jax.nn.silu(gate_pre) * up_pre).astype(bf16)


def swiglu_grads(gate_pre, up_pre, grad_mid):
    squash = jax.nn.sigmoid(gate_pre)
    grad_gate = grad_mid * up_pre * squash * (1.0 + gate_pre * (1.0 - squash))
    grad_up = grad_mid * (gate_pre * squash)
    return (grad_gate.astype(bf16), grad_up.astype(bf16))


def exchanges():
    return lax.axis_size("ctx") == 16


def hop(value, mask):
    return lax.ppermute(value, "ctx", [(i, i ^ mask) for i in range(16)])


def together(*values):
    return lax.optimization_barrier(values)


def gather_ctx(block, *stages):
    held = None
    if not exchanges():
        for stage in stages:
            held = stage(held)
        whole = lax.all_gather(block, "ctx", axis=0)
        at = lambda piece, mask: [(whole, 8 * piece + 4 * group + mask) for group in (0, 1)]
        return [[at(piece, mask) for mask in range(4)] for piece in range(whole.shape[0] // 8)], held

    def end(number, *hops):
        nonlocal held
        if number < len(stages):
            held = stages[number](held)
        held, *hops = together(held, *hops)
        return hops

    near, far, one, two = end(0, *(hop(block, mask) for mask in (4, 8, 1, 2)))
    far_near, near_one, near_two, three = end(
        1, hop(far, 4), hop(near, 1), hop(near, 2), hop(two, 1)
    )
    pair = jnp.stack([far, far_near])
    near_three, far_one, far_two = end(2, hop(three, 4), hop(pair, 1), hop(pair, 2))
    far_three = end(3, hop(far_two[0], 1), hop(far_one[1], 2))
    pairs = [(block, near), (one, near_one), (two, near_two), (three, near_three)]
    alone = lambda values: [(value[None], 0) for value in values]
    both = lambda values: [(values, 0), (values, 1)]
    return [
        [alone(values) for values in pairs],
        [both(pair), both(far_one), both(far_two), alone(far_three)],
    ], held


def block_operands(piece):
    blocks = [block for mask in piece for block in mask]
    specs = [
        pl.BlockSpec(
            (1, *array.shape[1:]), lambda i, base, at=at: (at, 0, 0), pipeline_mode=pl.Buffered(1)
        )
        for array, at in blocks
    ]
    return [array for array, _ in blocks], specs


def block_of_step(refs, mask):
    return jnp.where(pl.program_id(0) == 0, refs[2 * mask][0], refs[2 * mask + 1][0])


def plus(*values):
    return sum(value.astype(f32) for value in values)


def plane_hops(pieces):
    return [[hop(value, mask) for mask, value in enumerate(piece) if mask] for piece in pieces]


def line_hops(pieces, arrived):
    near, far = (plus(piece[0], *values) for piece, values in zip(pieces, arrived))
    sent = ((near[1], 4), (far[0], 8), (far[1], 12))
    return near[0], [hop(value.astype(bf16), mask) for value, mask in sent]


def whole_sum(pieces):
    whole = jnp.stack([jnp.stack(piece, axis=1) for piece in pieces])
    whole = whole.reshape(-1, *whole.shape[3:])
    return lax.psum_scatter(whole, "ctx", scatter_dimension=0).astype(f32)


def scatter_ctx(pieces, beside_plane=(), beside_line=(), near=None):
    if not exchanges():
        return whole_sum(pieces), beside_plane, beside_line
    near = near or plane_hops(pieces[:1])
    near, far, beside_plane = together(near, plane_hops(pieces[1:]), beside_plane)
    own, arrived = line_hops(pieces, [*near, *far])
    arrived, beside_line = together(arrived, beside_line)
    return plus(own, *arrived), beside_plane, beside_line


def piece_place(piece):
    if not exchanges():
        return jnp.array([piece, 0, 0], jnp.int32)
    own = lax.axis_index("ctx")
    return jnp.stack([(own >> 3) ^ piece, own & 3, (own >> 2) & 1])


def piece_order():
    masks = [p * 8 + g * 4 + m for p in (0, 1) for m in range(4) for g in (0, 1)]
    return jnp.array(masks, jnp.int32) ^ lax.axis_index("ctx")


def in_pieces(blocks):
    if not exchanges():
        groups = blocks.reshape(-1, 2, 4, *blocks.shape[1:])
        return [[piece[:, mask] for mask in range(4)] for piece in groups]
    ordered = jnp.take(blocks, piece_order(), axis=0, mode="clip")
    ordered = ordered.reshape(2, 4, 2, *blocks.shape[1:])
    return [[ordered[p, m] for m in range(4)] for p in (0, 1)]


def swap_cores(value):
    return lax.ppermute(value, "fsdp", [(0, 1), (1, 0)])


def gather_fsdp(block):
    if lax.axis_size("fsdp") == 2:
        return [block, swap_cores(block)]
    whole = lax.all_gather(block, "fsdp", axis=0)
    return [whole[i] for i in range(lax.axis_size("fsdp"))]


def scatter_fsdp(parts):
    if lax.axis_size("fsdp") == 2:
        return parts[0].astype(f32) + swap_cores(parts[1].astype(bf16)).astype(f32)
    stacked = jnp.stack([part.astype(bf16) for part in parts])
    return lax.psum_scatter(stacked, "fsdp", scatter_dimension=0).astype(f32)


def in_fsdp_order(parts):
    if lax.axis_size("fsdp") == 2:
        low = lax.axis_index("fsdp") == 0
        return [jnp.where(low, parts[0], parts[1]), jnp.where(low, parts[1], parts[0])]
    return parts


def to_owner(blocks):
    return lax.all_to_all(blocks, "ctx", split_axis=0, concat_axis=0, tiled=True)


LANES = 128
WIDE = NOPE + 2 * ROPE
megabytes = 1024 * 1024


def turn_columns(weights):
    half = weights.shape[-1] // 2
    return jnp.concatenate([-weights[..., half:], weights[..., :half]], axis=-1)


def project_kernel(base_ref, *refs):
    token_refs = refs[:8]
    gain_ref, kv_gain_ref, table_ref, query_w_ref, reduce_ref, expand_ref = refs[8:14]
    normed_ref, query_ref, key_ref, value_ref, latent_ref = refs[-5:]
    part = token_refs[0].shape[1]
    first_half = lax.broadcasted_iota(jnp.int32, (part, LANES), 1) < ROPE
    for mask in range(4):
        span = pl.ds(pl.multiple_of((mask ^ base_ref[1]) * part, part), part)
        tokens = block_of_step(token_refs, mask).astype(f32)
        normed = (tokens * rms_factor(tokens) * gain_ref[...]).astype(bf16)
        normed_ref[span, :] = normed
        table = table_ref[span, :]

        def rope(values):
            scaled = values * table
            return scaled + pltpu.roll(scaled, ROPE, 1)

        queries = mm(normed, query_w_ref[...])
        query_ref[span, :NOPE] = queries[:, :NOPE].astype(bf16)
        query_ref[span, NOPE:] = jnp.where(first_half, rope(queries[:, NOPE:]), 0.0).astype(bf16)
        compressed = mm(normed, reduce_ref[...])
        raw = compressed[:, :KVR]
        latent = (raw * rms_factor(raw) * kv_gain_ref[...]).astype(bf16)
        latent_ref[span, :] = latent
        expanded = mm(latent, expand_ref[...]).astype(bf16)
        key_ref[span, :NOPE] = expanded[:, :NOPE]
        key_ref[span, NOPE:] = rope(compressed[:, KVR:]).astype(bf16)
        value_ref[span, :] = expanded[:, NOPE:]


def project(pieces, gain, kv_gain, table, query_w, reduce_w, expand):
    length, width = table.shape[0], query_w.shape[0]
    widths = [width, WIDE, WIDE, VHEAD, KVR]
    held = []
    for piece, blocks in enumerate(pieces):
        blocks, block_specs = block_operands(blocks)
        steps, part = 2, blocks[0].shape[1]
        tile = 4 * part
        at = lambda i, base: (base[0] * 2 + (i ^ base[2]), 0)
        fixed = lambda i, base: (0, 0)
        whole = lambda shape: pl.BlockSpec(shape, fixed, pipeline_mode=pl.Buffered(1))
        count = steps * tile
        held = pl.pallas_call(
            project_kernel,
            grid_spec=pltpu.PrefetchScalarGridSpec(
                num_scalar_prefetch=1,
                grid=(steps,),
                in_specs=block_specs
                + [
                    whole((1, width)),
                    whole((1, KVR)),
                    pl.BlockSpec((tile, LANES), at),
                    whole((width, WIDE)),
                    whole((width, KVR + LANES)),
                    whole((KVR, NOPE + VHEAD)),
                ]
                + [pl.BlockSpec(memory_space=pl.ANY)] * len(held),
                out_specs=[pl.BlockSpec((tile, w), at) for w in widths],
            ),
            out_shape=[jax.ShapeDtypeStruct((length, w), bf16) for w in widths],
            input_output_aliases={15 + i: i for i in range(len(held))},
            compiler_params=pltpu.CompilerParams(vmem_limit_bytes=56 * megabytes),
            cost_estimate=pl.CostEstimate(
                flops=2 * count * width * (WIDE + KVR + LANES),
                bytes_accessed=4 * count * width + 2 * width * (WIDE + KVR + LANES),
                transcendentals=0,
            ),
            name="project",
        )(piece_place(piece), *blocks, gain, kv_gain, table, query_w, reduce_w, expand, *held)
    return held


def attend_kernel(key_tile, reach, pos_ref, query_ref, key_ref, value_ref, out_ref, low_ref, lse_ref):
    queries = query_ref[...]
    rows = queries.shape[0]
    positions = pos_ref[...]
    tiles = (pl.program_id(0) + 1) * reach // key_tile

    def step(index, carry):
        top, total, running = carry
        keys = key_ref[pl.ds(index * key_tile, key_tile), :]
        values = value_ref[pl.ds(index * key_tile, key_tile), :]
        scores = mm_nt(queries, keys) * score_scale
        key_pos = index * key_tile + lax.broadcasted_iota(jnp.int32, scores.shape, 1)
        scores = jnp.where(key_pos <= positions, scores, masked_score)
        new_top = jnp.maximum(top, jnp.max(scores, axis=-1, keepdims=True))
        weights = jnp.exp(scores - new_top)
        shrink = jnp.exp(top - new_top)
        total = total * shrink + jnp.sum(weights, axis=-1, keepdims=True)
        running = running * shrink + mm(weights.astype(bf16), values)
        return (new_top, total, running)

    start = (
        jnp.full((rows, 1), masked_score, f32),
        jnp.zeros((rows, 1), f32),
        jnp.zeros((rows, VHEAD), f32),
    )
    top, total, running = lax.fori_loop(0, tiles, step, start)
    outcome = running / total
    out_ref[...] = outcome
    low_ref[...] = outcome.astype(bf16)
    lse_ref[...] = top + jnp.log(total)


def attend_grad_kernel(
    key_tile, reach, pos_ref, table_ref, query_ref, key_ref, value_ref, out_ref, lse_ref, grad_ref,
    expand_ref, dquery_ref, dexpand_ref, dlatent_ref, dkey_ref, dvalue_ref,
):
    @pl.when(pl.program_id(0) == 0)
    def clear():
        dkey_ref[...] = jnp.zeros_like(dkey_ref)
        dvalue_ref[...] = jnp.zeros_like(dvalue_ref)

    queries = query_ref[...]
    grads = grad_ref[...]
    positions = pos_ref[...]
    lse = lse_ref[...]
    delta = jnp.sum(grads.astype(f32) * out_ref[...], axis=-1, keepdims=True)
    tiles = (pl.program_id(0) + 1) * reach // key_tile

    def step(index, dquery):
        span = pl.ds(index * key_tile, key_tile)
        keys = key_ref[span, :]
        values = value_ref[span, :]
        scores = mm_nt(queries, keys) * score_scale
        key_pos = index * key_tile + lax.broadcasted_iota(jnp.int32, scores.shape, 1)
        probs = jnp.where(key_pos <= positions, jnp.exp(scores - lse), 0.0)
        dprobs = mm_nt(grads, values)
        dscores = (probs * (dprobs - delta)).astype(bf16)
        dvalue_ref[span, :] += mm_tn(probs.astype(bf16), grads)
        dkey_ref[span, :] += mm_tn(dscores, queries)
        return dquery + mm(dscores, keys)

    dquery = lax.fori_loop(0, tiles, step, jnp.zeros(queries.shape, f32)) * score_scale
    scaled = dquery[:, NOPE:] * table_ref[...]
    lanes = lax.broadcasted_iota(jnp.int32, scaled.shape, 1)
    half = ROPE // 2
    turned = jnp.where(lanes < half, pltpu.roll(scaled, half, 1), -pltpu.roll(scaled, LANES - half, 1))
    dquery_ref[:, :NOPE] = dquery[:, :NOPE].astype(bf16)
    dquery_ref[:, NOPE:] = (scaled + turned)[:, :ROPE].astype(bf16)

    @pl.when(pl.program_id(0) == pl.num_programs(0) - 1)
    def finish():
        def rows(index, carry):
            span = pl.ds(index * key_tile, key_tile)
            dkey = dkey_ref[span, :] * score_scale
            low = jnp.concatenate([dkey[:, :NOPE], dvalue_ref[span, :]], axis=-1).astype(bf16)
            dexpand_ref[span, :] = low
            dlatent_ref[span, :KVR] = mm_nt(low, expand_ref[...]).astype(bf16)
            dlatent_ref[span, KVR:] = dkey[:, NOPE:].astype(bf16)
            return carry

        lax.fori_loop(0, dkey_ref.shape[0] // key_tile, rows, 0)


def attention_tiles(rows, keys):
    tile = min(512, keys)
    row_tile = rows * tile // keys
    return (row_tile, tile)


def attend(positions, queries, keys, values):
    rows, count = queries.shape[0], keys.shape[0]
    row_tile, tile = attention_tiles(rows, count)
    whole = lambda width: pl.BlockSpec((count, width), lambda i: (0, 0))
    part = lambda width: pl.BlockSpec((row_tile, width), lambda i: (i, 0))
    return pl.pallas_call(
        functools.partial(attend_kernel, tile, tile),
        grid=(rows // row_tile,),
        in_specs=[part(1), part(WIDE), whole(WIDE), whole(VHEAD)],
        out_specs=[part(VHEAD), part(VHEAD), part(1)],
        out_shape=[
            jax.ShapeDtypeStruct((rows, VHEAD), f32),
            jax.ShapeDtypeStruct((rows, VHEAD), bf16),
            jax.ShapeDtypeStruct((rows, 1), f32),
        ],
        compiler_params=pltpu.CompilerParams(vmem_limit_bytes=48 * megabytes),
        cost_estimate=pl.CostEstimate(
            flops=rows * count * (QK + VHEAD) * 2,
            bytes_accessed=4 * (rows + count) * (QK + VHEAD),
            transcendentals=rows * count // 2,
        ),
        name="attend",
    )(positions, queries, keys, values)


def attend_grad(positions, table, queries, keys, values, outcome, lse, grads, expand):
    rows, count = queries.shape[0], keys.shape[0]
    row_tile, tile = attention_tiles(rows, count)
    whole = lambda width: pl.BlockSpec((count, width), lambda i: (0, 0))
    part = lambda width: pl.BlockSpec((row_tile, width), lambda i: (i, 0))
    return pl.pallas_call(
        functools.partial(attend_grad_kernel, tile, tile),
        grid=(rows // row_tile,),
        in_specs=[
            part(1), part(LANES), part(WIDE), whole(WIDE), whole(VHEAD), part(VHEAD), part(1),
            part(VHEAD), pl.BlockSpec(expand.shape, lambda i: (0, 0)),
        ],
        out_specs=[part(QK), whole(NOPE + VHEAD), whole(KVR + LANES)],
        out_shape=[
            jax.ShapeDtypeStruct((rows, QK), bf16),
            jax.ShapeDtypeStruct((count, NOPE + VHEAD), bf16),
            jax.ShapeDtypeStruct((count, KVR + LANES), bf16),
        ],
        scratch_shapes=[pltpu.VMEM((count, WIDE), f32), pltpu.VMEM((count, VHEAD), f32)],
        compiler_params=pltpu.CompilerParams(vmem_limit_bytes=48 * megabytes),
        cost_estimate=pl.CostEstimate(
            flops=rows * count * (3 * QK + 2 * VHEAD) * 2,
            bytes_accessed=8 * (rows + count) * (QK + VHEAD),
            transcendentals=rows * count // 2,
        ),
        name="attend_grad",
    )(positions, table, queries, keys, values, outcome, lse, grads, expand)


def copy_blocks(base_ref, source, target, copied):
    step = pl.program_id(0)
    first = (base_ref[0] * 2 + (step ^ base_ref[2])) * 4

    def copies(group):
        return [
            pltpu.make_async_copy(
                source[2 * mask + group].at[0],
                target.at[first + (mask ^ base_ref[1])],
                copied.at[mask],
            )
            for mask in range(4)
        ]

    def each(act):
        for group in (0, 1):

            @pl.when(step == group)
            def run():
                for copy in copies(group):
                    act(copy)

    each(lambda copy: copy.start())
    return lambda: each(lambda copy: copy.wait())


def pick_all(pick_ref, gates_ref, blocks):
    return jnp.concatenate(
        [
            jnp.sum(pick_ref[block].astype(f32) * gates_ref[block], axis=-1, keepdims=True)
            for block in blocks
        ],
        axis=0,
    )


def forward_kernel(parts, base_ref, *refs):
    *refs, copied = refs
    ffn_refs, (pick_ref, gates_ref) = refs[:8], refs[8:10]
    gate_refs, rise_refs, down_refs = (refs[10 + i * parts : 10 + (i + 1) * parts] for i in range(3))
    sgate_ref, sup_ref, sdown_ref = refs[10 + 3 * parts : 13 + 3 * parts]
    outs = refs[-(10 + 3 * parts) :]
    out_refs, (tokens_ref, entries_ref, y_ref) = outs[:4], outs[4:7]
    mid_ref, sg_ref, su_ref = outs[7:10]
    m_refs, g_refs, u_refs = (outs[10 + i * parts : 10 + (i + 1) * parts] for i in range(3))
    slots = pick_ref.shape[1]
    blocks = [mask ^ base_ref[1] for mask in range(4)]
    spans = [slice(mask * slots, (mask + 1) * slots) for mask in range(4)]
    wait = copy_blocks(base_ref, ffn_refs, tokens_ref, copied)

    for mask, (block, span) in enumerate(zip(blocks, spans)):
        tokens = block_of_step(ffn_refs, mask)
        entries_ref[span, :] = mm(pick_ref[block], tokens).astype(bf16)
    gates = pick_all(pick_ref, gates_ref, blocks)
    entries = entries_ref[...]
    y = jnp.zeros(entries.shape, f32)
    for p in range(parts):
        gate = mm_nt(entries, gate_refs[p][...])
        rise = mm_nt(entries, rise_refs[p][...])
        g_refs[p][...] = gate.astype(bf16)
        u_refs[p][...] = rise.astype(bf16)
        middle = swiglu(gate, rise)
        m_refs[p][...] = middle
        y = y + mm(middle, down_refs[p][...])
    y = y.astype(bf16)
    y_ref[...] = y
    scaled = (gates * y.astype(f32)).astype(bf16)
    for mask, (block, span) in enumerate(zip(blocks, spans)):
        tokens = block_of_step(ffn_refs, mask)
        sgate = mm(tokens, sgate_ref[...])
        sup = mm(tokens, sup_ref[...])
        sg_ref[block] = sgate.astype(bf16)
        su_ref[block] = sup.astype(bf16)
        middle = swiglu(sgate, sup)
        mid_ref[block] = middle
        placed = mm_tn(pick_ref[block], scaled[span])
        out_refs[mask][0] = (mm(middle, sdown_ref[...]) + placed).astype(bf16)
    wait()


def backward_kernel(parts, base_ref, *refs):
    *refs, copied = refs
    up_refs, (pick_ref, gates_ref, y_ref, sg_ref, su_ref) = refs[:8], refs[8:13]
    g_refs, u_refs = (refs[13 + i * parts : 13 + (i + 1) * parts] for i in range(2))
    rest = refs[13 + 2 * parts :]
    gate_refs, rise_refs, down_refs = (rest[i * parts : (i + 1) * parts] for i in range(3))
    sgate_ref, sup_ref, sdown_ref = rest[3 * parts : 3 + 3 * parts]
    outs = refs[-(8 + 2 * parts) :]
    db_refs, (ups_ref, dy_ref, dgate_ref, pair_ref) = outs[:4], outs[4:8]
    dg_refs, du_refs = (outs[8 + i * parts : 8 + (i + 1) * parts] for i in range(2))
    slots = pick_ref.shape[1]
    blocks = [mask ^ base_ref[1] for mask in range(4)]
    spans = [slice(mask * slots, (mask + 1) * slots) for mask in range(4)]
    wait = copy_blocks(base_ref, up_refs, ups_ref, copied)

    for mask, (block, span) in enumerate(zip(blocks, spans)):
        upstream = block_of_step(up_refs, mask)
        dy_ref[span, :] = mm(pick_ref[block], upstream).astype(bf16)
    gates = pick_all(pick_ref, gates_ref, blocks)
    grad_rows = dy_ref[...].astype(f32)
    dgates = jnp.sum(grad_rows * y_ref[...].astype(f32), axis=-1, keepdims=True)
    dy = (gates * grad_rows).astype(bf16)
    dy_ref[...] = dy
    db = jnp.zeros(dy.shape, f32)
    for p in range(parts):
        dm = mm_nt(dy, down_refs[p][...])
        dg, du = swiglu_grads(g_refs[p][...].astype(f32), u_refs[p][...].astype(f32), dm)
        dg_refs[p][...] = dg
        du_refs[p][...] = du
        db = db + mm(dg, gate_refs[p][...]) + mm(du, rise_refs[p][...])
    db = db.astype(bf16)
    for mask, (block, span) in enumerate(zip(blocks, spans)):
        pick = pick_ref[block]
        dgate_ref[block] = jnp.sum(pick.astype(f32) * dgates[span], axis=0, keepdims=True)
        upstream = block_of_step(up_refs, mask)
        sgate, sup = sg_ref[block].astype(f32), su_ref[block].astype(f32)
        dsg, dsu = swiglu_grads(sgate, sup, mm_nt(upstream, sdown_ref[...]))
        pair_ref[0, block] = dsg
        pair_ref[1, block] = dsu
        db_refs[mask][0] = (
            mm_nt(dsg, sgate_ref[...]) + mm_nt(dsu, sup_ref[...]) + mm_tn(pick, db[span])
        ).astype(bf16)
    wait()


def expert_call(kernel, name, piece, blocks, tiled, weights, held_shapes, held, part, width, flops):
    operands, specs = block_operands(blocks)
    fixed = lambda i, base: (0, 0)

    groups = held_shapes[0][0].shape[0] // 4

    def spec(shape, axis=0):
        tile = tuple(n // groups if d == axis else n for d, n in enumerate(shape))
        at = lambda i, base: tuple(
            base[0] * 2 + (i ^ base[2]) if d == axis else 0 for d in range(len(shape))
        )
        return pl.BlockSpec(tile, at)

    out_specs = [pl.BlockSpec((1, part, width), lambda i, base: (i, 0, 0))] * 4
    for shape, axis in held_shapes:
        out_specs.append(
            pl.BlockSpec(memory_space=pl.ANY) if axis is None else spec(shape.shape, axis)
        )
    results = pl.pallas_call(
        kernel,
        grid_spec=pltpu.PrefetchScalarGridSpec(
            num_scalar_prefetch=1,
            grid=(2,),
            in_specs=specs
            + [spec(v.shape) for v in tiled]
            + [pl.BlockSpec(w.shape, fixed, pipeline_mode=pl.Buffered(1)) for w in weights]
            + [pl.BlockSpec(memory_space=pl.ANY)] * len(held),
            out_specs=out_specs,
            scratch_shapes=[pltpu.SemaphoreType.DMA((4,))],
        ),
        out_shape=[jax.ShapeDtypeStruct((2, part, width), bf16)] * 4
        + [shape for shape, _ in held_shapes],
        input_output_aliases={
            1 + len(operands) + len(tiled) + len(weights) + i: 4 + i for i in range(len(held))
        },
        compiler_params=pltpu.CompilerParams(vmem_limit_bytes=60 * megabytes),
        cost_estimate=pl.CostEstimate(
            flops=flops, bytes_accessed=40 * megabytes, transcendentals=1 << 20
        ),
        name=name,
    )(piece_place(piece), *operands, *tiled, *weights, *held)
    return results[:4], results[4:]


def expert_layers(pieces, ups, pick, gates, gate_w, up_w, down_w, sgate, sup, sdown):
    ctx, slots, part = pick.shape
    width, hidden = sgate.shape
    parts = len(gate_w)
    inner = [w.shape[0] for w in gate_w]
    weights = [*gate_w, *up_w, *down_w, sgate, sup, sdown]
    whole = lambda *shape, dtype=bf16: jax.ShapeDtypeStruct(shape, dtype)
    blocks = (whole(ctx, part, width), None)
    rows = (whole(ctx * slots, width), 0)
    units = [(whole(ctx * slots, w), 0) for w in inner]
    shared = (whole(ctx, part, hidden), 0)
    count = len(pieces)
    flops = 6 * (ctx * slots * width * sum(inner) + ctx * part * width * hidden) // count
    forward = functools.partial(forward_kernel, parts)
    backward = functools.partial(backward_kernel, parts)
    forward_shapes = [blocks, rows, rows, shared, shared, shared, *units * 3]
    backward_shapes = [
        blocks, rows, (whole(ctx, 1, part, dtype=f32), 0), (whole(2, ctx, part, hidden), 1), *units * 2
    ]
    outs, dbs, out_hops, db_hops, done, back = [], [], [], [], [], []
    for piece in range(count):
        out, done = expert_call(
            forward, "experts_forward", piece, pieces[piece], [pick, gates], weights,
            forward_shapes, done, part, width, flops,
        )
        if piece == 1 and exchanges():
            out, done, out_hops = together(out, done, out_hops)
        outs.append(out)
        if exchanges():
            out_hops = [*out_hops, *plane_hops([out])]
    tokens, entries, y, mid, sg, su, *units = done
    m, g, u = (units[i * parts : (i + 1) * parts] for i in range(3))
    for piece in range(count):
        db, back = expert_call(
            backward, "experts_backward", piece, ups[piece], [pick, gates, y, sg, su, *g, *u], weights,
            backward_shapes, back, part, width, flops,
        )
        if exchanges():
            if piece == 0:
                db, back, out_hops = together(db, back, out_hops)
            else:
                db, back, db_hops = together(db, back, db_hops)
            if piece == 0:
                db_hops = plane_hops([db])
        dbs.append(db)
    ups_flat, dy, dgates, pair, *units = back
    dg, du = (units[i * parts : (i + 1) * parts] for i in range(2))
    sources = tokens, ups_flat, mid, pair[0], pair[1]
    return (outs, out_hops), (dbs, db_hops), sources, entries, dy, dgates, m, dg, du


def shards(
    hidden_in, gain_attn, w_query, w_kv_down, gain_kv, w_kv_up, w_out, gain_ffn, w_router,
    shared_gate, shared_up, shared_down, expert_gate, expert_up, expert_down, routes, cotangent,
):
    part, width = hidden_in.shape[1:]
    ctx, fsdp = lax.axis_size("ctx"), lax.axis_size("fsdp")
    ctx_rank = lax.axis_index("ctx")
    length = part * ctx
    rows = w_query.shape[0]
    experts = w_router.shape[1]
    parts_of_head = ctx // HEADS
    query_part = part // parts_of_head
    first_row = (ctx_rank % parts_of_head) * query_part
    everywhere = ("ctx", "fsdp")

    def join_rows(parts):
        if fsdp != 2:
            return jnp.stack(parts, axis=1).reshape(-1, parts[0].shape[-1])
        rank = lax.axis_index("fsdp")
        whole = jnp.zeros((ctx, 2) + parts[0].shape[1:], parts[0].dtype)
        for place, value in ((rank, parts[0]), (1 - rank, parts[1])):
            whole = lax.dynamic_update_slice_in_dim(whole, value[:, None], place, 1)
        return whole.reshape(-1, parts[0].shape[-1])

    def to_rows(columns, count):
        grid = columns.reshape(ctx, fsdp, count, columns.shape[-1])
        grid = scatter_fsdp(in_fsdp_order([grid[:, i] for i in range(fsdp)]))
        return to_owner(grid.astype(bf16)).astype(f32)

    def head_blocks(values):
        blocks = values.reshape(values.shape[0], HEADS, -1).transpose(1, 0, 2)
        return jnp.repeat(blocks, parts_of_head, axis=0)

    def from_head_blocks(blocks):
        blocks = blocks.reshape(HEADS, parts_of_head, *blocks.shape[1:]).sum(axis=1)
        return blocks.transpose(1, 0, 2).reshape(blocks.shape[1], -1)

    compressed_width = KVR + ROPE
    turned_width = compressed_width + ROPE
    kv_rows = gain_kv.shape[0]
    small_width = turned_width + experts + 3
    small = jnp.concatenate(
        [
            w_kv_down,
            turn_columns(w_kv_down[:, KVR:]),
            w_router,
            gain_attn[:, None],
            gain_ffn[:, None],
            jnp.pad(gain_kv, (0, rows - kv_rows))[:, None],
            jnp.zeros((rows, -small_width % 128), bf16),
        ],
        axis=1,
    )
    small_full = lax.all_gather(small, everywhere, axis=0, tiled=True)
    reduce_full = small_full[:, :compressed_width]
    router_full = small_full[:, turned_width : small_width - 3]
    attn_gain = small_full[:, small_width - 3].astype(f32)
    ffn_gain = small_full[:, small_width - 2].astype(f32)
    kv_gain = small_full[:, small_width - 1].reshape(ctx * fsdp, rows)[:, :kv_rows]
    kv_gain = kv_gain.reshape(KVR).astype(f32)

    tokens_low = hidden_in.reshape(part, width)
    upstream_low = cotangent.reshape(part, width)
    hidden_shared = shared_gate.shape[1] // ctx
    query_blocks = head_blocks(w_query)
    route_rows = routes.reshape(part, TOP)
    chosen_hot = route_rows[:, :, None] == jnp.arange(experts, dtype=jnp.int32)[None, None, :]
    columns = [
        query_blocks,
        turn_columns(query_blocks[..., NOPE:]),
        head_blocks(w_kv_up).reshape(ctx, rows, -1),
        jnp.any(chosen_hot, axis=1).astype(bf16).T.reshape(ctx, rows, -1),
    ]
    column_blocks = jnp.concatenate(columns, axis=-1)
    expand_end = WIDE + columns[2].shape[-1]

    def joined_stage(received):
        return received, join_rows(gather_fsdp(received[..., :expand_end]))

    tokens_all, (received, by_rows) = gather_ctx(
        tokens_low, lambda _: None, lambda _: None, lambda _: to_owner(column_blocks), joined_stage
    )
    named_all = received[..., expand_end:].reshape(ctx, part)
    query_w = by_rows[:, :WIDE]
    expand = by_rows[:, WIDE:].reshape(KVR, NOPE + VHEAD)
    output_full = lax.all_gather(w_out, everywhere, axis=0, tiled=True)

    upstream_late, gate_late, up_late, _ = lax.optimization_barrier(
        (upstream_low, shared_gate, shared_up, tokens_all[-1][3][1][0])
    )
    columns = [v.reshape(rows, ctx, hidden_shared) for v in (gate_late, up_late)]
    shared_blocks = jnp.concatenate(columns, axis=2).transpose(1, 0, 2)
    shared_back = jnp.concatenate(in_fsdp_order(gather_fsdp(shared_down)), axis=0)
    gate_parts = gather_fsdp(expert_gate[0].T)
    up_parts = gather_fsdp(expert_up[0].T)
    down_parts = gather_fsdp(expert_down[0].T)

    slot_cap = min(part, part * TOP * 4 // (3 * experts))
    until = jnp.arange(part)[:, None] <= jnp.arange(part)[None, :]
    ordinal = mm(named_all, until.astype(bf16)) - 1.0
    slots = jnp.arange(slot_cap, dtype=f32)[None, :, None]
    pick = ((ordinal[:, None, :] == slots) & (named_all[:, None, :] > 0)).astype(bf16)

    cosine, sine = rope_tables(jnp.arange(length, dtype=jnp.int32))
    table = jnp.concatenate([cosine, sine], axis=-1)
    def query_rows(values):
        if parts_of_head == 1:
            return values
        blocks = values.reshape(ctx, part, values.shape[-1])
        blocks = lax.dynamic_slice_in_dim(blocks, first_row, query_part, 1)
        return blocks.reshape(ctx * query_part, values.shape[-1])

    def to_heads(values):
        split = values.reshape(parts_of_head, query_part, HEADS, values.shape[-1])
        sent = split.transpose(2, 0, 1, 3).reshape(ctx, query_part, values.shape[-1])
        return to_owner(sent).reshape(ctx * query_part, values.shape[-1])

    def from_heads(values):
        back = to_owner(values.reshape(ctx, query_part, values.shape[-1]))
        back = back.reshape(HEADS, parts_of_head, query_part, values.shape[-1])
        return back.transpose(1, 2, 0, 3).reshape(part, HEADS, values.shape[-1])

    query_pos = query_rows(jnp.arange(length, dtype=jnp.int32)[:, None])

    def first_stage(_):
        return project(
            tokens_all, attn_gain[None], kv_gain[None], table, query_w, small_full, expand
        )

    def second_stage(projected):
        _, query_all, key_head, value_head, _ = projected
        outcome = attend(query_pos, query_rows(query_all), key_head, value_head)
        return projected, outcome, to_owner(shared_blocks)

    def third_stage(held):
        projected, (outcome, outcome_low, lse), shared_in = held
        shared_in = join_rows(gather_fsdp(shared_in))
        return projected, outcome, lse, from_heads(outcome_low), shared_in

    upstream_all, (projected, outcome, lse, attended, shared_in) = gather_ctx(
        upstream_late, first_stage, second_stage, third_stage
    )
    shared_in = (shared_in[:, :hidden_shared], shared_in[:, hidden_shared:])
    normed_all, query_all, key_head, value_head, latent_all = projected
    query_head = query_rows(query_all)
    attended = attended.reshape(part, HEADS * VHEAD)
    tokens = tokens_low.astype(f32)
    residual = tokens + mm(attended, output_full)

    ffn_factor = rms_factor(residual)
    ffn_low = (residual * ffn_factor * ffn_gain).astype(bf16)
    logits = mm(ffn_low, router_full)
    chosen = jnp.sum(jnp.where(chosen_hot, logits[:, None, :], 0.0), axis=-1)
    gate_share = jax.nn.softmax(chosen, axis=-1)
    gates_own = jnp.sum(jnp.where(chosen_hot, gate_share[..., None], 0.0), axis=1)
    ffn_all, gates_all = gather_ctx(ffn_low, lambda _: None, lambda _: to_owner(gates_own.T))
    query_late, _ = lax.optimization_barrier((w_query, ffn_all[-1][3][1][0]))
    query_full = lax.all_gather(query_late, everywhere, axis=0, tiled=True)
    (out_parts, out_arrived), (grad_parts, grad_arrived), *rest = expert_layers(
        ffn_all, upstream_all, pick, gates_all[:, None, :], gate_parts, up_parts, down_parts,
        *shared_in, shared_back,
    )
    flat, entries, grad_entries, token_dgates, middle, gate_low, up_low = rest
    tokens_flat, upstream_flat, shared_mid, *shared_pair = (
        v.reshape(length, v.shape[-1]) for v in flat
    )

    sums = [(middle, grad_entries), (gate_low, entries), (up_low, entries)]
    sums = [[mm_tn(left, right) for left in lefts] for lefts, right in sums]
    sums = [[own, *(v.astype(bf16) for v in others)] for own, *others in sums]
    shared_sums = [mm_tn(shared_mid, upstream_flat), *(mm_tn(tokens_flat, v) for v in shared_pair)]
    ffn_grad, (sums, dgates_own), (shared_sums, query_full) = scatter_ctx(
        grad_parts, (sums, to_owner(token_dgates[:, 0])), (shared_sums, query_full), grad_arrived
    )
    grad_gates = jnp.sum(jnp.where(chosen_hot, dgates_own.T[:, None, :], 0.0), axis=-1)
    grad_expert_down, grad_expert_gate, grad_expert_up = (scatter_fsdp(v).T[None] for v in sums)
    down_rows = shared_down.shape[0]
    grad_back = shared_sums[0].reshape(fsdp, down_rows, width)
    grad_shared_down = scatter_fsdp(in_fsdp_order([grad_back[i] for i in range(fsdp)]))
    grad_in = to_rows(jnp.concatenate(shared_sums[1:], axis=-1), rows).transpose(1, 0, 2)
    grad_shared_gate = grad_in[..., :hidden_shared].reshape(rows, ctx * hidden_shared)
    grad_shared_up = grad_in[..., hidden_shared:].reshape(rows, ctx * hidden_shared)

    grad_chosen = gate_share * (
        grad_gates - jnp.sum(gate_share * grad_gates, axis=-1, keepdims=True)
    )
    grad_logits = jnp.sum(jnp.where(chosen_hot, grad_chosen[..., None], 0.0), axis=1).astype(bf16)
    grad_router = mm_tn(ffn_low, grad_logits)
    ffn_grad = ffn_grad + mm_nt(grad_logits, router_full)
    upstream = upstream_low.astype(f32)
    ffn_grad_in, grad_ffn_gain = rms_backward(residual, ffn_factor, ffn_gain, ffn_grad)
    grad_residual = upstream + ffn_grad_in
    grad_residual_low = grad_residual.astype(bf16)

    grad_attended = mm_nt(grad_residual_low, output_full).astype(bf16)
    grad_head = to_heads(grad_attended.reshape(part, HEADS, VHEAD))
    output_heads = attended.reshape(part, ctx, fsdp, rows)
    if exchanges():
        output_heads = jnp.take(output_heads, piece_order(), axis=1, mode="clip")
    output_heads = in_fsdp_order([output_heads[:, :, i].reshape(part, -1) for i in range(fsdp)])
    grad_output = [mm_tn(v, grad_residual_low) for v in output_heads]
    grad_output = scatter_fsdp(grad_output).astype(bf16).reshape(ctx, rows, width)
    if exchanges():
        grad_output = grad_output.reshape(2, 4, 2, rows, width)
        output_pieces = [[grad_output[p, m] for m in range(4)] for p in range(2)]
    else:
        output_pieces = in_pieces(grad_output)
    attention_grads = attend_grad(
        query_pos, query_rows(table), query_head, key_head, value_head, outcome, lse, grad_head, expand
    )
    latent_blocks = lambda v: in_pieces(v.reshape(ctx, part, KVR + LANES))
    if exchanges():
        out_sum, out_line = line_hops(out_parts, out_arrived)
        attention_grads, output_arrived, out_line = together(
            attention_grads, plane_hops(output_pieces), out_line
        )
        out_sum = plus(out_sum, *out_line)
        grad_query, grad_expanded, latent_part = attention_grads
        output_sum, output_line = line_hops(output_pieces, output_arrived)
        latent_pieces = latent_blocks(latent_part)
        arrived, output_line, query_own = together(
            plane_hops(latent_pieces), output_line, from_heads(grad_query)
        )
        grad_output = plus(output_sum, *output_line)
        latent_sum, latent_line = line_hops(latent_pieces, arrived)
        grad_normed = mm_nt(query_own.reshape(part, HEADS * QK), query_full)
        latent_line, grad_normed, grad_query, grad_expanded = together(
            latent_line, grad_normed, grad_query, grad_expanded
        )
        latent_sum = plus(latent_sum, *latent_line)
    else:
        grad_query, grad_expanded, latent_part = attention_grads
        out_sum = whole_sum(out_parts)
        grad_output = whole_sum(output_pieces)
        latent_sum = whole_sum(latent_blocks(latent_part))
        grad_normed = mm_nt(from_heads(grad_query).reshape(part, HEADS * QK), query_full)

    grad_query_w = mm_tn(query_rows(normed_all), grad_query).reshape(ctx, fsdp, rows, QK)
    grad_expand = mm_tn(latent_all, grad_expanded).reshape(ctx, fsdp, rows, -1)
    by_heads = jnp.concatenate([grad_query_w, grad_expand], axis=-1)
    by_heads = to_rows(by_heads.reshape(width, by_heads.shape[-1]), rows)
    grad_query_w = from_head_blocks(by_heads[..., :QK])
    grad_expand = from_head_blocks(by_heads[..., QK:].reshape(ctx, kv_rows, NOPE + VHEAD))

    own_rows = ctx_rank * part
    own_normed = lax.dynamic_slice_in_dim(normed_all, own_rows, part, 0)
    latent_raw = mm(own_normed, reduce_full[:, :KVR])
    grad_latent_raw, _ = rms_backward(
        latent_raw, rms_factor(latent_raw), kv_gain, latent_sum[:, :KVR]
    )
    own_cos = lax.dynamic_slice_in_dim(cosine, own_rows, part, 0)
    own_sin = lax.dynamic_slice_in_dim(sine, own_rows, part, 0)
    grad_compressed = jnp.concatenate(
        [grad_latent_raw, unrotate(latent_sum[:, KVR:compressed_width], own_cos, own_sin)], axis=-1
    ).astype(bf16)
    grad_small = jnp.concatenate(
        [
            mm_tn(own_normed, grad_compressed).astype(bf16),
            grad_router.astype(bf16),
            grad_ffn_gain[:, None].astype(bf16),
            jnp.zeros((width, -(compressed_width + experts + 1) % 128), bf16),
        ],
        axis=1,
    ).reshape(ctx, fsdp, rows, -1)
    grad_small = scatter_fsdp(in_fsdp_order([grad_small[:, i] for i in range(fsdp)]))
    grad_small, _, _ = scatter_ctx(in_pieces(grad_small.astype(bf16)))
    grad_reduce = grad_small[:, :compressed_width]
    grad_normed = grad_normed + mm_nt(grad_compressed, reduce_full)
    attn_grad_in, _ = rms_backward(tokens, rms_factor(tokens), attn_gain, grad_normed)
    grad_hidden_in = (grad_residual + attn_grad_in)[None]

    def gain_grad(gain, pairs):
        total = sum(jnp.sum(w.astype(f32) * g, axis=-1) for w, g in pairs)
        return total / gain.astype(f32)

    grad_attn_gain = gain_grad(gain_attn, [(w_query, grad_query_w), (w_kv_down, grad_reduce)])
    grad_kv_gain = gain_grad(gain_kv, [(w_kv_up, grad_expand)])
    out_sum, kept, _ = lax.optimization_barrier((out_sum, residual, latent_sum))
    hidden_out = (kept + out_sum).astype(bf16)
    after = compressed_width + experts
    return (
        hidden_out[None],
        grad_hidden_in,
        grad_attn_gain,
        grad_query_w,
        grad_reduce,
        grad_kv_gain,
        grad_expand,
        grad_output,
        grad_small[:, after],
        grad_small[:, compressed_width:after],
        grad_shared_gate,
        grad_shared_up,
        grad_shared_down,
        grad_expert_gate,
        grad_expert_up,
        grad_expert_down,
    )


def solution(mesh):
    dense = P(("ctx", "fsdp"), None)
    gain = P(("ctx", "fsdp"))
    tokens = P("fsdp", "ctx", None)
    expert = P("ctx", None, "fsdp")
    return jax.shard_map(
        shards,
        mesh=mesh,
        in_specs=(
            tokens, gain, dense, dense, gain, dense, dense, gain, dense, dense, dense, dense,
            expert, expert, expert, tokens, tokens,
        ),
        out_specs=(
            tokens, tokens, gain, dense, dense, gain, dense, dense, gain, dense, dense, dense,
            dense, expert, expert, expert,
        ),
        check_vma=False,
    )
```

profile of v0, /device:TPU:8, one launch (start us, length us, event | category | flops | bytes accessed | tf_op | source)
XLA Modules:
  0.0 995.2 jit_solution(8972211125658040001)
XLA Ops:
  22.1 16.5 %collective-permute-done = bf16[128,2048]{1,0:T(8,128)(2,1)} collective-permute-done((bf16[128,2048]{1,0:T(8,128)(2,1)}, bf16[128,2048]{1,0:T(8,128)(2,1)}, u32[]{:S(2)}, u32[]{:S(2)}) %collective-permute-start) | collective-permute-done | bytes 524320 | tf_op jit(solution)/shard_map/ppermute | solution.py:89
  50.8 5.2 all-to-all-start
  56.7 11.0 %collective-permute-done.4 = bf16[128,2048]{1,0:T(8,128)(2,1)S(1)} collective-permute-done((bf16[128,2048]{1,0:T(8,128)(2,1)S(1)}, bf16[128,2048]{1,0:T(8,128)(2,1)S(1)}, u32[]{:S(2)}, u32[]{:S(2)}) %collective-permute-start.4) | collective-permute-done | bytes 524320 | tf_op jit(solution)/shard_map/ppermute | solution.py:89
  67.7 12.6 %collective-permute-done.7 = bf16[128,2048]{1,0:T(8,128)(2,1)} collective-permute-done((bf16[128,2048]{1,0:T(8,128)(2,1)}, bf16[128,2048]{1,0:T(8,128)(2,1)}, u32[]{:S(2)}, u32[]{:S(2)}) %collective-permute-start.7) | collective-permute-done | bytes 524320 | tf_op jit(solution)/shard_map/ppermute | solution.py:89
  95.8 10.1 %collective-permute-done.9.refs_2_.refs_3_ = bf16[2,128,2048]{2,1,0:T(8,128)(2,1)S(1)} collective-permute-done((bf16[2,128,2048]{2,1,0:T(8,128)(2,1)S(1)}, bf16[2,128,2048]{2,1,0:T(8,128)(2,1)S(1)}, u32[]{:S(2)}, u32[]{:S(2)}) %collective-permute-start.9) | collective-permute-done | bytes 1048608 | tf_op jit(solution)/shard_map/ppermute | solution.py:89
  112.0 9.1 collective-permute-done.12
  131.2 7.1 all-to-all-start.1
  143.2 12.1 %project.2 = (bf16[2048,2048]{1,0:T(8,128)(2,1)}, bf16[2048,256]{1,0:T(8,128)(2,1)}, bf16[2048,256]{1,0:T(8,128)(2,1)}, bf16[2048,128]{1,0:T(8,128)(2,1)}, bf16[2048,512]{1,0:T(8,128)(2,1)}) custom-call(s32[3]{0:T(128)} %get-tuple-element.729.base_ref, bf16[1,128,2048]{2,1,0:T(8,128)(2,1)} %refs_0_.1, bf16[1,128,2048]{2,1,0:T(8,128)(2,1)} %bitcast.25.refs_1_, ...), custom_call_target="tpu_custom_call" | custom-call | flops 3758096384 | bytes 12058624 | tf_op jit(solution)/shard_map/project/pallas_call | solution.py:275
  155.3 12.0 %project.3 = (bf16[2048,2048]{1,0:T(8,128)(2,1)}, bf16[2048,256]{1,0:T(8,128)(2,1)}, bf16[2048,256]{1,0:T(8,128)(2,1)}, bf16[2048,128]{1,0:T(8,128)(2,1)}, bf16[2048,512]{1,0:T(8,128)(2,1)}) custom-call(s32[3]{0:T(128)} %get-tuple-element.730.base_ref, ...), custom_call_target="tpu_custom_call", output_to_operand_aliasing={{0}: (15, {}), {1}: (16, {}), {2}: (17, {}), {3}: (18, {}),... | custom-call | flops 3758096384 | bytes 12058624 | tf_op jit(solution)/shard_map/project/pallas_call | solution.py:275
  173.9 11.3 %attend.1 = (f32[2048,128]{1,0:T(8,128)S(1)}, bf16[2048,128]{1,0:T(8,128)(2,1)S(1)}, f32[2048,1]{1,0:T(8,128)S(1)}) custom-call(s32[2048,1]{1,0:T(8,128)S(1)} %iota.38.pos_ref, bf16[2048,256]{1,0:T(8,128)(2,1)S(1)} %copy-done.2, bf16[2048,256]{1,0:T(8,128)(2,1)} %get-tuple-element.425.key_ref, bf16[2048,128]{1,0:T(8,128)(2,1)S(1)} %copy-done.3), custom_call_target="tpu_custom_call" | custom-call | flops 2684354560 | bytes 5242880 | tf_op jit(solution)/shard_map/attend/pallas_call | solution.py:399
  190.3 11.4 %collective-permute-done.18 = bf16[128,2048]{1,0:T(8,128)(2,1)S(1)} collective-permute-done((bf16[128,2048]{1,0:T(8,128)(2,1)S(1)}, bf16[128,2048]{1,0:T(8,128)(2,1)S(1)}, u32[]{:S(2)}, u32[]{:S(2)}) %collective-permute-start.18) | collective-permute-done | bytes 524320 | tf_op jit(solution)/shard_map/ppermute | solution.py:89
  209.7 5.1 all-to-all-start.2
  217.9 18.0 %collective-permute-done.23 = bf16[128,2048]{1,0:T(8,128)(2,1)S(1)} collective-permute-done((bf16[128,2048]{1,0:T(8,128)(2,1)}, bf16[128,2048]{1,0:T(8,128)(2,1)S(1)}, u32[]{:S(2)}, u32[]{:S(2)}) %collective-permute-start.23) | collective-permute-done | bytes 524320 | tf_op jit(solution)/shard_map/ppermute | solution.py:89
  242.2 9.3 collective-permute-done.26
  267.3 15.1 %collective-permute-done.28 = bf16[128,2048]{1,0:T(8,128)(2,1)S(1)} collective-permute-done((bf16[128,2048]{1,0:T(8,128)(2,1)S(1)}, bf16[128,2048]{1,0:T(8,128)(2,1)S(1)}, u32[]{:S(2)}, u32[]{:S(2)}) %collective-permute-start.28) | collective-permute-done | bytes 524320 | tf_op jit(solution)/shard_map/ppermute | solution.py:89
  289.8 19.0 %all_to_all.56 = f32[16,1,128]{2,1,0:T(1,128)} all-to-all(f32[16,1,128]{2,1,0:T(1,128)S(1)} %bitcast.446), channel_id=1, replica_groups=mesh['ctx'=16,'fsdp'=2] {'ctx'}, dimensions={0} | all-to-all | bytes 16384 | tf_op jit(solution)/shard_map/all_to_all | solution.py:220
  313.3 9.7 collective-permute-done.36
  323.0 10.8 %collective-permute-done.37.refs_2_.refs_3_ = bf16[2,128,2048]{2,1,0:T(8,128)(2,1)S(1)} collective-permute-done((bf16[2,128,2048]{2,1,0:T(8,128)(2,1)S(1)}, bf16[2,128,2048]{2,1,0:T(8,128)(2,1)S(1)}, u32[]{:S(2)}, u32[]{:S(2)}) %collective-permute-start.37) | collective-permute-done | bytes 1048608 | tf_op jit(solution)/shard_map/ppermute | solution.py:89
  336.1 7.2 collective-permute-done.39
  359.1 29.4 %experts_forward.2 = (bf16[2,128,2048]{2,1,0:T(8,128)(2,1)}, bf16[2,128,2048]{2,1,0:T(8,128)(2,1)}, bf16[2,128,2048]{2,1,0:T(8,128)(2,1)}, bf16[2,128,2048]{2,1,...) custom-call(s32[3]{0:T(128)} %get-tuple-element.729.base_ref, ...), custom_call_target="tpu_custom_call" | custom-call | flops 11072962560 | bytes 41943040 | tf_op jit(solution)/shard_map/experts_forward/pallas_call | solution.py:591
  394.9 31.3 %experts_forward.3 = (bf16[2,128,2048]{2,1,0:T(8,128)(2,1)}, bf16[2,128,2048]{2,1,0:T(8,128)(2,1)}, bf16[2,128,2048]{2,1,0:T(8,128)(2,1)}, bf16[2,128,2048]{2,1,...) custom-call(s32[3]{0:T(128)} %get-tuple-element.730.base_ref, ...), custom_call_target="tpu_custom_call", output_to_operand_aliasing={{4}: (20, {}), {5}: (21, {}), {6}: (22, {}), {7}: (23, {}),... | custom-call | flops 11072962560 | bytes 41943040 | tf_op jit(solution)/shard_map/experts_forward/pallas_call | solution.py:591
  432.2 27.0 %collective-permute-done.47 = bf16[2,128,2048]{2,1,0:T(8,128)(2,1)} collective-permute-done((bf16[2,128,2048]{2,1,0:T(8,128)(2,1)}, bf16[2,128,2048]{2,1,0:T(8,128)(2,1)}, u32[]{:S(2)}, u32[]{:S(2)}) %collective-permute-start.47) | collective-permute-done | bytes 1048608 | tf_op jit(solution)/shard_map/ppermute | solution.py:89
  463.6 35.3 %experts_backward.2 = (bf16[2,128,2048]{2,1,0:T(8,128)(2,1)}, bf16[2,128,2048]{2,1,0:T(8,128)(2,1)}, bf16[2,128,2048]{2,1,0:T(8,128)(2,1)}, bf16[2,128,2048]{2,1...) custom-call(s32[3]{0:T(128)} %get-tuple-element.729.base_ref, ...), custom_call_target="tpu_custom_call" | custom-call | flops 11072962560 | bytes 41943040 | tf_op jit(solution)/shard_map/experts_backward/pallas_call | solution.py:591
  498.9 8.1 collective-permute-done.50
  519.9 34.5 %experts_backward.3 = (bf16[2,128,2048]{2,1,0:T(8,128)(2,1)}, bf16[2,128,2048]{2,1,0:T(8,128)(2,1)}, bf16[2,128,2048]{2,1,0:T(8,128)(2,1)}, bf16[2,128,2048]{2,1...) custom-call(s32[3]{0:T(128)} %get-tuple-element.730.base_ref, ...), custom_call_target="tpu_custom_call", output_to_operand_aliasing={{4}: (27, {}), {5}: (28, {}), {6}: (29, {}), {7}: (30, {}),... | custom-call | flops 11072962560 | bytes 41943040 | tf_op jit(solution)/shard_map/experts_backward/pallas_call | solution.py:591
  558.0 5.9 all-to-all-start.4
  565.7 6.4 fusion.92
  572.1 5.1 fusion.89
  591.3 5.0 fusion.91
  620.3 30.0 %collective-permute-done.58 = bf16[128,2048]{1,0:T(8,128)(2,1)S(1)} collective-permute-done((bf16[128,2048]{1,0:T(8,128)(2,1)S(1)}, bf16[128,2048]{1,0:T(8,128)(2,1)S(1)}, u32[]{:S(2)}, u32[]{:S(2)}) %collective-permute-start.58) | collective-permute-done | bytes 524320 | tf_op jit(solution)/shard_map/ppermute | solution.py:89
  651.1 11.0 %collective-permute-done.59 = bf16[128,2048]{1,0:T(8,128)(2,1)} collective-permute-done((bf16[128,2048]{1,0:T(8,128)(2,1)S(1)}, bf16[128,2048]{1,0:T(8,128)(2,1)}, u32[]{:S(2)}, u32[]{:S(2)}) %collective-permute-start.59) | collective-permute-done | bytes 524320 | tf_op jit(solution)/shard_map/ppermute | solution.py:89
  672.2 7.4 add_bitcast_fusion.2
  679.6 7.5 add_bitcast_fusion.1
  695.6 6.3 fusion.6
  703.0 7.6 all-to-all-start.5
  723.2 14.1 %all-to-all-done.5 = bf16[16,128,128]{2,1,0:T(8,128)(2,1)S(1)} async-done(((bf16[16,128,128]{2,1,0:T(8,128)(2,1)}), bf16[16,128,128]{2,1,0:T(8,128)(2,1)S(1)}, u32[]{:S(2)}, u32[]{:S(2)}) %all-to-all-start.5) | async-done | bytes 524320 | tf_op jit(solution)/shard_map/all_to_all | solution.py:220
  743.6 7.4 add_bitcast_fusion
  759.5 5.4 collective-permute-done.61
  767.4 17.5 %attend_grad.1 = (bf16[2048,192]{1,0:T(8,128)(2,1)S(1)}, bf16[2048,256]{1,0:T(8,128)(2,1)S(1)}, bf16[2048,640]{1,0:T(8,128)(2,1)}) custom-call(s32[2048,1]{1,0:T(8,128)S(1)} %iota.39.pos_ref, f32[2048,128]{1,0:T(8,128)S(1)} %copy-done, bf16[2048,256]{1,0:T(8,128)(2,1)} %get-tuple-element.424.query_ref, bf16[2048,256]{1,0:T(8,128)(2,1)} %get-tuple-element.425.key_ref, ...), custom_call_target="tpu_custom_call" | custom-call | flops 6979321856 | bytes 10485760 | tf_op jit(solution)/shard_map/attend_grad/pallas_call | solution.py:424
  787.5 15.2 %collective-permute-done.65 = bf16[2,64,2048]{2,1,0:T(8,128)(2,1)} collective-permute-done((bf16[2,64,2048]{2,1,0:T(8,128)(2,1)}, bf16[2,64,2048]{2,1,0:T(8,128)(2,1)}, u32[]{:S(2)}, u32[]{:S(2)}) %collective-permute-start.65) | collective-permute-done | bytes 524320 | tf_op jit(solution)/shard_map/ppermute | solution.py:89
  811.8 6.4 all-to-all-start.6
  841.1 10.0 %collective-permute-done.77 = bf16[64,2048]{1,0:T(8,128)(2,1)} collective-permute-done((bf16[64,2048]{1,0:T(8,128)(2,1)}, bf16[64,2048]{1,0:T(8,128)(2,1)}, u32[]{:S(2)}, u32[]{:S(2)}) %collective-permute-start.77) | collective-permute-done | bytes 262176 | tf_op jit(solution)/shard_map/ppermute | solution.py:89
  862.9 9.6 collective-permute-done.74
  877.7 10.2 %fusion.94 = f32[128,2048]{1,0:T(8,128)} fusion(bf16[128,3072]{0,1:T(8,128)(2,1)} %bitcast.137, bf16[2048,3072]{1,0:T(8,128)(2,1)} %all-gather.8.cloned.1.call-done), kind=kOutput, calls=%fused_computation.252 | convolution fusion | flops 1610612736 | bytes 14417920 | tf_op jit(solution)/shard_map/dot_general | solution.py:33
  894.1 6.6 fusion.95
  940.4 5.5 all-to-all-start.7
  948.3 14.9 %collective-permute-done.88 = bf16[2,64,640]{1,2,0:T(8,128)(2,1)} collective-permute-done((bf16[2,64,640]{1,2,0:T(8,128)(2,1)}, bf16[2,64,640]{1,2,0:T(8,128)(2,1)}, u32[]{:S(2)}, u32[]{:S(2)}) %collective-permute-start.88) | collective-permute-done | bytes 163872 | tf_op jit(solution)/shard_map/ppermute | solution.py:89
  973.4 7.0 collective-permute-done.91
  (604 shorter events, 378.8 us)
Async XLA Ops:
  7.2 131.2 %all-gather.4.cloned.1.call-start = ((), (), s32[]{:S(2)}) async-start(), calls=%async_computation.9 | async-start | bytes 3244032 | tf_op jit(solution)/shard_map/all_gather | solution.py:721
  12.9 240.8 %all-gather.6.cloned.1.call-start = ((), (), s32[]{:S(2)}) async-start(), calls=%async_computation.10 | async-start | bytes 8650752 | tf_op jit(solution)/shard_map/all_gather | solution.py:753
  46.5 33.8 %collective-permute-start.7 = (bf16[128,2048]{1,0:T(8,128)(2,1)}, bf16[128,2048]{1,0:T(8,128)(2,1)}, u32[]{:S(2)}, u32[]{:S(2)}) collective-permute-start(bf16[128,2048]{1,0:T(8,128)(2,1)} %collective-permute-done.3), channel_id=1, source_target_pairs={{0,2},{2,0},{4,6},{6,4},{8,10},{10,8},{12,14},{14,12},{16,18},{18,... | collective-permute-start | bytes 1572872 | tf_op jit(solution)/shard_map/ppermute | solution.py:89
  50.8 44.1 %all-to-all-start = ((bf16[16,64,322]{2,1,0:T(8,128)(2,1)}), bf16[16,64,322]{2,1,0:T(8,128)(2,1)}, u32[]{:S(2)}, u32[]{:S(2)}) async-start(bf16[16,64,322]{2,1,0:T(8,128)(2,1)} %concatenate.39), calls=%async_computation | async-start | bytes 1572864 | tf_op jit(solution)/shard_map/all_to_all | solution.py:220
  123.8 43.5 %collective-permute-start.14 = (bf16[128,2048]{1,0:T(8,128)(2,1)}, bf16[128,2048]{1,0:T(8,128)(2,1)}, u32[]{:S(2)}, u32[]{:S(2)}) collective-permute-start(bf16[128,2048]{1,0:T(8,128)(2,1)} %bitcast.32), channel_id=1, source_target_pairs={{0,8},{2,10},{4,12},{6,14},{8,0},{10,2},{12,4},{14,6},{16,24},{18,... | collective-permute-start | bytes 1572872 | tf_op jit(solution)/shard_map/ppermute | solution.py:89
  123.9 43.5 %collective-permute-start.15 = (bf16[128,2048]{1,0:T(8,128)(2,1)}, bf16[128,2048]{1,0:T(8,128)(2,1)S(1)}, u32[]{:S(2)}, u32[]{:S(2)}) collective-permute-start(bf16[128,2048]{1,0:T(8,128)(2,1)} %bitcast.32), channel_id=1, source_target_pairs={{0,16},{2,18},{4,20},{6,22},{8,24},{10,26},{12,28},{14,30},{16,0},... | collective-permute-start | bytes 1572872 | tf_op jit(solution)/shard_map/ppermute | solution.py:89
  124.5 42.8 %collective-permute-start.16 = (bf16[128,2048]{1,0:T(8,128)(2,1)}, bf16[128,2048]{1,0:T(8,128)(2,1)}, u32[]{:S(2)}, u32[]{:S(2)}) collective-permute-start(bf16[128,2048]{1,0:T(8,128)(2,1)} %bitcast.32), channel_id=1, source_target_pairs={{0,2},{2,0},{4,6},{6,4},{8,10},{10,8},{12,14},{14,12},{16,18},{18,... | collective-permute-start | bytes 1572872 | tf_op jit(solution)/shard_map/ppermute | solution.py:89
  125.1 42.3 %collective-permute-start.17 = (bf16[128,2048]{1,0:T(8,128)(2,1)}, bf16[128,2048]{1,0:T(8,128)(2,1)}, u32[]{:S(2)}, u32[]{:S(2)}) collective-permute-start(bf16[128,2048]{1,0:T(8,128)(2,1)} %bitcast.32), channel_id=1, source_target_pairs={{0,4},{2,6},{4,0},{6,2},{8,12},{10,14},{12,8},{14,10},{16,20},{18,... | collective-permute-start | bytes 1572872 | tf_op jit(solution)/shard_map/ppermute | solution.py:89
  131.2 59.0 %all-to-all-start.1 = ((bf16[16,64,352]{2,1,0:T(8,128)(2,1)}), bf16[16,64,352]{2,1,0:T(8,128)(2,1)S(1)}, u32[]{:S(2)}, u32[]{:S(2)}) async-start(bf16[16,64,352]{2,1,0:T(8,128)(2,1)} %maximum_bitcast_fusion), calls=%async_computation.1 | async-start | bytes 1572864 | tf_op jit(solution)/shard_map/all_to_all | solution.py:220
  167.4 34.2 %collective-permute-start.18 = (bf16[128,2048]{1,0:T(8,128)(2,1)S(1)}, bf16[128,2048]{1,0:T(8,128)(2,1)S(1)}, u32[]{:S(2)}, u32[]{:S(2)}) collective-permute-start(bf16[128,2048]{1,0:T(8,128)(2,1)S(1)} %collective-permute-done.15), channel_id=1, source_target_pairs={{0,8},{2,10},{4,12},{6,14},{8,0},{10,2},{12,4},{14,6},{16,24},{18,... | collective-permute-start | bytes 1572872 | tf_op jit(solution)/shard_map/ppermute | solution.py:89
  167.5 34.1 %collective-permute-start.19 = (bf16[128,2048]{1,0:T(8,128)(2,1)}, bf16[128,2048]{1,0:T(8,128)(2,1)S(1)}, u32[]{:S(2)}, u32[]{:S(2)}) collective-permute-start(bf16[128,2048]{1,0:T(8,128)(2,1)} %collective-permute-done.14), channel_id=1, source_target_pairs={{0,2},{2,0},{4,6},{6,4},{8,10},{10,8},{12,14},{14,12},{16,18},{18,... | collective-permute-start | bytes 1572872 | tf_op jit(solution)/shard_map/ppermute | solution.py:89
  169.5 32.1 %collective-permute-start.20 = (bf16[128,2048]{1,0:T(8,128)(2,1)}, bf16[128,2048]{1,0:T(8,128)(2,1)}, u32[]{:S(2)}, u32[]{:S(2)}) collective-permute-start(bf16[128,2048]{1,0:T(8,128)(2,1)} %collective-permute-done.14), channel_id=1, source_target_pairs={{0,4},{2,6},{4,0},{6,2},{8,12},{10,14},{12,8},{14,10},{16,20},{18,... | collective-permute-start | bytes 1572872 | tf_op jit(solution)/shard_map/ppermute | solution.py:89
  171.0 34.5 %collective-permute-start.21 = (bf16[128,2048]{1,0:T(8,128)(2,1)}, bf16[128,2048]{1,0:T(8,128)(2,1)}, u32[]{:S(2)}, u32[]{:S(2)}) collective-permute-start(bf16[128,2048]{1,0:T(8,128)(2,1)} %collective-permute-done.17), channel_id=1, source_target_pairs={{0,2},{2,0},{4,6},{6,4},{8,10},{10,8},{12,14},{14,12},{16,18},{18,... | collective-permute-start | bytes 1572872 | tf_op jit(solution)/shard_map/ppermute | solution.py:89
  214.9 447.3 %all-gather.8.cloned.1.call-start = ((), (), s32[]{:S(2)}) async-start(), calls=%async_computation.11 | async-start | bytes 12976128 | tf_op jit(solution)/shard_map/all_gather | solution.py:825
  388.5 40.7 %collective-permute-start.45 = (bf16[2,128,2048]{2,1,0:T(8,128)(2,1)}, bf16[2,128,2048]{2,1,0:T(8,128)(2,1)S(1)}, u32[]{:S(2)}, u32[]{:S(2)}) collective-permute-start(bf16[2,128,2048]{2,1,0:T(8,128)(2,1)} %get-tuple-element.393), channel_id=1, source_target_pairs={{0,2},{2,0},{4,6},{6,4},{8,10},{10,8},{12,14},{14,12},{16,18},{18,... | collective-permute-start | bytes 3145736 | tf_op jit(solution)/shard_map/ppermute | solution.py:89
  389.3 42.9 %collective-permute-start.46 = (bf16[2,128,2048]{2,1,0:T(8,128)(2,1)}, bf16[2,128,2048]{2,1,0:T(8,128)(2,1)}, u32[]{:S(2)}, u32[]{:S(2)}) collective-permute-start(bf16[2,128,2048]{2,1,0:T(8,128)(2,1)} %get-tuple-element.394), channel_id=1, source_target_pairs={{0,4},{2,6},{4,0},{6,2},{8,12},{10,14},{12,8},{14,10},{16,20},{18,... | collective-permute-start | bytes 3145736 | tf_op jit(solution)/shard_map/ppermute | solution.py:89
  390.1 69.1 %collective-permute-start.47 = (bf16[2,128,2048]{2,1,0:T(8,128)(2,1)}, bf16[2,128,2048]{2,1,0:T(8,128)(2,1)}, u32[]{:S(2)}, u32[]{:S(2)}) collective-permute-start(bf16[2,128,2048]{2,1,0:T(8,128)(2,1)} %get-tuple-element.395), channel_id=1, source_target_pairs={{0,6},{2,4},{4,2},{6,0},{8,14},{10,12},{12,10},{14,8},{16,22},{18,... | collective-permute-start | bytes 3145736 | tf_op jit(solution)/shard_map/ppermute | solution.py:89
  459.3 39.6 %collective-permute-start.48 = (bf16[2,128,2048]{2,1,0:T(8,128)(2,1)}, bf16[2,128,2048]{2,1,0:T(8,128)(2,1)S(1)}, u32[]{:S(2)}, u32[]{:S(2)}) collective-permute-start(bf16[2,128,2048]{2,1,0:T(8,128)(2,1)} %get-tuple-element.418), channel_id=1, source_target_pairs={{0,2},{2,0},{4,6},{6,4},{8,10},{10,8},{12,14},{14,12},{16,18},{18,... | collective-permute-start | bytes 3145736 | tf_op jit(solution)/shard_map/ppermute | solution.py:89
  460.1 38.8 %collective-permute-start.49 = (bf16[2,128,2048]{2,1,0:T(8,128)(2,1)}, bf16[2,128,2048]{2,1,0:T(8,128)(2,1)S(1)}, u32[]{:S(2)}, u32[]{:S(2)}) collective-permute-start(bf16[2,128,2048]{2,1,0:T(8,128)(2,1)} %get-tuple-element.419), channel_id=1, source_target_pairs={{0,4},{2,6},{4,0},{6,2},{8,12},{10,14},{12,8},{14,10},{16,20},{18,... | collective-permute-start | bytes 3145736 | tf_op jit(solution)/shard_map/ppermute | solution.py:89
  461.3 45.8 %collective-permute-start.50 = (bf16[2,128,2048]{2,1,0:T(8,128)(2,1)}, bf16[2,128,2048]{2,1,0:T(8,128)(2,1)}, u32[]{:S(2)}, u32[]{:S(2)}) collective-permute-start(bf16[2,128,2048]{2,1,0:T(8,128)(2,1)} %get-tuple-element.420), channel_id=1, source_target_pairs={{0,6},{2,4},{4,2},{6,0},{8,14},{10,12},{12,10},{14,8},{16,22},{18,... | collective-permute-start | bytes 3145736 | tf_op jit(solution)/shard_map/ppermute | solution.py:89
  507.1 47.3 %collective-permute-start.51 = (bf16[2,128,2048]{2,1,0:T(8,128)(2,1)}, bf16[2,128,2048]{2,1,0:T(8,128)(2,1)}, u32[]{:S(2)}, u32[]{:S(2)}) collective-permute-start(bf16[2,128,2048]{2,1,0:T(8,128)(2,1)} %get-tuple-element.452), channel_id=1, source_target_pairs={{0,2},{2,0},{4,6},{6,4},{8,10},{10,8},{12,14},{14,12},{16,18},{18,... | collective-permute-start | bytes 3145736 | tf_op jit(solution)/shard_map/ppermute | solution.py:89
  508.0 46.4 %collective-permute-start.52 = (bf16[2,128,2048]{2,1,0:T(8,128)(2,1)}, bf16[2,128,2048]{2,1,0:T(8,128)(2,1)}, u32[]{:S(2)}, u32[]{:S(2)}) collective-permute-start(bf16[2,128,2048]{2,1,0:T(8,128)(2,1)} %get-tuple-element.453), channel_id=1, source_target_pairs={{0,4},{2,6},{4,0},{6,2},{8,12},{10,14},{12,8},{14,10},{16,20},{18,... | collective-permute-start | bytes 3145736 | tf_op jit(solution)/shard_map/ppermute | solution.py:89
  509.3 45.1 %collective-permute-start.53 = (bf16[2,128,2048]{2,1,0:T(8,128)(2,1)}, bf16[2,128,2048]{2,1,0:T(8,128)(2,1)}, u32[]{:S(2)}, u32[]{:S(2)}) collective-permute-start(bf16[2,128,2048]{2,1,0:T(8,128)(2,1)} %get-tuple-element.454), channel_id=1, source_target_pairs={{0,6},{2,4},{4,2},{6,0},{8,14},{10,12},{12,10},{14,8},{16,22},{18,... | collective-permute-start | bytes 3145736 | tf_op jit(solution)/shard_map/ppermute | solution.py:89
  514.5 241.5 %collective-permute-start.67 = (bf16[128,2048]{1,0:T(8,128)(2,1)}, bf16[128,2048]{1,0:T(8,128)(2,1)}, u32[]{:S(2)}, u32[]{:S(2)}) collective-permute-start(bf16[128,2048]{1,0:T(8,128)(2,1)} %fusion.43), channel_id=1, source_target_pairs={{0,8},{2,10},{4,12},{6,14},{8,0},{10,2},{12,4},{14,6},{16,24},{18,... | collective-permute-start | bytes 1572872 | tf_op jit(solution)/shard_map/ppermute | solution.py:89
  554.4 51.4 %collective-permute-start.54 = (bf16[2,128,2048]{2,1,0:T(8,128)(2,1)}, bf16[2,128,2048]{2,1,0:T(8,128)(2,1)S(1)}, u32[]{:S(2)}, u32[]{:S(2)}) collective-permute-start(bf16[2,128,2048]{2,1,0:T(8,128)(2,1)} %get-tuple-element.458), channel_id=1, source_target_pairs={{0,2},{2,0},{4,6},{6,4},{8,10},{10,8},{12,14},{14,12},{16,18},{18,... | collective-permute-start | bytes 3145736 | tf_op jit(solution)/shard_map/ppermute | solution.py:89
  555.4 50.4 %collective-permute-start.55 = (bf16[2,128,2048]{2,1,0:T(8,128)(2,1)}, bf16[2,128,2048]{2,1,0:T(8,128)(2,1)}, u32[]{:S(2)}, u32[]{:S(2)}) collective-permute-start(bf16[2,128,2048]{2,1,0:T(8,128)(2,1)} %get-tuple-element.459), channel_id=1, source_target_pairs={{0,4},{2,6},{4,0},{6,2},{8,12},{10,14},{12,8},{14,10},{16,20},{18,... | collective-permute-start | bytes 3145736 | tf_op jit(solution)/shard_map/ppermute | solution.py:89
  556.4 49.5 %collective-permute-start.56 = (bf16[2,128,2048]{2,1,0:T(8,128)(2,1)}, bf16[2,128,2048]{2,1,0:T(8,128)(2,1)}, u32[]{:S(2)}, u32[]{:S(2)}) collective-permute-start(bf16[2,128,2048]{2,1,0:T(8,128)(2,1)} %get-tuple-element.460), channel_id=1, source_target_pairs={{0,6},{2,4},{4,2},{6,0},{8,14},{10,12},{12,10},{14,8},{16,22},{18,... | collective-permute-start | bytes 3145736 | tf_op jit(solution)/shard_map/ppermute | solution.py:89
  558.0 47.9 %all-to-all-start.4 = ((f32[16,1,128]{2,1,0:T(1,128)}), f32[16,1,128]{2,1,0:T(1,128)}, u32[]{:S(2)}, u32[]{:S(2)}) async-start(f32[16,1,128]{2,1,0:T(1,128)} %get-tuple-element.469), calls=%async_computation.4 | async-start | bytes 16384 | tf_op jit(solution)/shard_map/all_to_all | solution.py:220
  609.5 62.2 %collective-permute-start.95 = (bf16[704,2048]{1,0:T(8,128)(2,1)}, bf16[704,2048]{1,0:T(8,128)(2,1)}, u32[]{:S(2)}, u32[]{:S(2)}) collective-permute-start(bf16[704,2048]{1,0:T(8,128)(2,1)} %convolution_convert_fusion.2), channel_id=1, source_target_pairs={{0,1},{1,0},{2,3},{3,2},{4,5},{5,4},{6,7},{7,6},{8,9},{9,8},{10,11... | collective-permute-start | bytes 8650760 | tf_op jit(solution)/shard_map/ppermute | solution.py:195
  612.7 37.6 %collective-permute-start.58 = (bf16[128,2048]{1,0:T(8,128)(2,1)S(1)}, bf16[128,2048]{1,0:T(8,128)(2,1)S(1)}, u32[]{:S(2)}, u32[]{:S(2)}) collective-permute-start(bf16[128,2048]{1,0:T(8,128)(2,1)S(1)} %get-tuple-element.698), channel_id=1, source_target_pairs={{0,16},{2,18},{4,20},{6,22},{8,24},{10,26},{12,28},{14,30},{16,0},... | collective-permute-start | bytes 1572872 | tf_op jit(solution)/shard_map/ppermute | solution.py:89
  615.6 46.5 %collective-permute-start.59 = (bf16[128,2048]{1,0:T(8,128)(2,1)S(1)}, bf16[128,2048]{1,0:T(8,128)(2,1)}, u32[]{:S(2)}, u32[]{:S(2)}) collective-permute-start(bf16[128,2048]{1,0:T(8,128)(2,1)S(1)} %get-tuple-element.697), channel_id=1, source_target_pairs={{0,24},{2,26},{4,28},{6,30},{8,16},{10,18},{12,20},{14,22},{16,8},... | collective-permute-start | bytes 1572872 | tf_op jit(solution)/shard_map/ppermute | solution.py:89
  620.3 59.3 %collective-permute-start.96 = (bf16[704,2048]{1,0:T(8,128)(2,1)}, bf16[704,2048]{1,0:T(8,128)(2,1)}, u32[]{:S(2)}, u32[]{:S(2)}) collective-permute-start(bf16[704,2048]{1,0:T(8,128)(2,1)} %convolution_convert_fusion.1), channel_id=1, source_target_pairs={{0,1},{1,0},{2,3},{3,2},{4,5},{5,4},{6,7},{7,6},{8,9},{9,8},{10,11... | collective-permute-start | bytes 8650760 | tf_op jit(solution)/shard_map/ppermute | solution.py:195
  669.2 46.9 %collective-permute-start.60 = (bf16[1024,2048]{1,0:T(8,128)(2,1)}, bf16[1024,2048]{1,0:T(8,128)(2,1)}, u32[]{:S(2)}, u32[]{:S(2)}) collective-permute-start(bf16[1024,2048]{1,0:T(8,128)(2,1)} %convolution_convert_fusion), channel_id=1, source_target_pairs={{0,1},{1,0},{2,3},{3,2},{4,5},{5,4},{6,7},{7,6},{8,9},{9,8},{10,11... | collective-permute-start | bytes 12582920 | tf_op jit(solution)/shard_map/ppermute | solution.py:195
  670.3 86.3 %collective-permute-start.68 = (bf16[128,2048]{1,0:T(8,128)(2,1)}, bf16[128,2048]{1,0:T(8,128)(2,1)}, u32[]{:S(2)}, u32[]{:S(2)}) collective-permute-start(bf16[128,2048]{1,0:T(8,128)(2,1)} %get-tuple-element.696), channel_id=1, source_target_pairs={{0,16},{2,18},{4,20},{6,22},{8,24},{10,26},{12,28},{14,30},{16,0},... | collective-permute-start | bytes 1572872 | tf_op jit(solution)/shard_map/ppermute | solution.py:89
  671.7 70.3 %collective-permute-start.97 = (bf16[704,2048]{1,0:T(8,128)(2,1)}, bf16[704,2048]{1,0:T(8,128)(2,1)}, u32[]{:S(2)}, u32[]{:S(2)}) collective-permute-start(bf16[704,2048]{1,0:T(8,128)(2,1)} %convolution_convert_fusion.3), channel_id=1, source_target_pairs={{0,1},{1,0},{2,3},{3,2},{4,5},{5,4},{6,7},{7,6},{8,9},{9,8},{10,11... | collective-permute-start | bytes 8650760 | tf_op jit(solution)/shard_map/ppermute | solution.py:195
  703.0 34.3 %all-to-all-start.5 = ((bf16[16,128,128]{2,1,0:T(8,128)(2,1)}), bf16[16,128,128]{2,1,0:T(8,128)(2,1)S(1)}, u32[]{:S(2)}, u32[]{:S(2)}) async-start(bf16[16,128,128]{2,1,0:T(8,128)(2,1)} %bitcast.360), calls=%async_computation.5 | async-start | bytes 1048576 | tf_op jit(solution)/shard_map/all_to_all | solution.py:220
  711.4 46.7 %collective-permute-start.69 = (bf16[128,2048]{1,0:T(8,128)(2,1)}, bf16[128,2048]{1,0:T(8,128)(2,1)}, u32[]{:S(2)}, u32[]{:S(2)}) collective-permute-start(bf16[128,2048]{1,0:T(8,128)(2,1)} %get-tuple-element.695), channel_id=1, source_target_pairs={{0,24},{2,26},{4,28},{6,30},{8,16},{10,18},{12,20},{14,22},{16,8},... | collective-permute-start | bytes 1572872 | tf_op jit(solution)/shard_map/ppermute | solution.py:89
  716.2 35.9 %collective-permute-start.94 = (bf16[88,2048]{1,0:T(8,128)(2,1)}, bf16[88,2048]{1,0:T(8,128)(2,1)}, u32[]{:S(2)}, u32[]{:S(2)}) collective-permute-start(bf16[88,2048]{1,0:T(8,128)(2,1)} %select_convert_fusion.2), channel_id=1, source_target_pairs={{0,1},{1,0},{2,3},{3,2},{4,5},{5,4},{6,7},{7,6},{8,9},{9,8},{10,11... | collective-permute-start | bytes 1081352 | tf_op jit(solution)/shard_map/ppermute | solution.py:195
  737.3 47.6 %all-to-all-start.8 = ((bf16[16,64,352]{2,1,0:T(8,128)(2,1)}), bf16[16,64,352]{2,1,0:T(8,128)(2,1)}, u32[]{:S(2)}, u32[]{:S(2)}) async-start(bf16[16,64,352]{2,1,0:T(8,128)(2,1)} %fusion.5), calls=%async_computation.8 | async-start | bytes 1572864 | tf_op jit(solution)/shard_map/all_to_all | solution.py:220
  754.5 32.8 %collective-permute-start.62 = (bf16[2,64,2048]{2,1,0:T(8,128)(2,1)}, bf16[2,64,2048]{2,1,0:T(8,128)(2,1)}, u32[]{:S(2)}, u32[]{:S(2)}) collective-permute-start(bf16[2,64,2048]{2,1,0:T(8,128)(2,1)} %get-tuple-element.671), channel_id=1, source_target_pairs={{0,4},{2,6},{4,0},{6,2},{8,12},{10,14},{12,8},{14,10},{16,20},{18,... | collective-permute-start | bytes 1572872 | tf_op jit(solution)/shard_map/ppermute | solution.py:89
  756.0 31.4 %collective-permute-start.63 = (bf16[2,64,2048]{2,1,0:T(8,128)(2,1)}, bf16[2,64,2048]{2,1,0:T(8,128)(2,1)}, u32[]{:S(2)}, u32[]{:S(2)}) collective-permute-start(bf16[2,64,2048]{2,1,0:T(8,128)(2,1)} %get-tuple-element.670), channel_id=1, source_target_pairs={{0,6},{2,4},{4,2},{6,0},{8,14},{10,12},{12,10},{14,8},{16,22},{18,... | collective-permute-start | bytes 1572872 | tf_op jit(solution)/shard_map/ppermute | solution.py:89
  756.6 31.0 %collective-permute-start.64 = (bf16[2,64,2048]{2,1,0:T(8,128)(2,1)}, bf16[2,64,2048]{2,1,0:T(8,128)(2,1)}, u32[]{:S(2)}, u32[]{:S(2)}) collective-permute-start(bf16[2,64,2048]{2,1,0:T(8,128)(2,1)} %get-tuple-element.669), channel_id=1, source_target_pairs={{0,2},{2,0},{4,6},{6,4},{8,10},{10,8},{12,14},{14,12},{16,18},{18,... | collective-permute-start | bytes 1572872 | tf_op jit(solution)/shard_map/ppermute | solution.py:89
  758.0 44.7 %collective-permute-start.65 = (bf16[2,64,2048]{2,1,0:T(8,128)(2,1)}, bf16[2,64,2048]{2,1,0:T(8,128)(2,1)}, u32[]{:S(2)}, u32[]{:S(2)}) collective-permute-start(bf16[2,64,2048]{2,1,0:T(8,128)(2,1)} %get-tuple-element.668), channel_id=1, source_target_pairs={{0,4},{2,6},{4,0},{6,2},{8,12},{10,14},{12,8},{14,10},{16,20},{18,... | collective-permute-start | bytes 1572872 | tf_op jit(solution)/shard_map/ppermute | solution.py:89
  765.0 37.8 %collective-permute-start.66 = (bf16[2,64,2048]{2,1,0:T(8,128)(2,1)}, bf16[2,64,2048]{2,1,0:T(8,128)(2,1)}, u32[]{:S(2)}, u32[]{:S(2)}) collective-permute-start(bf16[2,64,2048]{2,1,0:T(8,128)(2,1)} %get-tuple-element.667), channel_id=1, source_target_pairs={{0,6},{2,4},{4,2},{6,0},{8,14},{10,12},{12,10},{14,8},{16,22},{18,... | collective-permute-start | bytes 1572872 | tf_op jit(solution)/shard_map/ppermute | solution.py:89
  809.7 48.9 %collective-permute-start.70 = (bf16[2,128,640]{2,1,0:T(8,128)(2,1)}, bf16[2,128,640]{2,1,0:T(8,128)(2,1)S(1)}, u32[]{:S(2)}, u32[]{:S(2)}) collective-permute-start(bf16[2,128,640]{2,1,0:T(8,128)(2,1)} %get-tuple-element.680), channel_id=1, source_target_pairs={{0,2},{2,0},{4,6},{6,4},{8,10},{10,8},{12,14},{14,12},{16,18},{18,... | collective-permute-start | bytes 983048 | tf_op jit(solution)/shard_map/ppermute | solution.py:89
  811.8 60.7 %all-to-all-start.6 = ((bf16[16,128,192]{1,2,0:T(8,128)(2,1)}), bf16[16,128,192]{1,2,0:T(8,128)(2,1)}, u32[]{:S(2)}, u32[]{:S(2)}) async-start(bf16[16,128,192]{1,2,0:T(8,128)(2,1)} %copy.315), calls=%async_computation.6 | async-start | bytes 1572864 | tf_op jit(solution)/shard_map/all_to_all | solution.py:220
  825.5 31.5 %collective-permute-start.78 = (bf16[64,2048]{1,0:T(8,128)(2,1)}, bf16[64,2048]{1,0:T(8,128)(2,1)}, u32[]{:S(2)}, u32[]{:S(2)}) collective-permute-start(bf16[64,2048]{1,0:T(8,128)(2,1)} %get-tuple-element.705), channel_id=1, source_target_pairs={{0,24},{2,26},{4,28},{6,30},{8,16},{10,18},{12,20},{14,22},{16,8},... | collective-permute-start | bytes 786440 | tf_op jit(solution)/shard_map/ppermute | solution.py:89
  902.1 33.5 %collective-permute-start.82 = (bf16[16,64,256]{2,1,0:T(8,128)(2,1)}, bf16[16,64,256]{2,1,0:T(8,128)(2,1)}, u32[]{:S(2)}, u32[]{:S(2)}) collective-permute-start(bf16[16,64,256]{2,1,0:T(8,128)(2,1)} %fusion.41), channel_id=1, source_target_pairs={{0,1},{1,0},{2,3},{3,2},{4,5},{5,4},{6,7},{7,6},{8,9},{9,8},{10,11... | collective-permute-start | bytes 1572872 | tf_op jit(solution)/shard_map/ppermute | solution.py:195
  (170 other events, 2667.2 us)
Sparse Core Ops, SparseCore 0:
  13.0 80.3 all-gather.3
  96.2 110.1 all-gather.5
  344.8 131.9 all-gather.7
where the time goes:
time: 1000 us; the launch traced here: 995 us
  waiting for transfers between devices  342 us (34%)
  Pallas kernels  183 us (18%)
  starting transfers between devices  156 us (16%)
  other arithmetic  100 us (10%)
  local copies, waits for them, and re-layouts  95 us (10%)
  matrix products  82.9 us (8%)
  blocking collectives  19 us (2%)
  between operations  16 us (2%)
    ppermute x84, waiting for transfers between devices, hop(): return lax.ppermute(value, 'ctx', [(i, i ^ mask) for i in range(16)])  319 us
    pallas_call x4, Pallas kernels, expert_call(): pl.pallas_call(kernel, grid_spec=pltpu.PrefetchScalarGridSpec(num_scalar_...  130 us
    ppermute x84, starting transfers between devices, hop(): return lax.ppermute(value, 'ctx', [(i, i ^ mask) for i in range(16)])  106 us
    dot_general x15, matrix products, mm_tn(): lax.dot_general(left, right, (((0,), (0,)), ((), ())), preferred_element_...  56.1 us
    all_to_all x8, starting transfers between devices, to_owner(): lax.all_to_all(blocks, 'ctx', split_axis=0, concat_axis=0, tiled=True)  47.7 us
    unnamed x231, local copies, waits for them, and re-layouts  25.8 us
    pallas_call x2, Pallas kernels, project(): pl.pallas_call(project_kernel, grid_spec=pltpu.PrefetchScalarGridSpec(num...  24.1 us
    broadcast_in_dim x3, other arithmetic, shards(): scatter_fsdp(v).T[None]  22.2 us
  transfers between devices with their start and end apart: 109, of which 43 were waited for; matrix products, arithmetic and copies ran while one was open for 23% of the time, Pallas kernels for 18%

commit v1 on v0

--- a/solution.py
+++ b/solution.py
@@ -96,33 +96,34 @@
 def gather_ctx(block, *stages):
     held = None
     if not exchanges():
-        for stage in stages:
-            held = stage(held)
         whole = lax.all_gather(block, "ctx", axis=0)
         at = lambda piece, mask: [(whole, 8 * piece + 4 * group + mask) for group in (0, 1)]
-        return [[at(piece, mask) for mask in range(4)] for piece in range(whole.shape[0] // 8)], held
+        pieces = [[at(piece, mask) for mask in range(4)] for piece in range(whole.shape[0] // 8)]
+        for stage in stages:
+            held = stage(held, pieces)
+        return pieces, held
 
     def end(number, *hops):
         nonlocal held
         if number < len(stages):
-            held = stages[number](held)
+            held = stages[number](held, pieces)
         held, *hops = together(held, *hops)
         return hops
 
-    near, far, one, two = end(0, *(hop(block, mask) for mask in (4, 8, 1, 2)))
-    far_near, near_one, near_two, three = end(
-        1, hop(far, 4), hop(near, 1), hop(near, 2), hop(two, 1)
-    )
-    pair = jnp.stack([far, far_near])
-    near_three, far_one, far_two = end(2, hop(three, 4), hop(pair, 1), hop(pair, 2))
-    far_three = end(3, hop(far_two[0], 1), hop(far_one[1], 2))
-    pairs = [(block, near), (one, near_one), (two, near_two), (three, near_three)]
+    pieces = []
+
     alone = lambda values: [(value[None], 0) for value in values]
     both = lambda values: [(values, 0), (values, 1)]
-    return [
-        [alone(values) for values in pairs],
-        [both(pair), both(far_one), both(far_two), alone(far_three)],
-    ], held
+    near, far, one, two = end(0, *(hop(block, mask) for mask in (4, 8, 1, 2)))
+    far_near, three, *near_others = end(
+        1, hop(far, 4), hop(two, 1), *(hop(near, mask) for mask in (1, 2, 3))
+    )
+    pairs = zip((block, one, two, three), (near, *near_others))
+    pieces = [[alone(values) for values in pairs]]
+    pair = jnp.stack([far, far_near])
+    far_one, far_two = end(2, hop(pair, 1), hop(pair, 2))
+    far_three = end(3, hop(far_two[0], 1), hop(far_one[1], 2))
+    return [*pieces, [both(pair), both(far_one), both(far_two), alone(far_three)]], held
 
 
 def block_operands(piece):
@@ -175,20 +176,6 @@
         return jnp.array([piece, 0, 0], jnp.int32)
     own = lax.axis_index("ctx")
     return jnp.stack([(own >> 3) ^ piece, own & 3, (own >> 2) & 1])
-
-
-def piece_order():
-    masks = [p * 8 + g * 4 + m for p in (0, 1) for m in range(4) for g in (0, 1)]
-    return jnp.array(masks, jnp.int32) ^ lax.axis_index("ctx")
-
-
-def in_pieces(blocks):
-    if not exchanges():
-        groups = blocks.reshape(-1, 2, 4, *blocks.shape[1:])
-        return [[piece[:, mask] for mask in range(4)] for piece in groups]
-    ordered = jnp.take(blocks, piece_order(), axis=0, mode="clip")
-    ordered = ordered.reshape(2, 4, 2, *blocks.shape[1:])
-    return [[ordered[p, m] for m in range(4)] for p in (0, 1)]
 
 
 def swap_cores(value):
@@ -379,7 +366,7 @@
             low = jnp.concatenate([dkey[:, :NOPE], dvalue_ref[span, :]], axis=-1).astype(bf16)
             dexpand_ref[span, :] = low
             dlatent_ref[span, :KVR] = mm_nt(low, expand_ref[...]).astype(bf16)
-            dlatent_ref[span, KVR:] = dkey[:, NOPE:].astype(bf16)
+            dlatent_ref[span, KVR:] = dkey[:, NOPE : NOPE + ROPE].astype(bf16)
             return carry
 
         lax.fori_loop(0, dkey_ref.shape[0] // key_tile, rows, 0)
@@ -428,11 +415,11 @@
             part(1), part(LANES), part(WIDE), whole(WIDE), whole(VHEAD), part(VHEAD), part(1),
             part(VHEAD), pl.BlockSpec(expand.shape, lambda i: (0, 0)),
         ],
-        out_specs=[part(QK), whole(NOPE + VHEAD), whole(KVR + LANES)],
+        out_specs=[part(QK), whole(NOPE + VHEAD), whole(KVR + ROPE)],
         out_shape=[
             jax.ShapeDtypeStruct((rows, QK), bf16),
             jax.ShapeDtypeStruct((count, NOPE + VHEAD), bf16),
-            jax.ShapeDtypeStruct((count, KVR + LANES), bf16),
+            jax.ShapeDtypeStruct((count, KVR + ROPE), bf16),
         ],
         scratch_shapes=[pltpu.VMEM((count, WIDE), f32), pltpu.VMEM((count, VHEAD), f32)],
         compiler_params=pltpu.CompilerParams(vmem_limit_bytes=48 * megabytes),
@@ -614,7 +601,7 @@
     return results[:4], results[4:]
 
 
-def expert_layers(pieces, ups, pick, gates, gate_w, up_w, down_w, sgate, sup, sdown):
+def expert_work(pick, gates, gate_w, up_w, down_w, sgate, sup, sdown):
     ctx, slots, part = pick.shape
     width, hidden = sgate.shape
     parts = len(gate_w)
@@ -625,44 +612,26 @@
     rows = (whole(ctx * slots, width), 0)
     units = [(whole(ctx * slots, w), 0) for w in inner]
     shared = (whole(ctx, part, hidden), 0)
-    count = len(pieces)
-    flops = 6 * (ctx * slots * width * sum(inner) + ctx * part * width * hidden) // count
-    forward = functools.partial(forward_kernel, parts)
-    backward = functools.partial(backward_kernel, parts)
+    flops = 48 * (slots * width * sum(inner) + part * width * hidden)
     forward_shapes = [blocks, rows, rows, shared, shared, shared, *units * 3]
-    backward_shapes = [
-        blocks, rows, (whole(ctx, 1, part, dtype=f32), 0), (whole(2, ctx, part, hidden), 1), *units * 2
-    ]
-    outs, dbs, out_hops, db_hops, done, back = [], [], [], [], [], []
-    for piece in range(count):
-        out, done = expert_call(
-            forward, "experts_forward", piece, pieces[piece], [pick, gates], weights,
-            forward_shapes, done, part, width, flops,
+    dgates = (whole(ctx, 1, part, dtype=f32), 0)
+    backward_shapes = [blocks, rows, dgates, (whole(2, ctx, part, hidden), 1), *units * 2]
+
+    def forward(piece, tokens, held):
+        return expert_call(
+            functools.partial(forward_kernel, parts), "experts_forward", piece, tokens, [pick, gates],
+            weights, forward_shapes, held, part, width, flops,
         )
-        if piece == 1 and exchanges():
-            out, done, out_hops = together(out, done, out_hops)
-        outs.append(out)
-        if exchanges():
-            out_hops = [*out_hops, *plane_hops([out])]
-    tokens, entries, y, mid, sg, su, *units = done
-    m, g, u = (units[i * parts : (i + 1) * parts] for i in range(3))
-    for piece in range(count):
-        db, back = expert_call(
-            backward, "experts_backward", piece, ups[piece], [pick, gates, y, sg, su, *g, *u], weights,
-            backward_shapes, back, part, width, flops,
+
+    def backward(piece, upstream, done, held):
+        _, _, y, _, sg, su, *units = done
+        tiled = [pick, gates, y, sg, su, *units[parts:]]
+        return expert_call(
+            functools.partial(backward_kernel, parts), "experts_backward", piece, upstream, tiled,
+            weights, backward_shapes, held, part, width, flops,
         )
-        if exchanges():
-            if piece == 0:
-                db, back, out_hops = together(db, back, out_hops)
-            else:
-                db, back, db_hops = together(db, back, db_hops)
-            if piece == 0:
-                db_hops = plane_hops([db])
-        dbs.append(db)
-    ups_flat, dy, dgates, pair, *units = back
-    dg, du = (units[i * parts : (i + 1) * parts] for i in range(2))
-    sources = tokens, ups_flat, mid, pair[0], pair[1]
-    return (outs, out_hops), (dbs, db_hops), sources, entries, dy, dgates, m, dg, du
+
+    return forward, backward
 
 
 def shards(
@@ -741,11 +710,11 @@
     column_blocks = jnp.concatenate(columns, axis=-1)
     expand_end = WIDE + columns[2].shape[-1]
 
-    def joined_stage(received):
+    def joined_stage(received, _):
         return received, join_rows(gather_fsdp(received[..., :expand_end]))
 
     tokens_all, (received, by_rows) = gather_ctx(
-        tokens_low, lambda _: None, lambda _: None, lambda _: to_owner(column_blocks), joined_stage
+        tokens_low, *[lambda *_: None] * 2, lambda *_: to_owner(column_blocks), joined_stage
     )
     named_all = received[..., expand_end:].reshape(ctx, part)
     query_w = by_rows[:, :WIDE]
@@ -789,17 +758,17 @@
 
     query_pos = query_rows(jnp.arange(length, dtype=jnp.int32)[:, None])
 
-    def first_stage(_):
+    def first_stage(*_):
         return project(
             tokens_all, attn_gain[None], kv_gain[None], table, query_w, small_full, expand
         )
 
-    def second_stage(projected):
+    def second_stage(projected, _):
         _, query_all, key_head, value_head, _ = projected
         outcome = attend(query_pos, query_rows(query_all), key_head, value_head)
         return projected, outcome, to_owner(shared_blocks)
 
-    def third_stage(held):
+    def third_stage(held, _):
         projected, (outcome, outcome_low, lse), shared_in = held
         shared_in = join_rows(gather_fsdp(shared_in))
         return projected, outcome, lse, from_heads(outcome_low), shared_in
@@ -820,16 +789,46 @@
     chosen = jnp.sum(jnp.where(chosen_hot, logits[:, None, :], 0.0), axis=-1)
     gate_share = jax.nn.softmax(chosen, axis=-1)
     gates_own = jnp.sum(jnp.where(chosen_hot, gate_share[..., None], 0.0), axis=1)
-    ffn_all, gates_all = gather_ctx(ffn_low, lambda _: None, lambda _: to_owner(gates_own.T))
+
+    work = lambda gates_all: expert_work(
+        pick, gates_all[:, None, :], gate_parts, up_parts, down_parts, *shared_in, shared_back
+    )
+
+    def near_forward(gates_all, pieces):
+        forward, _ = work(gates_all)
+        return gates_all, forward(0, pieces[0], [])
+
+    def near_backward(held, _):
+        gates_all, (out, done) = held
+        arrived = plane_hops([out]) if exchanges() else []
+        db, back = work(gates_all)[1](0, upstream_all[0], done, [])
+        return gates_all, out, done, db, back, arrived
+
+    ffn_all, (gates_all, out, done, db, back, out_arrived) = gather_ctx(
+        ffn_low, lambda *_: None, lambda *_: to_owner(gates_own.T), near_forward, near_backward
+    )
+    forward, backward = work(gates_all)
+    out_parts, grad_parts, grad_arrived = [out], [db], []
+    for piece in range(1, len(ffn_all)):
+        if exchanges():
+            grad_arrived = plane_hops([db])
+        out, done = forward(piece, ffn_all[piece], done)
+        out, done, grad_arrived = together(out, done, grad_arrived)
+        if exchanges():
+            out_arrived = [*out_arrived, *plane_hops([out])]
+        db, back = backward(piece, upstream_all[piece], done, back)
+        db, back, out_arrived = together(db, back, out_arrived)
+        out_parts.append(out)
+        grad_parts.append(db)
     query_late, _ = lax.optimization_barrier((w_query, ffn_all[-1][3][1][0]))
     query_full = lax.all_gather(query_late, everywhere, axis=0, tiled=True)
-    (out_parts, out_arrived), (grad_parts, grad_arrived), *rest = expert_layers(
-        ffn_all, upstream_all, pick, gates_all[:, None, :], gate_parts, up_parts, down_parts,
-        *shared_in, shared_back,
-    )
-    flat, entries, grad_entries, token_dgates, middle, gate_low, up_low = rest
+    tokens_flat, entries, _, shared_mid, _, _, *units = done
+    middle = units[:fsdp]
+    upstream_flat, grad_entries, token_dgates, shared_pair, *units = back
+    gate_low, up_low = units[:fsdp], units[fsdp:]
     tokens_flat, upstream_flat, shared_mid, *shared_pair = (
-        v.reshape(length, v.shape[-1]) for v in flat
+        v.reshape(length, v.shape[-1])
+        for v in (tokens_flat, upstream_flat, shared_mid, shared_pair[0], shared_pair[1])
     )
 
     sums = [(middle, grad_entries), (gate_low, entries), (up_low, entries)]
@@ -840,6 +839,39 @@
         grad_parts, (sums, to_owner(token_dgates[:, 0])), (shared_sums, query_full), grad_arrived
     )
     grad_gates = jnp.sum(jnp.where(chosen_hot, dgates_own.T[:, None, :], 0.0), axis=-1)
+    grad_chosen = gate_share * (
+        grad_gates - jnp.sum(gate_share * grad_gates, axis=-1, keepdims=True)
+    )
+    grad_logits = jnp.sum(jnp.where(chosen_hot, grad_chosen[..., None], 0.0), axis=1).astype(bf16)
+    grad_router = mm_tn(ffn_low, grad_logits)
+    ffn_grad = ffn_grad + mm_nt(grad_logits, router_full)
+    upstream = upstream_low.astype(f32)
+    ffn_grad_in, grad_ffn_gain = rms_backward(residual, ffn_factor, ffn_gain, ffn_grad)
+    grad_residual = upstream + ffn_grad_in
+    grad_residual_low = grad_residual.astype(bf16)
+
+    grad_attended = mm_nt(grad_residual_low, output_full).astype(bf16)
+    grad_head = to_heads(grad_attended.reshape(part, HEADS, VHEAD))
+    output_heads = attended.reshape(part, ctx, fsdp, rows)
+    output_heads = in_fsdp_order([output_heads[:, :, i].reshape(part, -1) for i in range(fsdp)])
+    grad_output = scatter_fsdp([mm_tn(v, grad_residual_low) for v in output_heads])
+    grad_output = grad_output.astype(bf16).reshape(ctx, rows, width)
+    grad_output = lax.psum_scatter(grad_output, "ctx", scatter_dimension=0).astype(f32)
+    attention_grads = attend_grad(
+        query_pos, query_rows(table), query_head, key_head, value_head, outcome, lse, grad_head, expand
+    )
+    if exchanges():
+        out_sum, out_line = line_hops(out_parts, out_arrived)
+        attention_grads, out_line = together(attention_grads, out_line)
+        out_sum = plus(out_sum, *out_line)
+    else:
+        out_sum = whole_sum(out_parts)
+    grad_query, grad_expanded, latent_part = attention_grads
+    latent_part, query_own, sums, shared_sums = together(
+        to_owner(latent_part.reshape(ctx, part, -1)), from_heads(grad_query), sums, shared_sums
+    )
+    latent_sum = jnp.sum(latent_part.astype(f32), axis=0)
+    grad_normed = mm_nt(query_own.reshape(part, HEADS * QK), query_full)
     grad_expert_down, grad_expert_gate, grad_expert_up = (scatter_fsdp(v).T[None] for v in sums)
     down_rows = shared_down.shape[0]
     grad_back = shared_sums[0].reshape(fsdp, down_rows, width)
@@ -847,60 +879,6 @@
     grad_in = to_rows(jnp.concatenate(shared_sums[1:], axis=-1), rows).transpose(1, 0, 2)
     grad_shared_gate = grad_in[..., :hidden_shared].reshape(rows, ctx * hidden_shared)
     grad_shared_up = grad_in[..., hidden_shared:].reshape(rows, ctx * hidden_shared)
-
-    grad_chosen = gate_share * (
-        grad_gates - jnp.sum(gate_share * grad_gates, axis=-1, keepdims=True)
-    )
-    grad_logits = jnp.sum(jnp.where(chosen_hot, grad_chosen[..., None], 0.0), axis=1).astype(bf16)
-    grad_router = mm_tn(ffn_low, grad_logits)
-    ffn_grad = ffn_grad + mm_nt(grad_logits, router_full)
-    upstream = upstream_low.astype(f32)
-    ffn_grad_in, grad_ffn_gain = rms_backward(residual, ffn_factor, ffn_gain, ffn_grad)
-    grad_residual = upstream + ffn_grad_in
-    grad_residual_low = grad_residual.astype(bf16)
-
-    grad_attended = mm_nt(grad_residual_low, output_full).astype(bf16)
-    grad_head = to_heads(grad_attended.reshape(part, HEADS, VHEAD))
-    output_heads = attended.reshape(part, ctx, fsdp, rows)
-    if exchanges():
-        output_heads = jnp.take(output_heads, piece_order(), axis=1, mode="clip")
-    output_heads = in_fsdp_order([output_heads[:, :, i].reshape(part, -1) for i in range(fsdp)])
-    grad_output = [mm_tn(v, grad_residual_low) for v in output_heads]
-    grad_output = scatter_fsdp(grad_output).astype(bf16).reshape(ctx, rows, width)
-    if exchanges():
-        grad_output = grad_output.reshape(2, 4, 2, rows, width)
-        output_pieces = [[grad_output[p, m] for m in range(4)] for p in range(2)]
-    else:
-        output_pieces = in_pieces(grad_output)
-    attention_grads = attend_grad(
-        query_pos, query_rows(table), query_head, key_head, value_head, outcome, lse, grad_head, expand
-    )
-    latent_blocks = lambda v: in_pieces(v.reshape(ctx, part, KVR + LANES))
-    if exchanges():
-        out_sum, out_line = line_hops(out_parts, out_arrived)
-        attention_grads, output_arrived, out_line = together(
-            attention_grads, plane_hops(output_pieces), out_line
-        )
-        out_sum = plus(out_sum, *out_line)
-        grad_query, grad_expanded, latent_part = attention_grads
-        output_sum, output_line = line_hops(output_pieces, output_arrived)
-        latent_pieces = latent_blocks(latent_part)
-        arrived, output_line, query_own = together(
-            plane_hops(latent_pieces), output_line, from_heads(grad_query)
-        )
-        grad_output = plus(output_sum, *output_line)
-        latent_sum, latent_line = line_hops(latent_pieces, arrived)
-        grad_normed = mm_nt(query_own.reshape(part, HEADS * QK), query_full)
-        latent_line, grad_normed, grad_query, grad_expanded = together(
-            latent_line, grad_normed, grad_query, grad_expanded
-        )
-        latent_sum = plus(latent_sum, *latent_line)
-    else:
-        grad_query, grad_expanded, latent_part = attention_grads
-        out_sum = whole_sum(out_parts)
-        grad_output = whole_sum(output_pieces)
-        latent_sum = whole_sum(latent_blocks(latent_part))
-        grad_normed = mm_nt(from_heads(grad_query).reshape(part, HEADS * QK), query_full)
 
     grad_query_w = mm_tn(query_rows(normed_all), grad_query).reshape(ctx, fsdp, rows, QK)
     grad_expand = mm_tn(latent_all, grad_expanded).reshape(ctx, fsdp, rows, -1)
@@ -930,7 +908,7 @@
         axis=1,
     ).reshape(ctx, fsdp, rows, -1)
     grad_small = scatter_fsdp(in_fsdp_order([grad_small[:, i] for i in range(fsdp)]))
-    grad_small, _, _ = scatter_ctx(in_pieces(grad_small.astype(bf16)))
+    grad_small = jnp.sum(to_owner(grad_small.astype(bf16)).astype(f32), axis=0)
     grad_reduce = grad_small[:, :compressed_width]
     grad_normed = grad_normed + mm_nt(grad_compressed, reduce_full)
     attn_grad_in, _ = rms_backward(tokens, rms_factor(tokens), attn_gain, grad_normed)

time: 1000 us -> 976 us (0.976)
  waiting for transfers between devices: 342 us -> 369 us
  starting transfers between devices: 156 us -> 135 us
  blocking collectives: 19 us -> 0 us
  other arithmetic: 100 us -> 83.5 us
    all_to_all x8 -> x11, waiting for transfers between devices: 18.5 us -> 96.2 us  [to_owner(): lax.all_to_all(blocks, 'ctx', split_axis=0, concat_axis=0, tiled=True)]
    ppermute x84 -> x57, waiting for transfers between devices: 319 us -> 270 us  [hop(): return lax.ppermute(value, 'ctx', [(i, i ^ mask) for i in range(16)])]
    ppermute x84 -> x57, starting transfers between devices: 106 us -> 70.5 us  [hop(): return lax.ppermute(value, 'ctx', [(i, i ^ mask) for i in range(16)])]
    all_to_all x1 -> x0, blocking collectives: 19 us -> none  [to_owner(): lax.all_to_all(blocks, 'ctx', split_axis=0, concat_axis=0, tiled=True)]
    all_to_all x8 -> x11, starting transfers between devices: 47.7 us -> 62.8 us  [to_owner(): lax.all_to_all(blocks, 'ctx', split_axis=0, concat_axis=0, tiled=True)]
    unnamed x231 -> x194, local copies, waits for them, and re-layouts: 25.8 us -> 18.8 us
  transfers between devices with their start and end apart: 109 -> 86, of which waited for: 43 -> 36; matrix products, arithmetic and copies ran while one was open for 23% -> 25% of each run, Pallas kernels for 18% -> 19%
where the time goes in v1:
time: 976 us; the launch traced here: 966 us
  waiting for transfers between devices  369 us (38%)
  Pallas kernels  183 us (19%)
  starting transfers between devices  135 us (14%)
  local copies, waits for them, and re-layouts  90.6 us (9%)
  matrix products  89.4 us (9%)
  other arithmetic  83.5 us (9%)
  between operations  15.5 us (2%)
    ppermute x57, waiting for transfers between devices, hop(): return lax.ppermute(value, 'ctx', [(i, i ^ mask) for i in range(16)])  270 us
    pallas_call x4, Pallas kernels, expert_call(): pl.pallas_call(kernel, grid_spec=pltpu.PrefetchScalarGridSpec(num_scalar_...  130 us
    all_to_all x11, waiting for transfers between devices, to_owner(): lax.all_to_all(blocks, 'ctx', split_axis=0, concat_axis=0, tiled=True)  96.2 us
    ppermute x57, starting transfers between devices, hop(): return lax.ppermute(value, 'ctx', [(i, i ^ mask) for i in range(16)])  70.5 us
    all_to_all x11, starting transfers between devices, to_owner(): lax.all_to_all(blocks, 'ctx', split_axis=0, concat_axis=0, tiled=True)  62.8 us
    dot_general x15, matrix products, mm_tn(): lax.dot_general(left, right, (((0,), (0,)), ((), ())), preferred_element_...  61 us
    pallas_call x2, Pallas kernels, project(): pl.pallas_call(project_kernel, grid_spec=pltpu.PrefetchScalarGridSpec(num...  24.2 us
    dot_general x4, matrix products, mm_nt(): lax.dot_general(left, right, (((1,), (1,)), ((), ())), preferred_element_...  19.9 us
  transfers between devices with their start and end apart: 86, of which 36 were waited for; matrix products, arithmetic and copies ran while one was open for 25% of the time, Pallas kernels for 19%

profile of v1, /device:TPU:8, one launch (start us, length us, event | category | flops | bytes accessed | tf_op | source)
XLA Modules:
  0.0 965.9 jit_solution(5178368692072262731)
XLA Ops:
  20.4 18.1 %collective-permute-done = bf16[128,2048]{1,0:T(8,128)(2,1)} collective-permute-done((bf16[128,2048]{1,0:T(8,128)(2,1)}, bf16[128,2048]{1,0:T(8,128)(2,1)}, u32[]{:S(2)}, u32[]{:S(2)}) %collective-permute-start) | collective-permute-done | bytes 524320 | tf_op jit(solution)/shard_map/ppermute | solution.py:89
  54.3 5.5 all-to-all-start
  60.4 10.1 %collective-permute-done.7 = bf16[128,2048]{1,0:T(8,128)(2,1)} collective-permute-done((bf16[128,2048]{1,0:T(8,128)(2,1)}, bf16[128,2048]{1,0:T(8,128)(2,1)}, u32[]{:S(2)}, u32[]{:S(2)}) %collective-permute-start.7) | collective-permute-done | bytes 524320 | tf_op jit(solution)/shard_map/ppermute | solution.py:89
  70.5 13.3 %collective-permute-done.8 = bf16[128,2048]{1,0:T(8,128)(2,1)} collective-permute-done((bf16[128,2048]{1,0:T(8,128)(2,1)}, bf16[128,2048]{1,0:T(8,128)(2,1)}, u32[]{:S(2)}, u32[]{:S(2)}) %collective-permute-start.8) | collective-permute-done | bytes 524320 | tf_op jit(solution)/shard_map/ppermute | solution.py:89
  83.8 11.1 %collective-permute-done.5 = bf16[128,2048]{1,0:T(8,128)(2,1)} collective-permute-done((bf16[128,2048]{1,0:T(8,128)(2,1)}, bf16[128,2048]{1,0:T(8,128)(2,1)}, u32[]{:S(2)}, u32[]{:S(2)}) %collective-permute-start.5) | collective-permute-done | bytes 524320 | tf_op jit(solution)/shard_map/ppermute | solution.py:89
  104.7 14.8 %collective-permute-done.10.refs_4_.refs_5_ = bf16[2,128,2048]{2,1,0:T(8,128)(2,1)S(1)} collective-permute-done((bf16[2,128,2048]{2,1,0:T(8,128)(2,1)S(1)}, bf16[2,128,2048]{2,1,0:T(8,128)(2,1)S(1)}, u32[]{:S(2)}, u32[]{:S(2)}) %collective-permute-start.10) | collective-permute-done | bytes 1048608 | tf_op jit(solution)/shard_map/ppermute | solution.py:89
  124.7 17.4 %collective-permute-done.12 = bf16[128,2048]{1,0:T(8,128)(2,1)S(1)} collective-permute-done((bf16[128,2048]{1,0:T(8,128)(2,1)S(1)}, bf16[128,2048]{1,0:T(8,128)(2,1)S(1)}, u32[]{:S(2)}, u32[]{:S(2)}) %collective-permute-start.12) | collective-permute-done | bytes 524320 | tf_op jit(solution)/shard_map/ppermute | solution.py:89
  162.3 12.1 %project.2 = (bf16[2048,2048]{1,0:T(8,128)(2,1)}, bf16[2048,256]{1,0:T(8,128)(2,1)}, bf16[2048,256]{1,0:T(8,128)(2,1)}, bf16[2048,128]{1,0:T(8,128)(2,1)}, bf16[2048,512]{1,0:T(8,128)(2,1)}) custom-call(s32[3]{0:T(128)} %get-tuple-element.734.base_ref, bf16[1,128,2048]{2,1,0:T(8,128)(2,1)} %refs_0_.1, bf16[1,128,2048]{2,1,0:T(8,128)(2,1)} %bitcast.25.refs_1_, ...), custom_call_target="tpu_custom_call" | custom-call | flops 3758096384 | bytes 12058624 | tf_op jit(solution)/shard_map/project/pallas_call | solution.py:262
  174.3 12.1 %project.3 = (bf16[2048,2048]{1,0:T(8,128)(2,1)}, bf16[2048,256]{1,0:T(8,128)(2,1)}, bf16[2048,256]{1,0:T(8,128)(2,1)}, bf16[2048,128]{1,0:T(8,128)(2,1)}, bf16[2048,512]{1,0:T(8,128)(2,1)}) custom-call(s32[3]{0:T(128)} %get-tuple-element.733.base_ref, ...), custom_call_target="tpu_custom_call", output_to_operand_aliasing={{0}: (15, {}), {1}: (16, {}), {2}: (17, {}), {3}: (18, {}),... | custom-call | flops 3758096384 | bytes 12058624 | tf_op jit(solution)/shard_map/project/pallas_call | solution.py:262
  194.5 11.3 %attend.1 = (f32[2048,128]{1,0:T(8,128)S(1)}, bf16[2048,128]{1,0:T(8,128)(2,1)S(1)}, f32[2048,1]{1,0:T(8,128)S(1)}) custom-call(s32[2048,1]{1,0:T(8,128)S(1)} %iota.38.pos_ref, bf16[2048,256]{1,0:T(8,128)(2,1)S(1)} %copy-done.2, bf16[2048,256]{1,0:T(8,128)(2,1)} %get-tuple-element.488.key_ref, bf16[2048,128]{1,0:T(8,128)(2,1)S(1)} %copy-done.3), custom_call_target="tpu_custom_call" | custom-call | flops 2684354560 | bytes 5242880 | tf_op jit(solution)/shard_map/attend/pallas_call | solution.py:386
  207.8 7.0 collective-permute-done.18
  217.5 10.3 %collective-permute-done.22 = bf16[128,2048]{1,0:T(8,128)(2,1)} collective-permute-done((bf16[128,2048]{1,0:T(8,128)(2,1)S(1)}, bf16[128,2048]{1,0:T(8,128)(2,1)}, u32[]{:S(2)}, u32[]{:S(2)}) %collective-permute-start.22) | collective-permute-done | bytes 524320 | tf_op jit(solution)/shard_map/ppermute | solution.py:89
  232.1 5.9 all-to-all-start.2
  243.7 15.1 %all-to-all-done.2 = bf16[16,128,128]{1,2,0:T(8,128)(2,1)S(1)} async-done(((bf16[16,128,128]{1,2,0:T(8,128)(2,1)}), bf16[16,128,128]{1,2,0:T(8,128)(2,1)S(1)}, u32[]{:S(2)}, u32[]{:S(2)}) %all-to-all-start.2) | async-done | bytes 524320 | tf_op jit(solution)/shard_map/all_to_all | solution.py:207
  263.4 8.7 collective-permute-done.26
  284.7 13.6 %collective-permute-done.28 = bf16[128,2048]{1,0:T(8,128)(2,1)S(1)} collective-permute-done((bf16[128,2048]{1,0:T(8,128)(2,1)S(1)}, bf16[128,2048]{1,0:T(8,128)(2,1)S(1)}, u32[]{:S(2)}, u32[]{:S(2)}) %collective-permute-start.28) | collective-permute-done | bytes 524320 | tf_op jit(solution)/shard_map/ppermute | solution.py:89
  309.5 9.3 collective-permute-done.32
  320.4 6.6 all-to-all-start.3
  328.6 5.7 collective-permute-done.34
  337.8 13.7 %collective-permute-done.35 = bf16[128,2048]{1,0:T(8,128)(2,1)} collective-permute-done((bf16[128,2048]{1,0:T(8,128)(2,1)}, bf16[128,2048]{1,0:T(8,128)(2,1)}, u32[]{:S(2)}, u32[]{:S(2)}) %collective-permute-start.35) | collective-permute-done | bytes 524320 | tf_op jit(solution)/shard_map/ppermute | solution.py:89
  355.6 29.3 %experts_forward.2 = (bf16[2,128,2048]{2,1,0:T(8,128)(2,1)}, bf16[2,128,2048]{2,1,0:T(8,128)(2,1)}, bf16[2,128,2048]{2,1,0:T(8,128)(2,1)}, bf16[2,128,2048]{2,1,...) custom-call(s32[3]{0:T(128)} %get-tuple-element.734.base_ref, ...), custom_call_target="tpu_custom_call" | custom-call | flops 11072962560 | bytes 41943040 | tf_op jit(solution)/shard_map/experts_forward/pallas_call | solution.py:578
  392.3 34.6 %experts_backward.2 = (bf16[2,128,2048]{2,1,0:T(8,128)(2,1)}, bf16[2,128,2048]{2,1,0:T(8,128)(2,1)}, bf16[2,128,2048]{2,1,0:T(8,128)(2,1)}, bf16[2,128,2048]{2,1...) custom-call(s32[3]{0:T(128)} %get-tuple-element.734.base_ref, ...), custom_call_target="tpu_custom_call" | custom-call | flops 11072962560 | bytes 41943040 | tf_op jit(solution)/shard_map/experts_backward/pallas_call | solution.py:578
  427.0 14.5 %collective-permute-done.46 = bf16[128,2048]{1,0:T(8,128)(2,1)S(1)} collective-permute-done((bf16[128,2048]{1,0:T(8,128)(2,1)}, bf16[128,2048]{1,0:T(8,128)(2,1)S(1)}, u32[]{:S(2)}, u32[]{:S(2)}) %collective-permute-start.46) | collective-permute-done | bytes 524320 | tf_op jit(solution)/shard_map/ppermute | solution.py:89
  445.8 29.8 %experts_forward.3 = (bf16[2,128,2048]{2,1,0:T(8,128)(2,1)}, bf16[2,128,2048]{2,1,0:T(8,128)(2,1)}, bf16[2,128,2048]{2,1,0:T(8,128)(2,1)}, bf16[2,128,2048]{2,1,...) custom-call(s32[3]{0:T(128)} %get-tuple-element.733.base_ref, ...), custom_call_target="tpu_custom_call", output_to_operand_aliasing={{4}: (20, {}), {5}: (21, {}), {6}: (22, {}), {7}: (23, {}),... | custom-call | flops 11072962560 | bytes 41943040 | tf_op jit(solution)/shard_map/experts_forward/pallas_call | solution.py:578
  476.7 25.2 %collective-permute-done.50 = bf16[2,128,2048]{2,1,0:T(8,128)(2,1)} collective-permute-done((bf16[2,128,2048]{2,1,0:T(8,128)(2,1)}, bf16[2,128,2048]{2,1,0:T(8,128)(2,1)}, u32[]{:S(2)}, u32[]{:S(2)}) %collective-permute-start.50) | collective-permute-done | bytes 1048608 | tf_op jit(solution)/shard_map/ppermute | solution.py:89
  506.3 36.5 %experts_backward.3 = (bf16[2,128,2048]{2,1,0:T(8,128)(2,1)}, bf16[2,128,2048]{2,1,0:T(8,128)(2,1)}, bf16[2,128,2048]{2,1,0:T(8,128)(2,1)}, bf16[2,128,2048]{2,1...) custom-call(s32[3]{0:T(128)} %get-tuple-element.733.base_ref, ...), custom_call_target="tpu_custom_call", output_to_operand_aliasing={{4}: (27, {}), {5}: (28, {}), {6}: (29, {}), {7}: (30, {}),... | custom-call | flops 11072962560 | bytes 41943040 | tf_op jit(solution)/shard_map/experts_backward/pallas_call | solution.py:578
  544.6 5.7 collective-permute-done.52
  550.3 18.0 %collective-permute-done.53 = bf16[2,128,2048]{2,1,0:T(8,128)(2,1)} collective-permute-done((bf16[2,128,2048]{2,1,0:T(8,128)(2,1)}, bf16[2,128,2048]{2,1,0:T(8,128)(2,1)}, u32[]{:S(2)}, u32[]{:S(2)}) %collective-permute-start.53) | collective-permute-done | bytes 1048608 | tf_op jit(solution)/shard_map/ppermute | solution.py:89
  578.5 6.9 all-to-all-start.4
  585.5 6.4 fusion.65
  615.7 5.2 fusion.61
  639.7 27.0 %collective-permute-done.58 = bf16[128,2048]{1,0:T(8,128)(2,1)S(1)} collective-permute-done((bf16[128,2048]{1,0:T(8,128)(2,1)S(1)}, bf16[128,2048]{1,0:T(8,128)(2,1)S(1)}, u32[]{:S(2)}, u32[]{:S(2)}) %collective-permute-start.58) | collective-permute-done | bytes 524320 | tf_op jit(solution)/shard_map/ppermute | solution.py:89
  666.6 11.1 %collective-permute-done.59 = bf16[128,2048]{1,0:T(8,128)(2,1)S(1)} collective-permute-done((bf16[128,2048]{1,0:T(8,128)(2,1)S(1)}, bf16[128,2048]{1,0:T(8,128)(2,1)S(1)}, u32[]{:S(2)}, u32[]{:S(2)}) %collective-permute-start.59) | collective-permute-done | bytes 524320 | tf_op jit(solution)/shard_map/ppermute | solution.py:89
  682.2 6.7 fusion.7
  690.0 5.6 all-to-all-start.5
  699.8 10.4 %all-to-all-done.5 = bf16[16,128,128]{2,1,0:T(8,128)(2,1)S(1)} async-done(((bf16[16,128,128]{2,1,0:T(8,128)(2,1)}), bf16[16,128,128]{2,1,0:T(8,128)(2,1)S(1)}, u32[]{:S(2)}, u32[]{:S(2)}) %all-to-all-start.5) | async-done | bytes 524320 | tf_op jit(solution)/shard_map/all_to_all | solution.py:207
  713.2 17.4 %attend_grad.1 = (bf16[2048,192]{1,0:T(8,128)(2,1)S(1)}, bf16[2048,256]{1,0:T(8,128)(2,1)S(1)}, bf16[2048,576]{1,0:T(8,128)(2,1)}) custom-call(s32[2048,1]{1,0:T(8,128)S(1)} %iota.39.pos_ref, f32[2048,128]{1,0:T(8,128)S(1)} %copy-done, bf16[2048,256]{1,0:T(8,128)(2,1)} %get-tuple-element.487.query_ref, bf16[2048,256]{1,0:T(8,128)(2,1)} %get-tuple-element.488.key_ref, ...), custom_call_target="tpu_custom_call" | custom-call | flops 6979321856 | bytes 10485760 | tf_op jit(solution)/shard_map/attend_grad/pallas_call | solution.py:411
  739.6 6.0 fusion.66
  749.0 7.0 all-to-all-done.7
  798.6 5.5 add_convert_fusion
  804.2 37.0 %all-to-all-done.6 = bf16[16,128,576]{1,2,0:T(8,128)(2,1)S(1)} async-done(((bf16[16,128,576]{1,2,0:T(8,128)(2,1)}), bf16[16,128,576]{1,2,0:T(8,128)(2,1)S(1)}, u32[]{:S(2)}, u32[]{:S(2)}) %all-to-all-start.6) | async-done | bytes 2359328 | tf_op jit(solution)/shard_map/all_to_all | solution.py:207
  867.8 9.9 %fusion.8 = (f32[128]{0:T(128)S(1)}, f32[128]{0:T(128)S(1)}, f32[128,2048]{1,0:T(8,128)}) fusion(bf16[1,128,2048]{2,1,0:T(8,128)(2,1)S(1)} %copy-done.31, f32[2048]{0:T(1024)S(1)} %copy-done.76, f32[128,2048]{1,0:T(8,128)S(1)} %fusion, bf16[128,3072]{0,1:T(8,128)(2,1)S(1)} %bitcast.309, bf16[2048,3072]{1,0:T(8,128)(2,1)} %all-gather.8.cloned.1.call-done), kind=kOutput, calls=%fused_computation.41 | convolution fusion | flops 1612447488 | bytes 16000000 | tf_op jit(solution)/shard_map/dot_general | solution.py:33
  882.5 7.0 all-to-all-start.10
  898.2 18.6 %all-to-all-done.10 = bf16[16,64,352]{2,1,0:T(8,128)(2,1)S(1)} async-done(((bf16[16,64,352]{2,1,0:T(8,128)(2,1)}), bf16[16,64,352]{2,1,0:T(8,128)(2,1)S(1)}, u32[]{:S(2)}, u32[]{:S(2)}) %all-to-all-start.10) | async-done | bytes 720928 | tf_op jit(solution)/shard_map/all_to_all | solution.py:207
  917.7 5.9 all-to-all-start.9
  933.9 7.5 add_bitcast_fusion
  941.5 5.3 add_bitcast_fusion.1
  946.8 5.7 add_bitcast_fusion.2
  (508 shorter events, 323.0 us)
Async XLA Ops:
  7.2 150.3 %all-gather.4.cloned.1.call-start = ((), (), s32[]{:S(2)}) async-start(), calls=%async_computation.12 | async-start | bytes 3244032 | tf_op jit(solution)/shard_map/all_gather | solution.py:690
  12.9 261.4 %all-gather.6.cloned.1.call-start = ((), (), s32[]{:S(2)}) async-start(), calls=%async_computation.13 | async-start | bytes 8650752 | tf_op jit(solution)/shard_map/all_gather | solution.py:722
  45.0 38.8 %collective-permute-start.8 = (bf16[128,2048]{1,0:T(8,128)(2,1)}, bf16[128,2048]{1,0:T(8,128)(2,1)}, u32[]{:S(2)}, u32[]{:S(2)}) collective-permute-start(bf16[128,2048]{1,0:T(8,128)(2,1)} %collective-permute-done), channel_id=1, source_target_pairs={{0,6},{2,4},{4,2},{6,0},{8,14},{10,12},{12,10},{14,8},{16,22},{18,... | collective-permute-start | bytes 1572872 | tf_op jit(solution)/shard_map/ppermute | solution.py:89
  45.5 38.3 %collective-permute-start.4 = (bf16[128,2048]{1,0:T(8,128)(2,1)S(1)}, bf16[128,2048]{1,0:T(8,128)(2,1)S(1)}, u32[]{:S(2)}, u32[]{:S(2)}) collective-permute-start(bf16[128,2048]{1,0:T(8,128)(2,1)S(1)} %collective-permute-done.1), channel_id=1, source_target_pairs={{0,8},{2,10},{4,12},{6,14},{8,0},{10,2},{12,4},{14,6},{16,24},{18,... | collective-permute-start | bytes 1572872 | tf_op jit(solution)/shard_map/ppermute | solution.py:89
  47.0 47.9 %collective-permute-start.5 = (bf16[128,2048]{1,0:T(8,128)(2,1)}, bf16[128,2048]{1,0:T(8,128)(2,1)}, u32[]{:S(2)}, u32[]{:S(2)}) collective-permute-start(bf16[128,2048]{1,0:T(8,128)(2,1)} %collective-permute-done.3), channel_id=1, source_target_pairs={{0,2},{2,0},{4,6},{6,4},{8,10},{10,8},{12,14},{14,12},{16,18},{18,... | collective-permute-start | bytes 1572872 | tf_op jit(solution)/shard_map/ppermute | solution.py:89
  54.3 50.4 %all-to-all-start = ((bf16[16,64,322]{2,1,0:T(8,128)(2,1)}), bf16[16,64,322]{2,1,0:T(8,128)(2,1)}, u32[]{:S(2)}, u32[]{:S(2)}) async-start(bf16[16,64,322]{2,1,0:T(8,128)(2,1)} %concatenate.39), calls=%async_computation | async-start | bytes 1572864 | tf_op jit(solution)/shard_map/all_to_all | solution.py:207
  143.3 43.2 %collective-permute-start.14 = (bf16[128,2048]{1,0:T(8,128)(2,1)}, bf16[128,2048]{1,0:T(8,128)(2,1)S(1)}, u32[]{:S(2)}, u32[]{:S(2)}) collective-permute-start(bf16[128,2048]{1,0:T(8,128)(2,1)} %bitcast.32), channel_id=1, source_target_pairs={{0,8},{2,10},{4,12},{6,14},{8,0},{10,2},{12,4},{14,6},{16,24},{18,... | collective-permute-start | bytes 1572872 | tf_op jit(solution)/shard_map/ppermute | solution.py:89
  143.3 43.2 %collective-permute-start.15 = (bf16[128,2048]{1,0:T(8,128)(2,1)}, bf16[128,2048]{1,0:T(8,128)(2,1)S(1)}, u32[]{:S(2)}, u32[]{:S(2)}) collective-permute-start(bf16[128,2048]{1,0:T(8,128)(2,1)} %bitcast.32), channel_id=1, source_target_pairs={{0,16},{2,18},{4,20},{6,22},{8,24},{10,26},{12,28},{14,30},{16,0},... | collective-permute-start | bytes 1572872 | tf_op jit(solution)/shard_map/ppermute | solution.py:89
  145.5 41.0 %collective-permute-start.16 = (bf16[128,2048]{1,0:T(8,128)(2,1)}, bf16[128,2048]{1,0:T(8,128)(2,1)S(1)}, u32[]{:S(2)}, u32[]{:S(2)}) collective-permute-start(bf16[128,2048]{1,0:T(8,128)(2,1)} %bitcast.32), channel_id=1, source_target_pairs={{0,2},{2,0},{4,6},{6,4},{8,10},{10,8},{12,14},{14,12},{16,18},{18,... | collective-permute-start | bytes 1572872 | tf_op jit(solution)/shard_map/ppermute | solution.py:89
  147.1 39.5 %collective-permute-start.17 = (bf16[128,2048]{1,0:T(8,128)(2,1)}, bf16[128,2048]{1,0:T(8,128)(2,1)}, u32[]{:S(2)}, u32[]{:S(2)}) collective-permute-start(bf16[128,2048]{1,0:T(8,128)(2,1)} %bitcast.32), channel_id=1, source_target_pairs={{0,4},{2,6},{4,0},{6,2},{8,12},{10,14},{12,8},{14,10},{16,20},{18,... | collective-permute-start | bytes 1572872 | tf_op jit(solution)/shard_map/ppermute | solution.py:89
  152.4 55.4 %all-to-all-start.1 = ((bf16[16,64,352]{2,1,0:T(8,128)(2,1)}), bf16[16,64,352]{2,1,0:T(8,128)(2,1)}, u32[]{:S(2)}, u32[]{:S(2)}) async-start(bf16[16,64,352]{2,1,0:T(8,128)(2,1)} %maximum_bitcast_fusion), calls=%async_computation.1 | async-start | bytes 1572864 | tf_op jit(solution)/shard_map/all_to_all | solution.py:207
  190.7 37.1 %collective-permute-start.22 = (bf16[128,2048]{1,0:T(8,128)(2,1)S(1)}, bf16[128,2048]{1,0:T(8,128)(2,1)}, u32[]{:S(2)}, u32[]{:S(2)}) collective-permute-start(bf16[128,2048]{1,0:T(8,128)(2,1)S(1)} %collective-permute-done.14), channel_id=1, source_target_pairs={{0,6},{2,4},{4,2},{6,0},{8,14},{10,12},{12,10},{14,8},{16,22},{18,... | collective-permute-start | bytes 1572872 | tf_op jit(solution)/shard_map/ppermute | solution.py:89
  227.9 30.9 %collective-permute-start.24 = (bf16[2,128,2048]{2,1,0:T(8,128)(2,1)S(1)}, bf16[2,128,2048]{2,1,0:T(8,128)(2,1)}, u32[]{:S(2)}, u32[]{:S(2)}) collective-permute-start(bf16[2,128,2048]{2,1,0:T(8,128)(2,1)S(1)} %pad_maximum_fusion.5.refs_0_.refs_1_), channel_id=1, source_target_pairs={{0,2},{2,0},{4,6},{6,4},{8,10},{10,8},{12,14},{14,12},{16,18},{18,... | collective-permute-start | bytes 3145736 | tf_op jit(solution)/shard_map/ppermute | solution.py:89
  282.3 73.3 %collective-permute-start.37 = (bf16[704,2048]{1,0:T(8,128)(2,1)}, bf16[704,2048]{1,0:T(8,128)(2,1)}, u32[]{:S(2)}, u32[]{:S(2)}) collective-permute-start(bf16[704,2048]{1,0:T(8,128)(2,1)} %bitcast.63.refs_10_.refs_17_), channel_id=1, source_target_pairs={{0,1},{1,0},{2,3},{3,2},{4,5},{5,4},{6,7},{7,6},{8,9},{9,8},{10,11... | collective-permute-start | bytes 8650760 | tf_op jit(solution)/shard_map/ppermute | solution.py:182
  298.3 57.3 %collective-permute-start.38 = (bf16[704,2048]{1,0:T(8,128)(2,1)}, bf16[704,2048]{1,0:T(8,128)(2,1)}, u32[]{:S(2)}, u32[]{:S(2)}) collective-permute-start(bf16[704,2048]{1,0:T(8,128)(2,1)} %bitcast.278), channel_id=1, source_target_pairs={{0,1},{1,0},{2,3},{3,2},{4,5},{5,4},{6,7},{7,6},{8,9},{9,8},{10,11... | collective-permute-start | bytes 8650760 | tf_op jit(solution)/shard_map/ppermute | solution.py:182
  301.7 53.8 %collective-permute-start.39 = (bf16[704,2048]{1,0:T(8,128)(2,1)}, bf16[704,2048]{1,0:T(8,128)(2,1)}, u32[]{:S(2)}, u32[]{:S(2)}) collective-permute-start(bf16[704,2048]{1,0:T(8,128)(2,1)} %bitcast.283), channel_id=1, source_target_pairs={{0,1},{1,0},{2,3},{3,2},{4,5},{5,4},{6,7},{7,6},{8,9},{9,8},{10,11... | collective-permute-start | bytes 8650760 | tf_op jit(solution)/shard_map/ppermute | solution.py:182
  327.0 351.5 %all-gather.8.cloned.1.call-start = ((), (), s32[]{:S(2)}) async-start(), calls=%async_computation.14 | async-start | bytes 12976128 | tf_op jit(solution)/shard_map/all_gather | solution.py:824
  351.6 33.3 %collective-permute-start.41 = (bf16[2,128,2048]{2,1,0:T(8,128)(2,1)S(1)}, bf16[2,128,2048]{2,1,0:T(8,128)(2,1)S(1)}, u32[]{:S(2)}, u32[]{:S(2)}) collective-permute-start(bf16[2,128,2048]{2,1,0:T(8,128)(2,1)S(1)} %pad_maximum_fusion.6.refs_0_.refs_1_), channel_id=1, source_target_pairs={{0,2},{2,0},{4,6},{6,4},{8,10},{10,8},{12,14},{14,12},{16,18},{18,... | collective-permute-start | bytes 3145736 | tf_op jit(solution)/shard_map/ppermute | solution.py:89
  353.2 31.8 %collective-permute-start.42 = (bf16[2,128,2048]{2,1,0:T(8,128)(2,1)S(1)}, bf16[2,128,2048]{2,1,0:T(8,128)(2,1)}, u32[]{:S(2)}, u32[]{:S(2)}) collective-permute-start(bf16[2,128,2048]{2,1,0:T(8,128)(2,1)S(1)} %pad_maximum_fusion.6.refs_0_.refs_1_), channel_id=1, source_target_pairs={{0,4},{2,6},{4,0},{6,2},{8,12},{10,14},{12,8},{14,10},{16,20},{18,... | collective-permute-start | bytes 3145736 | tf_op jit(solution)/shard_map/ppermute | solution.py:89
  384.9 56.9 %collective-permute-start.43 = (bf16[2,128,2048]{2,1,0:T(8,128)(2,1)}, bf16[2,128,2048]{2,1,0:T(8,128)(2,1)S(1)}, u32[]{:S(2)}, u32[]{:S(2)}) collective-permute-start(bf16[2,128,2048]{2,1,0:T(8,128)(2,1)} %get-tuple-element.380), channel_id=1, source_target_pairs={{0,2},{2,0},{4,6},{6,4},{8,10},{10,8},{12,14},{14,12},{16,18},{18,... | collective-permute-start | bytes 3145736 | tf_op jit(solution)/shard_map/ppermute | solution.py:89
  385.5 56.7 %collective-permute-start.44 = (bf16[2,128,2048]{2,1,0:T(8,128)(2,1)}, bf16[2,128,2048]{2,1,0:T(8,128)(2,1)}, u32[]{:S(2)}, u32[]{:S(2)}) collective-permute-start(bf16[2,128,2048]{2,1,0:T(8,128)(2,1)} %get-tuple-element.381), channel_id=1, source_target_pairs={{0,4},{2,6},{4,0},{6,2},{8,12},{10,14},{12,8},{14,10},{16,20},{18,... | collective-permute-start | bytes 3145736 | tf_op jit(solution)/shard_map/ppermute | solution.py:89
  386.1 56.1 %collective-permute-start.45 = (bf16[2,128,2048]{2,1,0:T(8,128)(2,1)}, bf16[2,128,2048]{2,1,0:T(8,128)(2,1)}, u32[]{:S(2)}, u32[]{:S(2)}) collective-permute-start(bf16[2,128,2048]{2,1,0:T(8,128)(2,1)} %get-tuple-element.382), channel_id=1, source_target_pairs={{0,6},{2,4},{4,2},{6,0},{8,14},{10,12},{12,10},{14,8},{16,22},{18,... | collective-permute-start | bytes 3145736 | tf_op jit(solution)/shard_map/ppermute | solution.py:89
  390.3 51.1 %collective-permute-start.46 = (bf16[128,2048]{1,0:T(8,128)(2,1)}, bf16[128,2048]{1,0:T(8,128)(2,1)S(1)}, u32[]{:S(2)}, u32[]{:S(2)}) collective-permute-start(bf16[128,2048]{1,0:T(8,128)(2,1)} %slice_bitcast_fusion.8), channel_id=1, source_target_pairs={{0,2},{2,0},{4,6},{6,4},{8,10},{10,8},{12,14},{14,12},{16,18},{18,... | collective-permute-start | bytes 1572872 | tf_op jit(solution)/shard_map/ppermute | solution.py:89
  391.7 50.0 %collective-permute-start.47 = (bf16[128,2048]{1,0:T(8,128)(2,1)}, bf16[128,2048]{1,0:T(8,128)(2,1)}, u32[]{:S(2)}, u32[]{:S(2)}) collective-permute-start(bf16[128,2048]{1,0:T(8,128)(2,1)} %slice_bitcast_fusion.7), channel_id=1, source_target_pairs={{0,4},{2,6},{4,0},{6,2},{8,12},{10,14},{12,8},{14,10},{16,20},{18,... | collective-permute-start | bytes 1572872 | tf_op jit(solution)/shard_map/ppermute | solution.py:89
  442.3 33.4 %collective-permute-start.48 = (bf16[2,128,2048]{2,1,0:T(8,128)(2,1)}, bf16[2,128,2048]{2,1,0:T(8,128)(2,1)S(1)}, u32[]{:S(2)}, u32[]{:S(2)}) collective-permute-start(bf16[2,128,2048]{2,1,0:T(8,128)(2,1)} %get-tuple-element.448), channel_id=1, source_target_pairs={{0,2},{2,0},{4,6},{6,4},{8,10},{10,8},{12,14},{14,12},{16,18},{18,... | collective-permute-start | bytes 3145736 | tf_op jit(solution)/shard_map/ppermute | solution.py:89
  443.4 33.3 %collective-permute-start.49 = (bf16[2,128,2048]{2,1,0:T(8,128)(2,1)}, bf16[2,128,2048]{2,1,0:T(8,128)(2,1)}, u32[]{:S(2)}, u32[]{:S(2)}) collective-permute-start(bf16[2,128,2048]{2,1,0:T(8,128)(2,1)} %get-tuple-element.449), channel_id=1, source_target_pairs={{0,4},{2,6},{4,0},{6,2},{8,12},{10,14},{12,8},{14,10},{16,20},{18,... | collective-permute-start | bytes 3145736 | tf_op jit(solution)/shard_map/ppermute | solution.py:89
  443.9 58.0 %collective-permute-start.50 = (bf16[2,128,2048]{2,1,0:T(8,128)(2,1)}, bf16[2,128,2048]{2,1,0:T(8,128)(2,1)}, u32[]{:S(2)}, u32[]{:S(2)}) collective-permute-start(bf16[2,128,2048]{2,1,0:T(8,128)(2,1)} %get-tuple-element.450), channel_id=1, source_target_pairs={{0,6},{2,4},{4,2},{6,0},{8,14},{10,12},{12,10},{14,8},{16,22},{18,... | collective-permute-start | bytes 3145736 | tf_op jit(solution)/shard_map/ppermute | solution.py:89
  501.9 42.7 %collective-permute-start.51 = (bf16[2,128,2048]{2,1,0:T(8,128)(2,1)}, bf16[2,128,2048]{2,1,0:T(8,128)(2,1)S(1)}, u32[]{:S(2)}, u32[]{:S(2)}) collective-permute-start(bf16[2,128,2048]{2,1,0:T(8,128)(2,1)} %get-tuple-element.481), channel_id=1, source_target_pairs={{0,2},{2,0},{4,6},{6,4},{8,10},{10,8},{12,14},{14,12},{16,18},{18,... | collective-permute-start | bytes 3145736 | tf_op jit(solution)/shard_map/ppermute | solution.py:89
  502.9 47.4 %collective-permute-start.52 = (bf16[2,128,2048]{2,1,0:T(8,128)(2,1)}, bf16[2,128,2048]{2,1,0:T(8,128)(2,1)S(1)}, u32[]{:S(2)}, u32[]{:S(2)}) collective-permute-start(bf16[2,128,2048]{2,1,0:T(8,128)(2,1)} %get-tuple-element.482), channel_id=1, source_target_pairs={{0,4},{2,6},{4,0},{6,2},{8,12},{10,14},{12,8},{14,10},{16,20},{18,... | collective-permute-start | bytes 3145736 | tf_op jit(solution)/shard_map/ppermute | solution.py:89
  505.8 62.5 %collective-permute-start.53 = (bf16[2,128,2048]{2,1,0:T(8,128)(2,1)}, bf16[2,128,2048]{2,1,0:T(8,128)(2,1)}, u32[]{:S(2)}, u32[]{:S(2)}) collective-permute-start(bf16[2,128,2048]{2,1,0:T(8,128)(2,1)} %get-tuple-element.483), channel_id=1, source_target_pairs={{0,6},{2,4},{4,2},{6,0},{8,14},{10,12},{12,10},{14,8},{16,22},{18,... | collective-permute-start | bytes 3145736 | tf_op jit(solution)/shard_map/ppermute | solution.py:89
  572.6 158.0 %collective-permute-start.61 = (bf16[128,2048]{1,0:T(8,128)(2,1)}, bf16[128,2048]{1,0:T(8,128)(2,1)}, u32[]{:S(2)}, u32[]{:S(2)}) collective-permute-start(bf16[128,2048]{1,0:T(8,128)(2,1)} %get-tuple-element.708), channel_id=1, source_target_pairs={{0,16},{2,18},{4,20},{6,22},{8,24},{10,26},{12,28},{14,30},{16,0},... | collective-permute-start | bytes 1572872 | tf_op jit(solution)/shard_map/ppermute | solution.py:89
  575.0 155.6 %collective-permute-start.62 = (bf16[128,2048]{1,0:T(8,128)(2,1)}, bf16[128,2048]{1,0:T(8,128)(2,1)}, u32[]{:S(2)}, u32[]{:S(2)}) collective-permute-start(bf16[128,2048]{1,0:T(8,128)(2,1)} %get-tuple-element.707), channel_id=1, source_target_pairs={{0,24},{2,26},{4,28},{6,30},{8,16},{10,18},{12,20},{14,22},{16,8},... | collective-permute-start | bytes 1572872 | tf_op jit(solution)/shard_map/ppermute | solution.py:89
  575.0 52.7 %collective-permute-start.54 = (bf16[2,128,2048]{2,1,0:T(8,128)(2,1)}, bf16[2,128,2048]{2,1,0:T(8,128)(2,1)}, u32[]{:S(2)}, u32[]{:S(2)}) collective-permute-start(bf16[2,128,2048]{2,1,0:T(8,128)(2,1)} %get-tuple-element.496), channel_id=1, source_target_pairs={{0,2},{2,0},{4,6},{6,4},{8,10},{10,8},{12,14},{14,12},{16,18},{18,... | collective-permute-start | bytes 3145736 | tf_op jit(solution)/shard_map/ppermute | solution.py:89
  575.9 51.8 %collective-permute-start.55 = (bf16[2,128,2048]{2,1,0:T(8,128)(2,1)}, bf16[2,128,2048]{2,1,0:T(8,128)(2,1)}, u32[]{:S(2)}, u32[]{:S(2)}) collective-permute-start(bf16[2,128,2048]{2,1,0:T(8,128)(2,1)} %get-tuple-element.497), channel_id=1, source_target_pairs={{0,4},{2,6},{4,0},{6,2},{8,12},{10,14},{12,8},{14,10},{16,20},{18,... | collective-permute-start | bytes 3145736 | tf_op jit(solution)/shard_map/ppermute | solution.py:89
  577.0 50.6 %collective-permute-start.56 = (bf16[2,128,2048]{2,1,0:T(8,128)(2,1)}, bf16[2,128,2048]{2,1,0:T(8,128)(2,1)}, u32[]{:S(2)}, u32[]{:S(2)}) collective-permute-start(bf16[2,128,2048]{2,1,0:T(8,128)(2,1)} %get-tuple-element.498), channel_id=1, source_target_pairs={{0,6},{2,4},{4,2},{6,0},{8,14},{10,12},{12,10},{14,8},{16,22},{18,... | collective-permute-start | bytes 3145736 | tf_op jit(solution)/shard_map/ppermute | solution.py:89
  578.5 49.2 %all-to-all-start.4 = ((f32[16,1,128]{2,1,0:T(1,128)}), f32[16,1,128]{2,1,0:T(1,128)S(1)}, u32[]{:S(2)}, u32[]{:S(2)}) async-start(f32[16,1,128]{2,1,0:T(1,128)} %get-tuple-element.507), calls=%async_computation.4 | async-start | bytes 16384 | tf_op jit(solution)/shard_map/all_to_all | solution.py:207
  630.5 36.2 %collective-permute-start.58 = (bf16[128,2048]{1,0:T(8,128)(2,1)S(1)}, bf16[128,2048]{1,0:T(8,128)(2,1)S(1)}, u32[]{:S(2)}, u32[]{:S(2)}) collective-permute-start(bf16[128,2048]{1,0:T(8,128)(2,1)S(1)} %get-tuple-element.710), channel_id=1, source_target_pairs={{0,16},{2,18},{4,20},{6,22},{8,24},{10,26},{12,28},{14,30},{16,0},... | collective-permute-start | bytes 1572872 | tf_op jit(solution)/shard_map/ppermute | solution.py:89
  633.4 44.4 %collective-permute-start.59 = (bf16[128,2048]{1,0:T(8,128)(2,1)S(1)}, bf16[128,2048]{1,0:T(8,128)(2,1)S(1)}, u32[]{:S(2)}, u32[]{:S(2)}) collective-permute-start(bf16[128,2048]{1,0:T(8,128)(2,1)S(1)} %get-tuple-element.709), channel_id=1, source_target_pairs={{0,24},{2,26},{4,28},{6,30},{8,16},{10,18},{12,20},{14,22},{16,8},... | collective-permute-start | bytes 1572872 | tf_op jit(solution)/shard_map/ppermute | solution.py:89
  635.7 42.9 %collective-permute-start.57 = (bf16[128,2048]{1,0:T(8,128)(2,1)S(1)}, bf16[128,2048]{1,0:T(8,128)(2,1)}, u32[]{:S(2)}, u32[]{:S(2)}) collective-permute-start(bf16[128,2048]{1,0:T(8,128)(2,1)S(1)} %fusion.28), channel_id=1, source_target_pairs={{0,8},{2,10},{4,12},{6,14},{8,0},{10,2},{12,4},{14,6},{16,24},{18,... | collective-permute-start | bytes 1572872 | tf_op jit(solution)/shard_map/ppermute | solution.py:89
  764.7 33.9 %collective-permute-start.65 = (bf16[1024,2048]{1,0:T(8,128)(2,1)}, bf16[1024,2048]{1,0:T(8,128)(2,1)}, u32[]{:S(2)}, u32[]{:S(2)}) collective-permute-start(bf16[1024,2048]{1,0:T(8,128)(2,1)} %convolution_convert_fusion), channel_id=1, source_target_pairs={{0,1},{1,0},{2,3},{3,2},{4,5},{5,4},{6,7},{7,6},{8,9},{9,8},{10,11... | collective-permute-start | bytes 12582920 | tf_op jit(solution)/shard_map/ppermute | solution.py:182
  774.9 66.3 %all-to-all-start.6 = ((bf16[16,128,576]{1,2,0:T(8,128)(2,1)}), bf16[16,128,576]{1,2,0:T(8,128)(2,1)S(1)}, u32[]{:S(2)}, u32[]{:S(2)}) async-start(bf16[16,128,576]{1,2,0:T(8,128)(2,1)} %copy.320), calls=%async_computation.6 | async-start | bytes 4718592 | tf_op jit(solution)/shard_map/all_to_all | solution.py:207
  779.4 177.9 %reduce-scatter.2.cloned.1.call-start = ((), (), s32[]{:S(2)}) async-start(), calls=%async_computation.15 | async-start | bytes 4456448 | tf_op jit(solution)/shard_map/reduce_scatter | solution.py:859
  841.6 92.4 %collective-permute-start.70 = (bf16[704,2048]{1,0:T(8,128)(2,1)}, bf16[704,2048]{1,0:T(8,128)(2,1)}, u32[]{:S(2)}, u32[]{:S(2)}) collective-permute-start(bf16[704,2048]{1,0:T(8,128)(2,1)} %convolution_convert_fusion.3), channel_id=1, source_target_pairs={{0,1},{1,0},{2,3},{3,2},{4,5},{5,4},{6,7},{7,6},{8,9},{9,8},{10,11... | collective-permute-start | bytes 8650760 | tf_op jit(solution)/shard_map/ppermute | solution.py:182
  841.6 99.8 %collective-permute-start.69 = (bf16[704,2048]{1,0:T(8,128)(2,1)}, bf16[704,2048]{1,0:T(8,128)(2,1)}, u32[]{:S(2)}, u32[]{:S(2)}) collective-permute-start(bf16[704,2048]{1,0:T(8,128)(2,1)} %convolution_convert_fusion.1), channel_id=1, source_target_pairs={{0,1},{1,0},{2,3},{3,2},{4,5},{5,4},{6,7},{7,6},{8,9},{9,8},{10,11... | collective-permute-start | bytes 8650760 | tf_op jit(solution)/shard_map/ppermute | solution.py:182
  842.1 104.6 %collective-permute-start.68 = (bf16[704,2048]{1,0:T(8,128)(2,1)}, bf16[704,2048]{1,0:T(8,128)(2,1)}, u32[]{:S(2)}, u32[]{:S(2)}) collective-permute-start(bf16[704,2048]{1,0:T(8,128)(2,1)} %convolution_convert_fusion.2), channel_id=1, source_target_pairs={{0,1},{1,0},{2,3},{3,2},{4,5},{5,4},{6,7},{7,6},{8,9},{9,8},{10,11... | collective-permute-start | bytes 8650760 | tf_op jit(solution)/shard_map/ppermute | solution.py:182
  843.5 49.7 %collective-permute-start.67 = (bf16[88,2048]{1,0:T(8,128)(2,1)}, bf16[88,2048]{1,0:T(8,128)(2,1)}, u32[]{:S(2)}, u32[]{:S(2)}) collective-permute-start(bf16[88,2048]{1,0:T(8,128)(2,1)} %select_convert_fusion.2), channel_id=1, source_target_pairs={{0,1},{1,0},{2,3},{3,2},{4,5},{5,4},{6,7},{7,6},{8,9},{9,8},{10,11... | collective-permute-start | bytes 1081352 | tf_op jit(solution)/shard_map/ppermute | solution.py:182
  882.5 34.3 %all-to-all-start.10 = ((bf16[16,64,352]{2,1,0:T(8,128)(2,1)}), bf16[16,64,352]{2,1,0:T(8,128)(2,1)S(1)}, u32[]{:S(2)}, u32[]{:S(2)}) async-start(bf16[16,64,352]{2,1,0:T(8,128)(2,1)} %fusion.6), calls=%async_computation.11 | async-start | bytes 1572864 | tf_op jit(solution)/shard_map/all_to_all | solution.py:207
  917.7 36.7 %all-to-all-start.9 = ((bf16[16,64,640]{2,1,0:T(8,128)(2,1)}), bf16[16,64,640]{2,1,0:T(8,128)(2,1)S(1)}, u32[]{:S(2)}, u32[]{:S(2)}) async-start(bf16[16,64,640]{2,1,0:T(8,128)(2,1)} %fusion.2), calls=%async_computation.9 | async-start | bytes 2621440 | tf_op jit(solution)/shard_map/all_to_all | solution.py:207
  (134 other events, 2134.7 us)
Sparse Core Ops, SparseCore 0:
  13.0 79.8 all-gather.3
  95.7 116.9 all-gather.5
  442.4 150.9 all-gather.7
  804.3 116.5 reduce-scatter.1

commit v2 on v1

--- a/solution.py
+++ b/solution.py
@@ -82,7 +82,7 @@
 
 
 def exchanges():
-    return lax.axis_size("ctx") == 16
+    return lax.axis_size("ctx") == 16 and lax.axis_size("fsdp") == 2
 
 
 def hop(value, mask):
@@ -93,7 +93,7 @@
     return lax.optimization_barrier(values)
 
 
-def gather_ctx(block, *stages):
+def gather_ctx(block, *stages, early=False):
     held = None
     if not exchanges():
         whole = lax.all_gather(block, "ctx", axis=0)
@@ -115,13 +115,21 @@
     alone = lambda values: [(value[None], 0) for value in values]
     both = lambda values: [(values, 0), (values, 1)]
     near, far, one, two = end(0, *(hop(block, mask) for mask in (4, 8, 1, 2)))
-    far_near, three, *near_others = end(
-        1, hop(far, 4), hop(two, 1), *(hop(near, mask) for mask in (1, 2, 3))
-    )
-    pairs = zip((block, one, two, three), (near, *near_others))
-    pieces = [[alone(values) for values in pairs]]
+    if early:
+        far_near, three, *near_others = end(
+            1, hop(far, 4), hop(two, 1), *(hop(near, mask) for mask in (1, 2, 3))
+        )
+        pieces = [[alone(v) for v in zip((block, one, two, three), (near, *near_others))]]
+    else:
+        far_near, three, *near_others = end(
+            1, hop(far, 4), hop(two, 1), *(hop(near, mask) for mask in (1, 2))
+        )
     pair = jnp.stack([far, far_near])
-    far_one, far_two = end(2, hop(pair, 1), hop(pair, 2))
+    relayed = () if early else (hop(three, 4),)
+    far_one, far_two, *relayed = end(2, hop(pair, 1), hop(pair, 2), *relayed)
+    if not early:
+        near_others = [*near_others, *relayed]
+        pieces = [[alone(v) for v in zip((block, one, two, three), (near, *near_others))]]
     far_three = end(3, hop(far_two[0], 1), hop(far_one[1], 2))
     return [*pieces, [both(pair), both(far_one), both(far_two), alone(far_three)]], held
 
@@ -690,10 +698,6 @@
     small_full = lax.all_gather(small, everywhere, axis=0, tiled=True)
     reduce_full = small_full[:, :compressed_width]
     router_full = small_full[:, turned_width : small_width - 3]
-    attn_gain = small_full[:, small_width - 3].astype(f32)
-    ffn_gain = small_full[:, small_width - 2].astype(f32)
-    kv_gain = small_full[:, small_width - 1].reshape(ctx * fsdp, rows)[:, :kv_rows]
-    kv_gain = kv_gain.reshape(KVR).astype(f32)
 
     tokens_low = hidden_in.reshape(part, width)
     upstream_low = cotangent.reshape(part, width)
@@ -711,9 +715,12 @@
     expand_end = WIDE + columns[2].shape[-1]
 
     def joined_stage(received, _):
-        return received, join_rows(gather_fsdp(received[..., :expand_end]))
-
-    tokens_all, (received, by_rows) = gather_ctx(
+        gains = small_full[:, small_width - 3 :].astype(f32)
+        kv_gain = gains[:, 2].reshape(ctx * fsdp, rows)[:, :kv_rows].reshape(KVR)
+        by_rows = join_rows(gather_fsdp(received[..., :expand_end]))
+        return received, by_rows, gains[:, 0], gains[:, 1], kv_gain
+
+    tokens_all, (received, by_rows, attn_gain, ffn_gain, kv_gain) = gather_ctx(
         tokens_low, *[lambda *_: None] * 2, lambda *_: to_owner(column_blocks), joined_stage
     )
     named_all = received[..., expand_end:].reshape(ctx, part)
@@ -765,17 +772,19 @@
 
     def second_stage(projected, _):
         _, query_all, key_head, value_head, _ = projected
-        outcome = attend(query_pos, query_rows(query_all), key_head, value_head)
-        return projected, outcome, to_owner(shared_blocks)
+        return projected, attend(query_pos, query_rows(query_all), key_head, value_head)
 
     def third_stage(held, _):
-        projected, (outcome, outcome_low, lse), shared_in = held
-        shared_in = join_rows(gather_fsdp(shared_in))
-        return projected, outcome, lse, from_heads(outcome_low), shared_in
+        projected, (outcome, outcome_low, lse) = held
+        return projected, outcome, lse, from_heads(outcome_low)
+
+    def fourth_stage(held, _):
+        return *held, to_owner(shared_blocks)
 
     upstream_all, (projected, outcome, lse, attended, shared_in) = gather_ctx(
-        upstream_late, first_stage, second_stage, third_stage
-    )
+        upstream_late, first_stage, second_stage, third_stage, fourth_stage
+    )
+    shared_in = join_rows(gather_fsdp(shared_in))
     shared_in = (shared_in[:, :hidden_shared], shared_in[:, hidden_shared:])
     normed_all, query_all, key_head, value_head, latent_all = projected
     query_head = query_rows(query_all)
@@ -805,7 +814,8 @@
         return gates_all, out, done, db, back, arrived
 
     ffn_all, (gates_all, out, done, db, back, out_arrived) = gather_ctx(
-        ffn_low, lambda *_: None, lambda *_: to_owner(gates_own.T), near_forward, near_backward
+        ffn_low, lambda *_: None, lambda *_: to_owner(gates_own.T), near_forward, near_backward,
+        early=True,
     )
     forward, backward = work(gates_all)
     out_parts, grad_parts, grad_arrived = [out], [db], []
@@ -867,25 +877,22 @@
     else:
         out_sum = whole_sum(out_parts)
     grad_query, grad_expanded, latent_part = attention_grads
-    latent_part, query_own, sums, shared_sums = together(
-        to_owner(latent_part.reshape(ctx, part, -1)), from_heads(grad_query), sums, shared_sums
-    )
+    sums = [scatter_fsdp(v) for v in sums]
+    latent_part, grad_query, grad_expanded, shared_sums, sums = together(
+        to_owner(latent_part.reshape(ctx, part, -1)), grad_query, grad_expanded, shared_sums, sums
+    )
+    query_own = from_heads(grad_query)
     latent_sum = jnp.sum(latent_part.astype(f32), axis=0)
-    grad_normed = mm_nt(query_own.reshape(part, HEADS * QK), query_full)
-    grad_expert_down, grad_expert_gate, grad_expert_up = (scatter_fsdp(v).T[None] for v in sums)
+    grad_expert_down, grad_expert_gate, grad_expert_up = (v.T[None] for v in sums)
     down_rows = shared_down.shape[0]
     grad_back = shared_sums[0].reshape(fsdp, down_rows, width)
     grad_shared_down = scatter_fsdp(in_fsdp_order([grad_back[i] for i in range(fsdp)]))
-    grad_in = to_rows(jnp.concatenate(shared_sums[1:], axis=-1), rows).transpose(1, 0, 2)
-    grad_shared_gate = grad_in[..., :hidden_shared].reshape(rows, ctx * hidden_shared)
-    grad_shared_up = grad_in[..., hidden_shared:].reshape(rows, ctx * hidden_shared)
+    grad_in = to_rows(jnp.concatenate(shared_sums[1:], axis=-1), rows)
 
     grad_query_w = mm_tn(query_rows(normed_all), grad_query).reshape(ctx, fsdp, rows, QK)
     grad_expand = mm_tn(latent_all, grad_expanded).reshape(ctx, fsdp, rows, -1)
     by_heads = jnp.concatenate([grad_query_w, grad_expand], axis=-1)
     by_heads = to_rows(by_heads.reshape(width, by_heads.shape[-1]), rows)
-    grad_query_w = from_head_blocks(by_heads[..., :QK])
-    grad_expand = from_head_blocks(by_heads[..., QK:].reshape(ctx, kv_rows, NOPE + VHEAD))
 
     own_rows = ctx_rank * part
     own_normed = lax.dynamic_slice_in_dim(normed_all, own_rows, part, 0)
@@ -908,7 +915,17 @@
         axis=1,
     ).reshape(ctx, fsdp, rows, -1)
     grad_small = scatter_fsdp(in_fsdp_order([grad_small[:, i] for i in range(fsdp)]))
-    grad_small = jnp.sum(to_owner(grad_small.astype(bf16)).astype(f32), axis=0)
+    grad_small, by_heads, query_own, grad_in = together(
+        grad_small.astype(bf16), by_heads, query_own, grad_in
+    )
+    grad_normed = mm_nt(query_own.reshape(part, HEADS * QK), query_full)
+    grad_small, grad_normed = together(to_owner(grad_small), grad_normed)
+    grad_small = jnp.sum(grad_small.astype(f32), axis=0)
+    grad_in = grad_in.transpose(1, 0, 2)
+    grad_shared_gate = grad_in[..., :hidden_shared].reshape(rows, ctx * hidden_shared)
+    grad_shared_up = grad_in[..., hidden_shared:].reshape(rows, ctx * hidden_shared)
+    grad_query_w = from_head_blocks(by_heads[..., :QK])
+    grad_expand = from_head_blocks(by_heads[..., QK:].reshape(ctx, kv_rows, NOPE + VHEAD))
     grad_reduce = grad_small[:, :compressed_width]
     grad_normed = grad_normed + mm_nt(grad_compressed, reduce_full)
     attn_grad_in, _ = rms_backward(tokens, rms_factor(tokens), attn_gain, grad_normed)

time: 976 us -> 942 us (0.965)
  waiting for transfers between devices: 369 us -> 315 us
    ppermute x57, waiting for transfers between devices: 270 us -> 216 us  [hop(): return lax.ppermute(value, 'ctx', [(i, i ^ mask) for i in range(16)])]
    add x1 -> x4, other arithmetic: 2.01 us -> 21.7 us  [scatter_fsdp(): return parts[0].astype(f32) + swap_cores(parts[1].astype(bf16)).astype(f32)]
    broadcast_in_dim x3 -> x0, other arithmetic: 18.5 us -> none  [shards(): scatter_fsdp(v).T[None]]
  transfers between devices with their start and end apart: 86 -> 86, of which waited for: 36 -> 37; matrix products, arithmetic and copies ran while one was open for 25% -> 27% of each run, Pallas kernels for 19% -> 20%
where the time goes in v2:
time: 942 us; the launch traced here: 932 us
  waiting for transfers between devices  315 us (33%)
  Pallas kernels  184 us (20%)
  starting transfers between devices  143 us (15%)
  local copies, waits for them, and re-layouts  93.4 us (10%)
  other arithmetic  92.7 us (10%)
  matrix products  88.7 us (9%)
  between operations  15.4 us (2%)
    ppermute x57, waiting for transfers between devices, hop(): return lax.ppermute(value, 'ctx', [(i, i ^ mask) for i in range(16)])  216 us
    pallas_call x4, Pallas kernels, expert_call(): pl.pallas_call(kernel, grid_spec=pltpu.PrefetchScalarGridSpec(num_scalar_...  131 us
    all_to_all x11, waiting for transfers between devices, to_owner(): lax.all_to_all(blocks, 'ctx', split_axis=0, concat_axis=0, tiled=True)  99 us
    ppermute x57, starting transfers between devices, hop(): return lax.ppermute(value, 'ctx', [(i, i ^ mask) for i in range(16)])  74.8 us
    all_to_all x11, starting transfers between devices, to_owner(): lax.all_to_all(blocks, 'ctx', split_axis=0, concat_axis=0, tiled=True)  66.4 us
    dot_general x15, matrix products, mm_tn(): lax.dot_general(left, right, (((0,), (0,)), ((), ())), preferred_element_...  57.2 us
    pallas_call x2, Pallas kernels, project(): pl.pallas_call(project_kernel, grid_spec=pltpu.PrefetchScalarGridSpec(num...  24.2 us
    dot_general x4, matrix products, mm_nt(): lax.dot_general(left, right, (((1,), (1,)), ((), ())), preferred_element_...  22.3 us
  transfers between devices with their start and end apart: 86, of which 37 were waited for; matrix products, arithmetic and copies ran while one was open for 27% of the time, Pallas kernels for 20%

profile of v2, /device:TPU:8, one launch (start us, length us, event | category | flops | bytes accessed | tf_op | source)
XLA Modules:
  0.0 932.5 jit_solution(17495286534692431511)
XLA Ops:
  20.4 18.1 %collective-permute-done = bf16[128,2048]{1,0:T(8,128)(2,1)} collective-permute-done((bf16[128,2048]{1,0:T(8,128)(2,1)}, bf16[128,2048]{1,0:T(8,128)(2,1)}, u32[]{:S(2)}, u32[]{:S(2)}) %collective-permute-start) | collective-permute-done | bytes 524320 | tf_op jit(solution)/shard_map/ppermute | solution.py:89
  53.1 5.5 all-to-all-start
  64.1 14.4 %collective-permute-done.5 = bf16[128,2048]{1,0:T(8,128)(2,1)} collective-permute-done((bf16[128,2048]{1,0:T(8,128)(2,1)}, bf16[128,2048]{1,0:T(8,128)(2,1)}, u32[]{:S(2)}, u32[]{:S(2)}) %collective-permute-start.5) | collective-permute-done | bytes 524320 | tf_op jit(solution)/shard_map/ppermute | solution.py:89
  95.9 9.6 %collective-permute-done.8.refs_2_.refs_3_ = bf16[2,128,2048]{2,1,0:T(8,128)(2,1)S(1)} collective-permute-done((bf16[2,128,2048]{2,1,0:T(8,128)(2,1)S(1)}, bf16[2,128,2048]{2,1,0:T(8,128)(2,1)S(1)}, u32[]{:S(2)}, u32[]{:S(2)}) %collective-permute-start.8) | collective-permute-done | bytes 1048608 | tf_op jit(solution)/shard_map/ppermute | solution.py:89
  132.3 12.1 %project.2 = (bf16[2048,2048]{1,0:T(8,128)(2,1)}, bf16[2048,256]{1,0:T(8,128)(2,1)}, bf16[2048,256]{1,0:T(8,128)(2,1)}, bf16[2048,128]{1,0:T(8,128)(2,1)}, bf16[2048,512]{1,0:T(8,128)(2,1)}) custom-call(s32[3]{0:T(128)} %get-tuple-element.745.base_ref, bf16[1,128,2048]{2,1,0:T(8,128)(2,1)} %refs_0_.1, bf16[1,128,2048]{2,1,0:T(8,128)(2,1)} %bitcast.27.refs_1_, ...), custom_call_target="tpu_custom_call" | custom-call | flops 3758096384 | bytes 12058624 | tf_op jit(solution)/shard_map/project/pallas_call | solution.py:270
  144.4 12.1 %project.3 = (bf16[2048,2048]{1,0:T(8,128)(2,1)}, bf16[2048,256]{1,0:T(8,128)(2,1)}, bf16[2048,256]{1,0:T(8,128)(2,1)}, bf16[2048,128]{1,0:T(8,128)(2,1)}, bf16[2048,512]{1,0:T(8,128)(2,1)}) custom-call(s32[3]{0:T(128)} %get-tuple-element.744.base_ref, ...), custom_call_target="tpu_custom_call", output_to_operand_aliasing={{0}: (15, {}), {1}: (16, {}), {2}: (17, {}), {3}: (18, {}),... | custom-call | flops 3758096384 | bytes 12058624 | tf_op jit(solution)/shard_map/project/pallas_call | solution.py:270
  165.4 11.6 %attend.1 = (f32[2048,128]{1,0:T(8,128)S(1)}, bf16[2048,128]{1,0:T(8,128)(2,1)S(1)}, f32[2048,1]{1,0:T(8,128)S(1)}) custom-call(s32[2048,1]{1,0:T(8,128)S(1)} %iota.38.pos_ref, bf16[2048,256]{1,0:T(8,128)(2,1)S(1)} %copy-done.2, bf16[2048,256]{1,0:T(8,128)(2,1)} %get-tuple-element.494.key_ref, bf16[2048,128]{1,0:T(8,128)(2,1)S(1)} %copy-done.3), custom_call_target="tpu_custom_call" | custom-call | flops 2684354560 | bytes 5242880 | tf_op jit(solution)/shard_map/attend/pallas_call | solution.py:394
  179.0 5.3 collective-permute-done.18
  185.7 10.9 %collective-permute-done.20 = bf16[128,2048]{1,0:T(8,128)(2,1)S(1)} collective-permute-done((bf16[128,2048]{1,0:T(8,128)(2,1)S(1)}, bf16[128,2048]{1,0:T(8,128)(2,1)S(1)}, u32[]{:S(2)}, u32[]{:S(2)}) %collective-permute-start.20) | collective-permute-done | bytes 524320 | tf_op jit(solution)/shard_map/ppermute | solution.py:89
  200.4 6.1 all-to-all-start.1
  210.2 18.0 %all-to-all-done.1 = bf16[16,128,128]{1,2,0:T(8,128)(2,1)S(1)} async-done(((bf16[16,128,128]{1,2,0:T(8,128)(2,1)}), bf16[16,128,128]{1,2,0:T(8,128)(2,1)S(1)}, u32[]{:S(2)}, u32[]{:S(2)}) %all-to-all-start.1) | async-done | bytes 524320 | tf_op jit(solution)/shard_map/all_to_all | solution.py:215
  228.2 6.5 all-to-all-start.2
  239.9 13.1 %all-to-all-done.2 = bf16[16,64,352]{2,1,0:T(8,128)(2,1)} async-done(((bf16[16,64,352]{2,1,0:T(8,128)(2,1)}), bf16[16,64,352]{2,1,0:T(8,128)(2,1)}, u32[]{:S(2)}, u32[]{:S(2)}) %all-to-all-start.2) | async-done | bytes 720928 | tf_op jit(solution)/shard_map/all_to_all | solution.py:215
  270.0 12.1 %collective-permute-done.27 = bf16[128,2048]{1,0:T(8,128)(2,1)} collective-permute-done((bf16[128,2048]{1,0:T(8,128)(2,1)S(1)}, bf16[128,2048]{1,0:T(8,128)(2,1)}, u32[]{:S(2)}, u32[]{:S(2)}) %collective-permute-start.27) | collective-permute-done | bytes 524320 | tf_op jit(solution)/shard_map/ppermute | solution.py:89
  295.5 6.9 collective-permute-done.31
  304.3 5.2 all-to-all-start.3
  311.1 8.2 collective-permute-done.33
  322.5 11.1 %collective-permute-done.34 = bf16[128,2048]{1,0:T(8,128)(2,1)} collective-permute-done((bf16[128,2048]{1,0:T(8,128)(2,1)}, bf16[128,2048]{1,0:T(8,128)(2,1)}, u32[]{:S(2)}, u32[]{:S(2)}) %collective-permute-start.34) | collective-permute-done | bytes 524320 | tf_op jit(solution)/shard_map/ppermute | solution.py:89
  338.8 29.7 %experts_forward.2 = (bf16[2,128,2048]{2,1,0:T(8,128)(2,1)}, bf16[2,128,2048]{2,1,0:T(8,128)(2,1)}, bf16[2,128,2048]{2,1,0:T(8,128)(2,1)}, bf16[2,128,2048]{2,1,...) custom-call(s32[3]{0:T(128)} %get-tuple-element.745.base_ref, ...), custom_call_target="tpu_custom_call" | custom-call | flops 11072962560 | bytes 41943040 | tf_op jit(solution)/shard_map/experts_forward/pallas_call | solution.py:586
  377.0 34.5 %experts_backward.2 = (bf16[2,128,2048]{2,1,0:T(8,128)(2,1)}, bf16[2,128,2048]{2,1,0:T(8,128)(2,1)}, bf16[2,128,2048]{2,1,0:T(8,128)(2,1)}, bf16[2,128,2048]{2,1...) custom-call(s32[3]{0:T(128)} %get-tuple-element.745.base_ref, ...), custom_call_target="tpu_custom_call" | custom-call | flops 11072962560 | bytes 41943040 | tf_op jit(solution)/shard_map/experts_backward/pallas_call | solution.py:586
  411.5 12.6 %collective-permute-done.46 = bf16[128,2048]{1,0:T(8,128)(2,1)S(1)} collective-permute-done((bf16[128,2048]{1,0:T(8,128)(2,1)}, bf16[128,2048]{1,0:T(8,128)(2,1)S(1)}, u32[]{:S(2)}, u32[]{:S(2)}) %collective-permute-start.46) | collective-permute-done | bytes 524320 | tf_op jit(solution)/shard_map/ppermute | solution.py:89
  428.8 29.9 %experts_forward.3 = (bf16[2,128,2048]{2,1,0:T(8,128)(2,1)}, bf16[2,128,2048]{2,1,0:T(8,128)(2,1)}, bf16[2,128,2048]{2,1,0:T(8,128)(2,1)}, bf16[2,128,2048]{2,1,...) custom-call(s32[3]{0:T(128)} %get-tuple-element.744.base_ref, ...), custom_call_target="tpu_custom_call", output_to_operand_aliasing={{4}: (20, {}), {5}: (21, {}), {6}: (22, {}), {7}: (23, {}),... | custom-call | flops 11072962560 | bytes 41943040 | tf_op jit(solution)/shard_map/experts_forward/pallas_call | solution.py:586
  461.3 26.6 %collective-permute-done.50 = bf16[2,128,2048]{2,1,0:T(8,128)(2,1)} collective-permute-done((bf16[2,128,2048]{2,1,0:T(8,128)(2,1)}, bf16[2,128,2048]{2,1,0:T(8,128)(2,1)}, u32[]{:S(2)}, u32[]{:S(2)}) %collective-permute-start.50) | collective-permute-done | bytes 1048608 | tf_op jit(solution)/shard_map/ppermute | solution.py:89
  492.2 36.6 %experts_backward.3 = (bf16[2,128,2048]{2,1,0:T(8,128)(2,1)}, bf16[2,128,2048]{2,1,0:T(8,128)(2,1)}, bf16[2,128,2048]{2,1,0:T(8,128)(2,1)}, bf16[2,128,2048]{2,1...) custom-call(s32[3]{0:T(128)} %get-tuple-element.744.base_ref, ...), custom_call_target="tpu_custom_call", output_to_operand_aliasing={{4}: (27, {}), {5}: (28, {}), {6}: (29, {}), {7}: (30, {}),... | custom-call | flops 11072962560 | bytes 41943040 | tf_op jit(solution)/shard_map/experts_backward/pallas_call | solution.py:586
  531.9 25.4 %collective-permute-done.53 = bf16[2,128,2048]{2,1,0:T(8,128)(2,1)} collective-permute-done((bf16[2,128,2048]{2,1,0:T(8,128)(2,1)}, bf16[2,128,2048]{2,1,0:T(8,128)(2,1)}, u32[]{:S(2)}, u32[]{:S(2)}) %collective-permute-start.53) | collective-permute-done | bytes 1048608 | tf_op jit(solution)/shard_map/ppermute | solution.py:89
  560.8 6.9 all-to-all-start.4
  591.1 5.0 fusion.64
  600.8 5.3 fusion.63
  623.8 17.0 %collective-permute-done.58 = bf16[128,2048]{1,0:T(8,128)(2,1)S(1)} collective-permute-done((bf16[128,2048]{1,0:T(8,128)(2,1)S(1)}, bf16[128,2048]{1,0:T(8,128)(2,1)S(1)}, u32[]{:S(2)}, u32[]{:S(2)}) %collective-permute-start.58) | collective-permute-done | bytes 524320 | tf_op jit(solution)/shard_map/ppermute | solution.py:89
  640.9 7.3 collective-permute-done.59
  651.6 6.6 fusion.9
  659.3 7.3 all-to-all-start.5
  680.0 17.5 %attend_grad.1 = (bf16[2048,192]{1,0:T(8,128)(2,1)S(1)}, bf16[2048,256]{1,0:T(8,128)(2,1)S(1)}, bf16[2048,576]{1,0:T(8,128)(2,1)}) custom-call(s32[2048,1]{1,0:T(8,128)S(1)} %iota.39.pos_ref, f32[2048,128]{1,0:T(8,128)S(1)} %copy-done, bf16[2048,256]{1,0:T(8,128)(2,1)} %get-tuple-element.493.query_ref, bf16[2048,256]{1,0:T(8,128)(2,1)} %get-tuple-element.494.key_ref, ...), custom_call_target="tpu_custom_call" | custom-call | flops 6979321856 | bytes 10485760 | tf_op jit(solution)/shard_map/attend_grad/pallas_call | solution.py:419
  701.8 5.2 all-to-all-start.6
  708.5 7.5 convert_add_fusion
  716.0 7.5 convert_add_fusion.1
  723.5 5.8 convert_add_fusion.2
  731.1 5.4 add_convert_fusion
  736.5 31.3 %all-to-all-done.6 = bf16[16,128,576]{1,2,0:T(8,128)(2,1)} async-done(((bf16[16,128,576]{1,2,0:T(8,128)(2,1)}), bf16[16,128,576]{1,2,0:T(8,128)(2,1)}, u32[]{:S(2)}, u32[]{:S(2)}) %all-to-all-start.6) | async-done | bytes 2359328 | tf_op jit(solution)/shard_map/all_to_all | solution.py:215
  781.1 6.0 fusion.68
  799.1 7.5 all-to-all-start.7
  811.0 15.6 %all-to-all-done.7 = bf16[16,64,256]{2,1,0:T(8,128)(2,1)S(1)} async-done(((bf16[16,64,256]{2,1,0:T(8,128)(2,1)}), bf16[16,64,256]{2,1,0:T(8,128)(2,1)S(1)}, u32[]{:S(2)}, u32[]{:S(2)}) %all-to-all-start.7) | async-done | bytes 524320 | tf_op jit(solution)/shard_map/all_to_all | solution.py:215
  826.6 5.0 all-to-all-start.9
  846.9 8.0 all-to-all-done.9
  854.9 6.1 all-to-all-start.8
  870.9 8.8 all-to-all-done.8
  879.7 5.0 all-to-all-start.10
  903.7 10.2 %fusion.70 = f32[128,2048]{1,0:T(8,128)} fusion(bf16[128,3072]{0,1:T(8,128)(2,1)} %bitcast.125, bf16[2048,3072]{1,0:T(8,128)(2,1)} %all-gather.8.cloned.1.call-done), kind=kOutput, calls=%fused_computation.187 | convolution fusion | flops 1610612736 | bytes 14417920 | tf_op jit(solution)/shard_map/dot_general | solution.py:33
  (506 shorter events, 327.3 us)
Async XLA Ops:
  7.2 107.7 %all-gather.4.cloned.1.call-start = ((), (), s32[]{:S(2)}) async-start(), calls=%async_computation.12 | async-start | bytes 3244032 | tf_op jit(solution)/shard_map/all_gather | solution.py:698
  12.9 243.1 %all-gather.6.cloned.1.call-start = ((), (), s32[]{:S(2)}) async-start(), calls=%async_computation.13 | async-start | bytes 8650752 | tf_op jit(solution)/shard_map/all_gather | solution.py:729
  13.7 28.2 %collective-permute-start.1 = (bf16[128,2048]{1,0:T(8,128)(2,1)}, bf16[128,2048]{1,0:T(8,128)(2,1)S(1)}, u32[]{:S(2)}, u32[]{:S(2)}) collective-permute-start(bf16[128,2048]{1,0:T(8,128)(2,1)} %bitcast.310), channel_id=1, source_target_pairs={{0,16},{2,18},{4,20},{6,22},{8,24},{10,26},{12,28},{14,30},{16,0},... | collective-permute-start | bytes 1572872 | tf_op jit(solution)/shard_map/ppermute | solution.py:89
  46.5 32.0 %collective-permute-start.5 = (bf16[128,2048]{1,0:T(8,128)(2,1)}, bf16[128,2048]{1,0:T(8,128)(2,1)}, u32[]{:S(2)}, u32[]{:S(2)}) collective-permute-start(bf16[128,2048]{1,0:T(8,128)(2,1)} %collective-permute-done.3), channel_id=1, source_target_pairs={{0,2},{2,0},{4,6},{6,4},{8,10},{10,8},{12,14},{14,12},{16,18},{18,... | collective-permute-start | bytes 1572872 | tf_op jit(solution)/shard_map/ppermute | solution.py:89
  53.1 41.8 %all-to-all-start = ((bf16[16,64,322]{2,1,0:T(8,128)(2,1)}), bf16[16,64,322]{2,1,0:T(8,128)(2,1)}, u32[]{:S(2)}, u32[]{:S(2)}) async-start(bf16[16,64,322]{2,1,0:T(8,128)(2,1)} %concatenate.39), calls=%async_computation | async-start | bytes 1572864 | tf_op jit(solution)/shard_map/all_to_all | solution.py:215
  127.2 29.5 %collective-permute-start.14 = (bf16[128,2048]{1,0:T(8,128)(2,1)S(1)}, bf16[128,2048]{1,0:T(8,128)(2,1)S(1)}, u32[]{:S(2)}, u32[]{:S(2)}) collective-permute-start(bf16[128,2048]{1,0:T(8,128)(2,1)S(1)} %bitcast.329), channel_id=1, source_target_pairs={{0,8},{2,10},{4,12},{6,14},{8,0},{10,2},{12,4},{14,6},{16,24},{18,... | collective-permute-start | bytes 1572872 | tf_op jit(solution)/shard_map/ppermute | solution.py:89
  127.3 32.1 %collective-permute-start.15 = (bf16[128,2048]{1,0:T(8,128)(2,1)S(1)}, bf16[128,2048]{1,0:T(8,128)(2,1)S(1)}, u32[]{:S(2)}, u32[]{:S(2)}) collective-permute-start(bf16[128,2048]{1,0:T(8,128)(2,1)S(1)} %bitcast.330), channel_id=1, source_target_pairs={{0,16},{2,18},{4,20},{6,22},{8,24},{10,26},{12,28},{14,30},{16,0},... | collective-permute-start | bytes 1572872 | tf_op jit(solution)/shard_map/ppermute | solution.py:89
  129.2 30.2 %collective-permute-start.16 = (bf16[128,2048]{1,0:T(8,128)(2,1)S(1)}, bf16[128,2048]{1,0:T(8,128)(2,1)S(1)}, u32[]{:S(2)}, u32[]{:S(2)}) collective-permute-start(bf16[128,2048]{1,0:T(8,128)(2,1)S(1)} %bitcast.331), channel_id=1, source_target_pairs={{0,2},{2,0},{4,6},{6,4},{8,10},{10,8},{12,14},{14,12},{16,18},{18,... | collective-permute-start | bytes 1572872 | tf_op jit(solution)/shard_map/ppermute | solution.py:89
  129.8 29.7 %collective-permute-start.17 = (bf16[128,2048]{1,0:T(8,128)(2,1)S(1)}, bf16[128,2048]{1,0:T(8,128)(2,1)}, u32[]{:S(2)}, u32[]{:S(2)}) collective-permute-start(bf16[128,2048]{1,0:T(8,128)(2,1)S(1)} %bitcast.332), channel_id=1, source_target_pairs={{0,4},{2,6},{4,0},{6,2},{8,12},{10,14},{12,8},{14,10},{16,20},{18,... | collective-permute-start | bytes 1572872 | tf_op jit(solution)/shard_map/ppermute | solution.py:89
  161.1 35.5 %collective-permute-start.20 = (bf16[128,2048]{1,0:T(8,128)(2,1)S(1)}, bf16[128,2048]{1,0:T(8,128)(2,1)S(1)}, u32[]{:S(2)}, u32[]{:S(2)}) collective-permute-start(bf16[128,2048]{1,0:T(8,128)(2,1)S(1)} %collective-permute-done.14), channel_id=1, source_target_pairs={{0,2},{2,0},{4,6},{6,4},{8,10},{10,8},{12,14},{14,12},{16,18},{18,... | collective-permute-start | bytes 1572872 | tf_op jit(solution)/shard_map/ppermute | solution.py:89
  161.6 35.0 %collective-permute-start.21 = (bf16[128,2048]{1,0:T(8,128)(2,1)S(1)}, bf16[128,2048]{1,0:T(8,128)(2,1)S(1)}, u32[]{:S(2)}, u32[]{:S(2)}) collective-permute-start(bf16[128,2048]{1,0:T(8,128)(2,1)S(1)} %collective-permute-done.14), channel_id=1, source_target_pairs={{0,4},{2,6},{4,0},{6,2},{8,12},{10,14},{12,8},{14,10},{16,20},{18,... | collective-permute-start | bytes 1572872 | tf_op jit(solution)/shard_map/ppermute | solution.py:89
  197.4 37.3 %collective-permute-start.22 = (bf16[2,128,2048]{2,1,0:T(8,128)(2,1)S(1)}, bf16[2,128,2048]{2,1,0:T(8,128)(2,1)}, u32[]{:S(2)}, u32[]{:S(2)}) collective-permute-start(bf16[2,128,2048]{2,1,0:T(8,128)(2,1)S(1)} %pad_maximum_fusion.5.refs_0_.refs_1_), channel_id=1, source_target_pairs={{0,2},{2,0},{4,6},{6,4},{8,10},{10,8},{12,14},{14,12},{16,18},{18,... | collective-permute-start | bytes 3145736 | tf_op jit(solution)/shard_map/ppermute | solution.py:89
  197.9 36.8 %collective-permute-start.23 = (bf16[2,128,2048]{2,1,0:T(8,128)(2,1)S(1)}, bf16[2,128,2048]{2,1,0:T(8,128)(2,1)}, u32[]{:S(2)}, u32[]{:S(2)}) collective-permute-start(bf16[2,128,2048]{2,1,0:T(8,128)(2,1)S(1)} %pad_maximum_fusion.5.refs_0_.refs_1_), channel_id=1, source_target_pairs={{0,4},{2,6},{4,0},{6,2},{8,12},{10,14},{12,8},{14,10},{16,20},{18,... | collective-permute-start | bytes 3145736 | tf_op jit(solution)/shard_map/ppermute | solution.py:89
  200.4 27.8 %all-to-all-start.1 = ((bf16[16,128,128]{1,2,0:T(8,128)(2,1)}), bf16[16,128,128]{1,2,0:T(8,128)(2,1)S(1)}, u32[]{:S(2)}, u32[]{:S(2)}) async-start(bf16[16,128,128]{1,2,0:T(8,128)(2,1)} %copy.309), calls=%async_computation.1 | async-start | bytes 1048576 | tf_op jit(solution)/shard_map/all_to_all | solution.py:215
  206.5 28.2 %collective-permute-start.24 = (bf16[128,2048]{1,0:T(8,128)(2,1)}, bf16[128,2048]{1,0:T(8,128)(2,1)}, u32[]{:S(2)}, u32[]{:S(2)}) collective-permute-start(bf16[128,2048]{1,0:T(8,128)(2,1)} %copy-done.87), channel_id=1, source_target_pairs={{0,8},{2,10},{4,12},{6,14},{8,0},{10,2},{12,4},{14,6},{16,24},{18,... | collective-permute-start | bytes 1572872 | tf_op jit(solution)/shard_map/ppermute | solution.py:89
  282.1 56.7 %collective-permute-start.36 = (bf16[704,2048]{1,0:T(8,128)(2,1)}, bf16[704,2048]{1,0:T(8,128)(2,1)}, u32[]{:S(2)}, u32[]{:S(2)}) collective-permute-start(bf16[704,2048]{1,0:T(8,128)(2,1)} %bitcast.276), channel_id=1, source_target_pairs={{0,1},{1,0},{2,3},{3,2},{4,5},{5,4},{6,7},{7,6},{8,9},{9,8},{10,11... | collective-permute-start | bytes 8650760 | tf_op jit(solution)/shard_map/ppermute | solution.py:190
  285.6 53.2 %collective-permute-start.37 = (bf16[704,2048]{1,0:T(8,128)(2,1)}, bf16[704,2048]{1,0:T(8,128)(2,1)}, u32[]{:S(2)}, u32[]{:S(2)}) collective-permute-start(bf16[704,2048]{1,0:T(8,128)(2,1)} %bitcast.281), channel_id=1, source_target_pairs={{0,1},{1,0},{2,3},{3,2},{4,5},{5,4},{6,7},{7,6},{8,9},{9,8},{10,11... | collective-permute-start | bytes 8650760 | tf_op jit(solution)/shard_map/ppermute | solution.py:190
  285.6 53.2 %collective-permute-start.38 = (bf16[704,2048]{1,0:T(8,128)(2,1)}, bf16[704,2048]{1,0:T(8,128)(2,1)}, u32[]{:S(2)}, u32[]{:S(2)}) collective-permute-start(bf16[704,2048]{1,0:T(8,128)(2,1)} %bitcast.286), channel_id=1, source_target_pairs={{0,1},{1,0},{2,3},{3,2},{4,5},{5,4},{6,7},{7,6},{8,9},{9,8},{10,11... | collective-permute-start | bytes 8650760 | tf_op jit(solution)/shard_map/ppermute | solution.py:190
  309.5 339.4 %all-gather.8.cloned.1.call-start = ((), (), s32[]{:S(2)}) async-start(), calls=%async_computation.14 | async-start | bytes 12976128 | tf_op jit(solution)/shard_map/all_gather | solution.py:834
  334.9 33.7 %collective-permute-start.41 = (bf16[2,128,2048]{2,1,0:T(8,128)(2,1)S(1)}, bf16[2,128,2048]{2,1,0:T(8,128)(2,1)}, u32[]{:S(2)}, u32[]{:S(2)}) collective-permute-start(bf16[2,128,2048]{2,1,0:T(8,128)(2,1)S(1)} %pad_maximum_fusion.6.refs_0_.refs_1_), channel_id=1, source_target_pairs={{0,2},{2,0},{4,6},{6,4},{8,10},{10,8},{12,14},{14,12},{16,18},{18,... | collective-permute-start | bytes 3145736 | tf_op jit(solution)/shard_map/ppermute | solution.py:89
  336.4 32.2 %collective-permute-start.42 = (bf16[2,128,2048]{2,1,0:T(8,128)(2,1)S(1)}, bf16[2,128,2048]{2,1,0:T(8,128)(2,1)}, u32[]{:S(2)}, u32[]{:S(2)}) collective-permute-start(bf16[2,128,2048]{2,1,0:T(8,128)(2,1)S(1)} %pad_maximum_fusion.6.refs_0_.refs_1_), channel_id=1, source_target_pairs={{0,4},{2,6},{4,0},{6,2},{8,12},{10,14},{12,8},{14,10},{16,20},{18,... | collective-permute-start | bytes 3145736 | tf_op jit(solution)/shard_map/ppermute | solution.py:89
  368.6 55.9 %collective-permute-start.43 = (bf16[2,128,2048]{2,1,0:T(8,128)(2,1)}, bf16[2,128,2048]{2,1,0:T(8,128)(2,1)S(1)}, u32[]{:S(2)}, u32[]{:S(2)}) collective-permute-start(bf16[2,128,2048]{2,1,0:T(8,128)(2,1)} %get-tuple-element.387), channel_id=1, source_target_pairs={{0,2},{2,0},{4,6},{6,4},{8,10},{10,8},{12,14},{14,12},{16,18},{18,... | collective-permute-start | bytes 3145736 | tf_op jit(solution)/shard_map/ppermute | solution.py:89
  369.2 56.0 %collective-permute-start.44 = (bf16[2,128,2048]{2,1,0:T(8,128)(2,1)}, bf16[2,128,2048]{2,1,0:T(8,128)(2,1)}, u32[]{:S(2)}, u32[]{:S(2)}) collective-permute-start(bf16[2,128,2048]{2,1,0:T(8,128)(2,1)} %get-tuple-element.388), channel_id=1, source_target_pairs={{0,4},{2,6},{4,0},{6,2},{8,12},{10,14},{12,8},{14,10},{16,20},{18,... | collective-permute-start | bytes 3145736 | tf_op jit(solution)/shard_map/ppermute | solution.py:89
  369.8 55.5 %collective-permute-start.45 = (bf16[2,128,2048]{2,1,0:T(8,128)(2,1)}, bf16[2,128,2048]{2,1,0:T(8,128)(2,1)}, u32[]{:S(2)}, u32[]{:S(2)}) collective-permute-start(bf16[2,128,2048]{2,1,0:T(8,128)(2,1)} %get-tuple-element.389), channel_id=1, source_target_pairs={{0,6},{2,4},{4,2},{6,0},{8,14},{10,12},{12,10},{14,8},{16,22},{18,... | collective-permute-start | bytes 3145736 | tf_op jit(solution)/shard_map/ppermute | solution.py:89
  374.0 50.1 %collective-permute-start.46 = (bf16[128,2048]{1,0:T(8,128)(2,1)}, bf16[128,2048]{1,0:T(8,128)(2,1)S(1)}, u32[]{:S(2)}, u32[]{:S(2)}) collective-permute-start(bf16[128,2048]{1,0:T(8,128)(2,1)} %slice_bitcast_fusion.8), channel_id=1, source_target_pairs={{0,2},{2,0},{4,6},{6,4},{8,10},{10,8},{12,14},{14,12},{16,18},{18,... | collective-permute-start | bytes 1572872 | tf_op jit(solution)/shard_map/ppermute | solution.py:89
  376.5 48.0 %collective-permute-start.47 = (bf16[128,2048]{1,0:T(8,128)(2,1)}, bf16[128,2048]{1,0:T(8,128)(2,1)S(1)}, u32[]{:S(2)}, u32[]{:S(2)}) collective-permute-start(bf16[128,2048]{1,0:T(8,128)(2,1)} %slice_bitcast_fusion.7), channel_id=1, source_target_pairs={{0,4},{2,6},{4,0},{6,2},{8,12},{10,14},{12,8},{14,10},{16,20},{18,... | collective-permute-start | bytes 1572872 | tf_op jit(solution)/shard_map/ppermute | solution.py:89
  425.3 33.4 %collective-permute-start.48 = (bf16[2,128,2048]{2,1,0:T(8,128)(2,1)}, bf16[2,128,2048]{2,1,0:T(8,128)(2,1)}, u32[]{:S(2)}, u32[]{:S(2)}) collective-permute-start(bf16[2,128,2048]{2,1,0:T(8,128)(2,1)} %get-tuple-element.454), channel_id=1, source_target_pairs={{0,2},{2,0},{4,6},{6,4},{8,10},{10,8},{12,14},{14,12},{16,18},{18,... | collective-permute-start | bytes 3145736 | tf_op jit(solution)/shard_map/ppermute | solution.py:89
  426.6 34.7 %collective-permute-start.49 = (bf16[2,128,2048]{2,1,0:T(8,128)(2,1)}, bf16[2,128,2048]{2,1,0:T(8,128)(2,1)}, u32[]{:S(2)}, u32[]{:S(2)}) collective-permute-start(bf16[2,128,2048]{2,1,0:T(8,128)(2,1)} %get-tuple-element.455), channel_id=1, source_target_pairs={{0,4},{2,6},{4,0},{6,2},{8,12},{10,14},{12,8},{14,10},{16,20},{18,... | collective-permute-start | bytes 3145736 | tf_op jit(solution)/shard_map/ppermute | solution.py:89
  427.7 60.2 %collective-permute-start.50 = (bf16[2,128,2048]{2,1,0:T(8,128)(2,1)}, bf16[2,128,2048]{2,1,0:T(8,128)(2,1)}, u32[]{:S(2)}, u32[]{:S(2)}) collective-permute-start(bf16[2,128,2048]{2,1,0:T(8,128)(2,1)} %get-tuple-element.456), channel_id=1, source_target_pairs={{0,6},{2,4},{4,2},{6,0},{8,14},{10,12},{12,10},{14,8},{16,22},{18,... | collective-permute-start | bytes 3145736 | tf_op jit(solution)/shard_map/ppermute | solution.py:89
  487.9 44.0 %collective-permute-start.51 = (bf16[2,128,2048]{2,1,0:T(8,128)(2,1)}, bf16[2,128,2048]{2,1,0:T(8,128)(2,1)}, u32[]{:S(2)}, u32[]{:S(2)}) collective-permute-start(bf16[2,128,2048]{2,1,0:T(8,128)(2,1)} %get-tuple-element.487), channel_id=1, source_target_pairs={{0,2},{2,0},{4,6},{6,4},{8,10},{10,8},{12,14},{14,12},{16,18},{18,... | collective-permute-start | bytes 3145736 | tf_op jit(solution)/shard_map/ppermute | solution.py:89
  489.4 42.5 %collective-permute-start.52 = (bf16[2,128,2048]{2,1,0:T(8,128)(2,1)}, bf16[2,128,2048]{2,1,0:T(8,128)(2,1)}, u32[]{:S(2)}, u32[]{:S(2)}) collective-permute-start(bf16[2,128,2048]{2,1,0:T(8,128)(2,1)} %get-tuple-element.488), channel_id=1, source_target_pairs={{0,4},{2,6},{4,0},{6,2},{8,12},{10,14},{12,8},{14,10},{16,20},{18,... | collective-permute-start | bytes 3145736 | tf_op jit(solution)/shard_map/ppermute | solution.py:89
  489.4 67.8 %collective-permute-start.53 = (bf16[2,128,2048]{2,1,0:T(8,128)(2,1)}, bf16[2,128,2048]{2,1,0:T(8,128)(2,1)}, u32[]{:S(2)}, u32[]{:S(2)}) collective-permute-start(bf16[2,128,2048]{2,1,0:T(8,128)(2,1)} %get-tuple-element.489), channel_id=1, source_target_pairs={{0,6},{2,4},{4,2},{6,0},{8,14},{10,12},{12,10},{14,8},{16,22},{18,... | collective-permute-start | bytes 3145736 | tf_op jit(solution)/shard_map/ppermute | solution.py:89
  557.3 54.5 %collective-permute-start.54 = (bf16[2,128,2048]{2,1,0:T(8,128)(2,1)}, bf16[2,128,2048]{2,1,0:T(8,128)(2,1)S(1)}, u32[]{:S(2)}, u32[]{:S(2)}) collective-permute-start(bf16[2,128,2048]{2,1,0:T(8,128)(2,1)} %get-tuple-element.502), channel_id=1, source_target_pairs={{0,2},{2,0},{4,6},{6,4},{8,10},{10,8},{12,14},{14,12},{16,18},{18,... | collective-permute-start | bytes 3145736 | tf_op jit(solution)/shard_map/ppermute | solution.py:89
  558.8 52.9 %collective-permute-start.55 = (bf16[2,128,2048]{2,1,0:T(8,128)(2,1)}, bf16[2,128,2048]{2,1,0:T(8,128)(2,1)}, u32[]{:S(2)}, u32[]{:S(2)}) collective-permute-start(bf16[2,128,2048]{2,1,0:T(8,128)(2,1)} %get-tuple-element.503), channel_id=1, source_target_pairs={{0,4},{2,6},{4,0},{6,2},{8,12},{10,14},{12,8},{14,10},{16,20},{18,... | collective-permute-start | bytes 3145736 | tf_op jit(solution)/shard_map/ppermute | solution.py:89
  558.8 52.9 %collective-permute-start.56 = (bf16[2,128,2048]{2,1,0:T(8,128)(2,1)}, bf16[2,128,2048]{2,1,0:T(8,128)(2,1)}, u32[]{:S(2)}, u32[]{:S(2)}) collective-permute-start(bf16[2,128,2048]{2,1,0:T(8,128)(2,1)} %get-tuple-element.504), channel_id=1, source_target_pairs={{0,6},{2,4},{4,2},{6,0},{8,14},{10,12},{12,10},{14,8},{16,22},{18,... | collective-permute-start | bytes 3145736 | tf_op jit(solution)/shard_map/ppermute | solution.py:89
  560.8 51.0 %all-to-all-start.4 = ((f32[16,1,128]{2,1,0:T(1,128)}), f32[16,1,128]{2,1,0:T(1,128)S(1)}, u32[]{:S(2)}, u32[]{:S(2)}) async-start(f32[16,1,128]{2,1,0:T(1,128)} %get-tuple-element.513), calls=%async_computation.4 | async-start | bytes 16384 | tf_op jit(solution)/shard_map/all_to_all | solution.py:215
  571.5 102.5 %collective-permute-start.61 = (bf16[128,2048]{1,0:T(8,128)(2,1)}, bf16[128,2048]{1,0:T(8,128)(2,1)}, u32[]{:S(2)}, u32[]{:S(2)}) collective-permute-start(bf16[128,2048]{1,0:T(8,128)(2,1)} %get-tuple-element.719), channel_id=1, source_target_pairs={{0,16},{2,18},{4,20},{6,22},{8,24},{10,26},{12,28},{14,30},{16,0},... | collective-permute-start | bytes 1572872 | tf_op jit(solution)/shard_map/ppermute | solution.py:89
  573.9 123.6 %collective-permute-start.62 = (bf16[128,2048]{1,0:T(8,128)(2,1)}, bf16[128,2048]{1,0:T(8,128)(2,1)}, u32[]{:S(2)}, u32[]{:S(2)}) collective-permute-start(bf16[128,2048]{1,0:T(8,128)(2,1)} %get-tuple-element.718), channel_id=1, source_target_pairs={{0,24},{2,26},{4,28},{6,30},{8,16},{10,18},{12,20},{14,22},{16,8},... | collective-permute-start | bytes 1572872 | tf_op jit(solution)/shard_map/ppermute | solution.py:89
  617.2 30.9 %collective-permute-start.59 = (bf16[128,2048]{1,0:T(8,128)(2,1)S(1)}, bf16[128,2048]{1,0:T(8,128)(2,1)S(1)}, u32[]{:S(2)}, u32[]{:S(2)}) collective-permute-start(bf16[128,2048]{1,0:T(8,128)(2,1)S(1)} %get-tuple-element.720), channel_id=1, source_target_pairs={{0,24},{2,26},{4,28},{6,30},{8,16},{10,18},{12,20},{14,22},{16,8},... | collective-permute-start | bytes 1572872 | tf_op jit(solution)/shard_map/ppermute | solution.py:89
  620.3 28.6 %collective-permute-start.57 = (bf16[128,2048]{1,0:T(8,128)(2,1)S(1)}, bf16[128,2048]{1,0:T(8,128)(2,1)}, u32[]{:S(2)}, u32[]{:S(2)}) collective-permute-start(bf16[128,2048]{1,0:T(8,128)(2,1)S(1)} %fusion.30), channel_id=1, source_target_pairs={{0,8},{2,10},{4,12},{6,14},{8,0},{10,2},{12,4},{14,6},{16,24},{18,... | collective-permute-start | bytes 1572872 | tf_op jit(solution)/shard_map/ppermute | solution.py:89
  669.2 39.2 %collective-permute-start.65 = (bf16[704,2048]{1,0:T(8,128)(2,1)}, bf16[704,2048]{1,0:T(8,128)(2,1)}, u32[]{:S(2)}, u32[]{:S(2)}) collective-permute-start(bf16[704,2048]{1,0:T(8,128)(2,1)} %convolution_convert_fusion.1), channel_id=1, source_target_pairs={{0,1},{1,0},{2,3},{3,2},{4,5},{5,4},{6,7},{7,6},{8,9},{9,8},{10,11... | collective-permute-start | bytes 8650760 | tf_op jit(solution)/shard_map/ppermute | solution.py:190
  670.4 45.6 %collective-permute-start.64 = (bf16[704,2048]{1,0:T(8,128)(2,1)}, bf16[704,2048]{1,0:T(8,128)(2,1)}, u32[]{:S(2)}, u32[]{:S(2)}) collective-permute-start(bf16[704,2048]{1,0:T(8,128)(2,1)} %convolution_convert_fusion.2), channel_id=1, source_target_pairs={{0,1},{1,0},{2,3},{3,2},{4,5},{5,4},{6,7},{7,6},{8,9},{9,8},{10,11... | collective-permute-start | bytes 8650760 | tf_op jit(solution)/shard_map/ppermute | solution.py:190
  674.0 57.1 %collective-permute-start.69 = (bf16[1024,2048]{1,0:T(8,128)(2,1)}, bf16[1024,2048]{1,0:T(8,128)(2,1)}, u32[]{:S(2)}, u32[]{:S(2)}) collective-permute-start(bf16[1024,2048]{1,0:T(8,128)(2,1)} %convolution_convert_fusion), channel_id=1, source_target_pairs={{0,1},{1,0},{2,3},{3,2},{4,5},{5,4},{6,7},{7,6},{8,9},{9,8},{10,11... | collective-permute-start | bytes 12582920 | tf_op jit(solution)/shard_map/ppermute | solution.py:190
  701.8 66.0 %all-to-all-start.6 = ((bf16[16,128,576]{1,2,0:T(8,128)(2,1)}), bf16[16,128,576]{1,2,0:T(8,128)(2,1)}, u32[]{:S(2)}, u32[]{:S(2)}) async-start(bf16[16,128,576]{1,2,0:T(8,128)(2,1)} %copy.320), calls=%async_computation.6 | async-start | bytes 4718592 | tf_op jit(solution)/shard_map/all_to_all | solution.py:215
  707.1 216.9 %reduce-scatter.2.cloned.1.call-start = ((), (), s32[]{:S(2)}) async-start(), calls=%async_computation.15 | async-start | bytes 4456448 | tf_op jit(solution)/shard_map/reduce_scatter | solution.py:869
  799.1 27.5 %all-to-all-start.7 = ((bf16[16,64,256]{2,1,0:T(8,128)(2,1)}), bf16[16,64,256]{2,1,0:T(8,128)(2,1)S(1)}, u32[]{:S(2)}, u32[]{:S(2)}) async-start(bf16[16,64,256]{2,1,0:T(8,128)(2,1)} %fusion.24), calls=%async_computation.7 | async-start | bytes 1048576 | tf_op jit(solution)/shard_map/all_to_all | solution.py:215
  826.6 28.3 %all-to-all-start.9 = ((bf16[16,64,352]{2,1,0:T(8,128)(2,1)}), bf16[16,64,352]{2,1,0:T(8,128)(2,1)}, u32[]{:S(2)}, u32[]{:S(2)}) async-start(bf16[16,64,352]{2,1,0:T(8,128)(2,1)} %fusion.8), calls=%async_computation.9 | async-start | bytes 1572864 | tf_op jit(solution)/shard_map/all_to_all | solution.py:215
  879.7 35.3 %all-to-all-start.10 = ((bf16[16,64,640]{2,1,0:T(8,128)(2,1)}), bf16[16,64,640]{2,1,0:T(8,128)(2,1)}, u32[]{:S(2)}, u32[]{:S(2)}) async-start(bf16[16,64,640]{2,1,0:T(8,128)(2,1)} %fusion.2), calls=%async_computation.10 | async-start | bytes 2621440 | tf_op jit(solution)/shard_map/all_to_all | solution.py:215
  (134 other events, 2048.3 us)
Sparse Core Ops, SparseCore 0:
  13.0 81.2 all-gather.3
  97.2 102.8 all-gather.5
  425.4 132.3 all-gather.7
  736.6 120.2 reduce-scatter.1

commit v3 on v2

--- a/solution.py
+++ b/solution.py
@@ -887,11 +887,11 @@
     down_rows = shared_down.shape[0]
     grad_back = shared_sums[0].reshape(fsdp, down_rows, width)
     grad_shared_down = scatter_fsdp(in_fsdp_order([grad_back[i] for i in range(fsdp)]))
-    grad_in = to_rows(jnp.concatenate(shared_sums[1:], axis=-1), rows)
+    grad_in = jnp.concatenate(shared_sums[1:], axis=-1).reshape(ctx, fsdp, rows, -1)
 
     grad_query_w = mm_tn(query_rows(normed_all), grad_query).reshape(ctx, fsdp, rows, QK)
     grad_expand = mm_tn(latent_all, grad_expanded).reshape(ctx, fsdp, rows, -1)
-    by_heads = jnp.concatenate([grad_query_w, grad_expand], axis=-1)
+    by_heads = jnp.concatenate([grad_query_w, grad_expand, grad_in], axis=-1)
     by_heads = to_rows(by_heads.reshape(width, by_heads.shape[-1]), rows)
 
     own_rows = ctx_rank * part
@@ -915,17 +915,16 @@
         axis=1,
     ).reshape(ctx, fsdp, rows, -1)
     grad_small = scatter_fsdp(in_fsdp_order([grad_small[:, i] for i in range(fsdp)]))
-    grad_small, by_heads, query_own, grad_in = together(
-        grad_small.astype(bf16), by_heads, query_own, grad_in
-    )
+    grad_small, by_heads, query_own = together(grad_small.astype(bf16), by_heads, query_own)
     grad_normed = mm_nt(query_own.reshape(part, HEADS * QK), query_full)
     grad_small, grad_normed = together(to_owner(grad_small), grad_normed)
     grad_small = jnp.sum(grad_small.astype(f32), axis=0)
-    grad_in = grad_in.transpose(1, 0, 2)
+    heads_end = by_heads.shape[-1] - 2 * hidden_shared
+    grad_in = by_heads[..., heads_end:].transpose(1, 0, 2)
     grad_shared_gate = grad_in[..., :hidden_shared].reshape(rows, ctx * hidden_shared)
     grad_shared_up = grad_in[..., hidden_shared:].reshape(rows, ctx * hidden_shared)
     grad_query_w = from_head_blocks(by_heads[..., :QK])
-    grad_expand = from_head_blocks(by_heads[..., QK:].reshape(ctx, kv_rows, NOPE + VHEAD))
+    grad_expand = from_head_blocks(by_heads[..., QK:heads_end].reshape(ctx, kv_rows, NOPE + VHEAD))
     grad_reduce = grad_small[:, :compressed_width]
     grad_normed = grad_normed + mm_nt(grad_compressed, reduce_full)
     attn_grad_in, _ = rms_backward(tokens, rms_factor(tokens), attn_gain, grad_normed)

time: 942 us -> 955 us (1.014)
  waiting for transfers between devices: 315 us -> 342 us
    all_to_all x11 -> x10, waiting for transfers between devices: 99 us -> 118 us  [to_owner(): lax.all_to_all(blocks, 'ctx', split_axis=0, concat_axis=0, tiled=True)]
    all_to_all x11 -> x10, starting transfers between devices: 66.4 us -> 61.8 us  [to_owner(): lax.all_to_all(blocks, 'ctx', split_axis=0, concat_axis=0, tiled=True)]
    unnamed x198 -> x188, local copies, waits for them, and re-layouts: 19 us -> 21.1 us
  transfers between devices with their start and end apart: 86 -> 84, of which waited for: 37 -> 36; matrix products, arithmetic and copies ran while one was open for 27% -> 26% of each run, Pallas kernels for 20% -> 19%
where the time goes in v3:
time: 955 us; the launch traced here: 949 us
  waiting for transfers between devices  342 us (36%)
  Pallas kernels  184 us (19%)
  starting transfers between devices  139 us (15%)
  local copies, waits for them, and re-layouts  92.5 us (10%)
  matrix products  90.1 us (9%)
  other arithmetic  86.7 us (9%)
  between operations  15.5 us (2%)
    ppermute x57, waiting for transfers between devices, hop(): return lax.ppermute(value, 'ctx', [(i, i ^ mask) for i in range(16)])  223 us
    pallas_call x4, Pallas kernels, expert_call(): pl.pallas_call(kernel, grid_spec=pltpu.PrefetchScalarGridSpec(num_scalar_...  131 us
    all_to_all x10, waiting for transfers between devices, to_owner(): lax.all_to_all(blocks, 'ctx', split_axis=0, concat_axis=0, tiled=True)  118 us
    ppermute x57, starting transfers between devices, hop(): return lax.ppermute(value, 'ctx', [(i, i ^ mask) for i in range(16)])  75.9 us
    all_to_all x10, starting transfers between devices, to_owner(): lax.all_to_all(blocks, 'ctx', split_axis=0, concat_axis=0, tiled=True)  61.8 us
    dot_general x15, matrix products, mm_tn(): lax.dot_general(left, right, (((0,), (0,)), ((), ())), preferred_element_...  58.9 us
    pallas_call x2, Pallas kernels, project(): pl.pallas_call(project_kernel, grid_spec=pltpu.PrefetchScalarGridSpec(num...  24.1 us
    dot_general x4, matrix products, mm_nt(): lax.dot_general(left, right, (((1,), (1,)), ((), ())), preferred_element_...  22.1 us
  transfers between devices with their start and end apart: 84, of which 36 were waited for; matrix products, arithmetic and copies ran while one was open for 26% of the time, Pallas kernels for 19%

profile of v3, /device:TPU:8, one launch (start us, length us, event | category | flops | bytes accessed | tf_op | source)
XLA Modules:
  0.0 949.1 jit_solution(16116252821547755249)
XLA Ops:
  20.4 18.1 %collective-permute-done = bf16[128,2048]{1,0:T(8,128)(2,1)} collective-permute-done((bf16[128,2048]{1,0:T(8,128)(2,1)}, bf16[128,2048]{1,0:T(8,128)(2,1)}, u32[]{:S(2)}, u32[]{:S(2)}) %collective-permute-start) | collective-permute-done | bytes 524320 | tf_op jit(solution)/shard_map/ppermute | solution.py:89
  53.1 5.5 all-to-all-start
  64.1 14.4 %collective-permute-done.5 = bf16[128,2048]{1,0:T(8,128)(2,1)} collective-permute-done((bf16[128,2048]{1,0:T(8,128)(2,1)}, bf16[128,2048]{1,0:T(8,128)(2,1)}, u32[]{:S(2)}, u32[]{:S(2)}) %collective-permute-start.5) | collective-permute-done | bytes 524320 | tf_op jit(solution)/shard_map/ppermute | solution.py:89
  95.9 9.6 %collective-permute-done.8.refs_2_.refs_3_ = bf16[2,128,2048]{2,1,0:T(8,128)(2,1)S(1)} collective-permute-done((bf16[2,128,2048]{2,1,0:T(8,128)(2,1)S(1)}, bf16[2,128,2048]{2,1,0:T(8,128)(2,1)S(1)}, u32[]{:S(2)}, u32[]{:S(2)}) %collective-permute-start.8) | collective-permute-done | bytes 1048608 | tf_op jit(solution)/shard_map/ppermute | solution.py:89
  131.7 12.0 %project.2 = (bf16[2048,2048]{1,0:T(8,128)(2,1)}, bf16[2048,256]{1,0:T(8,128)(2,1)}, bf16[2048,256]{1,0:T(8,128)(2,1)}, bf16[2048,128]{1,0:T(8,128)(2,1)}, bf16[2048,512]{1,0:T(8,128)(2,1)}) custom-call(s32[3]{0:T(128)} %get-tuple-element.743.base_ref, bf16[1,128,2048]{2,1,0:T(8,128)(2,1)} %refs_0_.1, bf16[1,128,2048]{2,1,0:T(8,128)(2,1)} %bitcast.27.refs_1_, ...), custom_call_target="tpu_custom_call" | custom-call | flops 3758096384 | bytes 12058624 | tf_op jit(solution)/shard_map/project/pallas_call | solution.py:270
  143.8 12.1 %project.3 = (bf16[2048,2048]{1,0:T(8,128)(2,1)}, bf16[2048,256]{1,0:T(8,128)(2,1)}, bf16[2048,256]{1,0:T(8,128)(2,1)}, bf16[2048,128]{1,0:T(8,128)(2,1)}, bf16[2048,512]{1,0:T(8,128)(2,1)}) custom-call(s32[3]{0:T(128)} %get-tuple-element.742.base_ref, ...), custom_call_target="tpu_custom_call", output_to_operand_aliasing={{0}: (15, {}), {1}: (16, {}), {2}: (17, {}), {3}: (18, {}),... | custom-call | flops 3758096384 | bytes 12058624 | tf_op jit(solution)/shard_map/project/pallas_call | solution.py:270
  165.3 11.5 %attend.1 = (f32[2048,128]{1,0:T(8,128)S(1)}, bf16[2048,128]{1,0:T(8,128)(2,1)S(1)}, f32[2048,1]{1,0:T(8,128)S(1)}) custom-call(s32[2048,1]{1,0:T(8,128)S(1)} %iota.38.pos_ref, bf16[2048,256]{1,0:T(8,128)(2,1)S(1)} %copy-done.2, bf16[2048,256]{1,0:T(8,128)(2,1)} %get-tuple-element.493.key_ref, bf16[2048,128]{1,0:T(8,128)(2,1)S(1)} %copy-done.3), custom_call_target="tpu_custom_call" | custom-call | flops 2684354560 | bytes 5242880 | tf_op jit(solution)/shard_map/attend/pallas_call | solution.py:394
  178.9 5.9 collective-permute-done.18
  185.6 11.9 %collective-permute-done.20 = bf16[128,2048]{1,0:T(8,128)(2,1)S(1)} collective-permute-done((bf16[128,2048]{1,0:T(8,128)(2,1)}, bf16[128,2048]{1,0:T(8,128)(2,1)S(1)}, u32[]{:S(2)}, u32[]{:S(2)}) %collective-permute-start.20) | collective-permute-done | bytes 524320 | tf_op jit(solution)/shard_map/ppermute | solution.py:89
  200.9 6.0 all-to-all-start.1
  211.6 17.1 %all-to-all-done.1 = bf16[16,128,128]{1,2,0:T(8,128)(2,1)S(1)} async-done(((bf16[16,128,128]{1,2,0:T(8,128)(2,1)}), bf16[16,128,128]{1,2,0:T(8,128)(2,1)S(1)}, u32[]{:S(2)}, u32[]{:S(2)}) %all-to-all-start.1) | async-done | bytes 524320 | tf_op jit(solution)/shard_map/all_to_all | solution.py:215
  228.7 6.7 all-to-all-start.2
  240.6 13.4 %all-to-all-done.2 = bf16[16,64,352]{2,1,0:T(8,128)(2,1)} async-done(((bf16[16,64,352]{2,1,0:T(8,128)(2,1)}), bf16[16,64,352]{2,1,0:T(8,128)(2,1)}, u32[]{:S(2)}, u32[]{:S(2)}) %all-to-all-start.2) | async-done | bytes 720928 | tf_op jit(solution)/shard_map/all_to_all | solution.py:215
  270.9 12.1 %collective-permute-done.27 = bf16[128,2048]{1,0:T(8,128)(2,1)} collective-permute-done((bf16[128,2048]{1,0:T(8,128)(2,1)S(1)}, bf16[128,2048]{1,0:T(8,128)(2,1)}, u32[]{:S(2)}, u32[]{:S(2)}) %collective-permute-start.27) | collective-permute-done | bytes 524320 | tf_op jit(solution)/shard_map/ppermute | solution.py:89
  296.6 6.4 collective-permute-done.31
  305.6 5.0 all-to-all-start.3
  312.2 7.9 collective-permute-done.33
  323.3 11.6 %collective-permute-done.34 = bf16[128,2048]{1,0:T(8,128)(2,1)} collective-permute-done((bf16[128,2048]{1,0:T(8,128)(2,1)}, bf16[128,2048]{1,0:T(8,128)(2,1)}, u32[]{:S(2)}, u32[]{:S(2)}) %collective-permute-start.34) | collective-permute-done | bytes 524320 | tf_op jit(solution)/shard_map/ppermute | solution.py:89
  340.1 29.7 %experts_forward.2 = (bf16[2,128,2048]{2,1,0:T(8,128)(2,1)}, bf16[2,128,2048]{2,1,0:T(8,128)(2,1)}, bf16[2,128,2048]{2,1,0:T(8,128)(2,1)}, bf16[2,128,2048]{2,1,...) custom-call(s32[3]{0:T(128)} %get-tuple-element.743.base_ref, ...), custom_call_target="tpu_custom_call" | custom-call | flops 11072962560 | bytes 41943040 | tf_op jit(solution)/shard_map/experts_forward/pallas_call | solution.py:586
  376.5 34.5 %experts_backward.2 = (bf16[2,128,2048]{2,1,0:T(8,128)(2,1)}, bf16[2,128,2048]{2,1,0:T(8,128)(2,1)}, bf16[2,128,2048]{2,1,0:T(8,128)(2,1)}, bf16[2,128,2048]{2,1...) custom-call(s32[3]{0:T(128)} %get-tuple-element.743.base_ref, ...), custom_call_target="tpu_custom_call" | custom-call | flops 11072962560 | bytes 41943040 | tf_op jit(solution)/shard_map/experts_backward/pallas_call | solution.py:586
  411.0 14.3 %collective-permute-done.46 = bf16[128,2048]{1,0:T(8,128)(2,1)S(1)} collective-permute-done((bf16[128,2048]{1,0:T(8,128)(2,1)S(1)}, bf16[128,2048]{1,0:T(8,128)(2,1)S(1)}, u32[]{:S(2)}, u32[]{:S(2)}) %collective-permute-start.46) | collective-permute-done | bytes 524320 | tf_op jit(solution)/shard_map/ppermute | solution.py:89
  430.5 29.9 %experts_forward.3 = (bf16[2,128,2048]{2,1,0:T(8,128)(2,1)}, bf16[2,128,2048]{2,1,0:T(8,128)(2,1)}, bf16[2,128,2048]{2,1,0:T(8,128)(2,1)}, bf16[2,128,2048]{2,1,...) custom-call(s32[3]{0:T(128)} %get-tuple-element.742.base_ref, ...), custom_call_target="tpu_custom_call", output_to_operand_aliasing={{4}: (20, {}), {5}: (21, {}), {6}: (22, {}), {7}: (23, {}),... | custom-call | flops 11072962560 | bytes 41943040 | tf_op jit(solution)/shard_map/experts_forward/pallas_call | solution.py:586
  464.6 25.7 %collective-permute-done.50 = bf16[2,128,2048]{2,1,0:T(8,128)(2,1)} collective-permute-done((bf16[2,128,2048]{2,1,0:T(8,128)(2,1)}, bf16[2,128,2048]{2,1,0:T(8,128)(2,1)}, u32[]{:S(2)}, u32[]{:S(2)}) %collective-permute-start.50) | collective-permute-done | bytes 1048608 | tf_op jit(solution)/shard_map/ppermute | solution.py:89
  493.8 36.5 %experts_backward.3 = (bf16[2,128,2048]{2,1,0:T(8,128)(2,1)}, bf16[2,128,2048]{2,1,0:T(8,128)(2,1)}, bf16[2,128,2048]{2,1,0:T(8,128)(2,1)}, bf16[2,128,2048]{2,1...) custom-call(s32[3]{0:T(128)} %get-tuple-element.742.base_ref, ...), custom_call_target="tpu_custom_call", output_to_operand_aliasing={{4}: (27, {}), {5}: (28, {}), {6}: (29, {}), {7}: (30, {}),... | custom-call | flops 11072962560 | bytes 41943040 | tf_op jit(solution)/shard_map/experts_backward/pallas_call | solution.py:586
  530.3 5.1 collective-permute-done.51
  535.9 22.7 %collective-permute-done.53 = bf16[2,128,2048]{2,1,0:T(8,128)(2,1)} collective-permute-done((bf16[2,128,2048]{2,1,0:T(8,128)(2,1)}, bf16[2,128,2048]{2,1,0:T(8,128)(2,1)}, u32[]{:S(2)}, u32[]{:S(2)}) %collective-permute-start.53) | collective-permute-done | bytes 1048608 | tf_op jit(solution)/shard_map/ppermute | solution.py:89
  562.1 6.3 all-to-all-start.4
  591.5 5.0 fusion.61
  601.1 5.3 fusion.60
  624.0 19.1 %collective-permute-done.58 = bf16[128,2048]{1,0:T(8,128)(2,1)S(1)} collective-permute-done((bf16[128,2048]{1,0:T(8,128)(2,1)S(1)}, bf16[128,2048]{1,0:T(8,128)(2,1)S(1)}, u32[]{:S(2)}, u32[]{:S(2)}) %collective-permute-start.58) | collective-permute-done | bytes 524320 | tf_op jit(solution)/shard_map/ppermute | solution.py:89
  643.1 9.3 collective-permute-done.59
  655.9 6.7 fusion.10
  663.6 7.0 all-to-all-start.5
  674.8 8.5 all-to-all-done.5
  686.3 17.5 %attend_grad.1 = (bf16[2048,192]{1,0:T(8,128)(2,1)S(1)}, bf16[2048,256]{1,0:T(8,128)(2,1)S(1)}, bf16[2048,576]{1,0:T(8,128)(2,1)}) custom-call(s32[2048,1]{1,0:T(8,128)S(1)} %iota.39.pos_ref, f32[2048,128]{1,0:T(8,128)S(1)} %copy-done, bf16[2048,256]{1,0:T(8,128)(2,1)} %get-tuple-element.492.query_ref, bf16[2048,256]{1,0:T(8,128)(2,1)} %get-tuple-element.493.key_ref, ...), custom_call_target="tpu_custom_call" | custom-call | flops 6979321856 | bytes 10485760 | tf_op jit(solution)/shard_map/attend_grad/pallas_call | solution.py:419
  708.1 5.8 all-to-all-start.6
  718.9 7.5 convert_add_fusion
  726.4 5.8 convert_add_fusion.1
  736.1 28.4 %all-to-all-done.6 = bf16[16,128,576]{1,2,0:T(8,128)(2,1)} async-done(((bf16[16,128,576]{1,2,0:T(8,128)(2,1)}), bf16[16,128,576]{1,2,0:T(8,128)(2,1)}, u32[]{:S(2)}, u32[]{:S(2)}) %all-to-all-start.6) | async-done | bytes 2359328 | tf_op jit(solution)/shard_map/all_to_all | solution.py:215
  776.1 6.1 fusion.65
  788.4 5.4 add_convert_fusion
  803.1 6.2 all-to-all-start.7
  830.3 23.2 %all-to-all-done.7 = bf16[16,64,608]{2,1,0:T(8,128)(2,1)} async-done(((bf16[16,64,608]{2,1,0:T(8,128)(2,1)}), bf16[16,64,608]{2,1,0:T(8,128)(2,1)}, u32[]{:S(2)}, u32[]{:S(2)}) %all-to-all-start.7) | async-done | bytes 1245216 | tf_op jit(solution)/shard_map/all_to_all | solution.py:215
  853.5 7.0 all-to-all-start.8
  870.6 17.2 %all-to-all-done.8 = bf16[16,128,192]{1,2,0:T(8,128)(2,1)S(1)} async-done(((bf16[16,128,192]{1,2,0:T(8,128)(2,1)}), bf16[16,128,192]{1,2,0:T(8,128)(2,1)S(1)}, u32[]{:S(2)}, u32[]{:S(2)}) %all-to-all-start.8) | async-done | bytes 786464 | tf_op jit(solution)/shard_map/all_to_all | solution.py:215
  887.7 6.1 all-to-all-start.9
  911.3 10.0 %fusion.67 = f32[128,2048]{1,0:T(8,128)} fusion(bf16[128,3072]{0,1:T(8,128)(2,1)S(1)} %bitcast.300, bf16[2048,3072]{1,0:T(8,128)(2,1)} %all-gather.8.cloned.1.call-done), kind=kOutput, calls=%fused_computation.181 | convolution fusion | flops 1610612736 | bytes 14417920 | tf_op jit(solution)/shard_map/dot_general | solution.py:33
  921.3 10.4 %all-to-all-done.9 = bf16[16,64,640]{2,1,0:T(8,128)(2,1)} async-done(((bf16[16,64,640]{2,1,0:T(8,128)(2,1)}), bf16[16,64,640]{2,1,0:T(8,128)(2,1)}, u32[]{:S(2)}, u32[]{:S(2)}) %all-to-all-start.9) | async-done | bytes 1310752 | tf_op jit(solution)/shard_map/all_to_all | solution.py:215
  (492 shorter events, 323.9 us)
Async XLA Ops:
  7.2 107.7 %all-gather.4.cloned.1.call-start = ((), (), s32[]{:S(2)}) async-start(), calls=%async_computation.11 | async-start | bytes 3244032 | tf_op jit(solution)/shard_map/all_gather | solution.py:698
  12.9 243.8 %all-gather.6.cloned.1.call-start = ((), (), s32[]{:S(2)}) async-start(), calls=%async_computation.12 | async-start | bytes 8650752 | tf_op jit(solution)/shard_map/all_gather | solution.py:729
  46.5 32.0 %collective-permute-start.5 = (bf16[128,2048]{1,0:T(8,128)(2,1)}, bf16[128,2048]{1,0:T(8,128)(2,1)}, u32[]{:S(2)}, u32[]{:S(2)}) collective-permute-start(bf16[128,2048]{1,0:T(8,128)(2,1)} %collective-permute-done.3), channel_id=1, source_target_pairs={{0,2},{2,0},{4,6},{6,4},{8,10},{10,8},{12,14},{14,12},{16,18},{18,... | collective-permute-start | bytes 1572872 | tf_op jit(solution)/shard_map/ppermute | solution.py:89
  53.1 41.8 %all-to-all-start = ((bf16[16,64,322]{2,1,0:T(8,128)(2,1)}), bf16[16,64,322]{2,1,0:T(8,128)(2,1)}, u32[]{:S(2)}, u32[]{:S(2)}) async-start(bf16[16,64,322]{2,1,0:T(8,128)(2,1)} %concatenate.39), calls=%async_computation | async-start | bytes 1572864 | tf_op jit(solution)/shard_map/all_to_all | solution.py:215
  126.6 29.9 %collective-permute-start.14 = (bf16[128,2048]{1,0:T(8,128)(2,1)S(1)}, bf16[128,2048]{1,0:T(8,128)(2,1)}, u32[]{:S(2)}, u32[]{:S(2)}) collective-permute-start(bf16[128,2048]{1,0:T(8,128)(2,1)S(1)} %bitcast.324), channel_id=1, source_target_pairs={{0,8},{2,10},{4,12},{6,14},{8,0},{10,2},{12,4},{14,6},{16,24},{18,... | collective-permute-start | bytes 1572872 | tf_op jit(solution)/shard_map/ppermute | solution.py:89
  126.7 32.6 %collective-permute-start.15 = (bf16[128,2048]{1,0:T(8,128)(2,1)S(1)}, bf16[128,2048]{1,0:T(8,128)(2,1)S(1)}, u32[]{:S(2)}, u32[]{:S(2)}) collective-permute-start(bf16[128,2048]{1,0:T(8,128)(2,1)S(1)} %bitcast.325), channel_id=1, source_target_pairs={{0,16},{2,18},{4,20},{6,22},{8,24},{10,26},{12,28},{14,30},{16,0},... | collective-permute-start | bytes 1572872 | tf_op jit(solution)/shard_map/ppermute | solution.py:89
  128.8 30.5 %collective-permute-start.16 = (bf16[128,2048]{1,0:T(8,128)(2,1)S(1)}, bf16[128,2048]{1,0:T(8,128)(2,1)S(1)}, u32[]{:S(2)}, u32[]{:S(2)}) collective-permute-start(bf16[128,2048]{1,0:T(8,128)(2,1)S(1)} %bitcast.326), channel_id=1, source_target_pairs={{0,2},{2,0},{4,6},{6,4},{8,10},{10,8},{12,14},{14,12},{16,18},{18,... | collective-permute-start | bytes 1572872 | tf_op jit(solution)/shard_map/ppermute | solution.py:89
  129.1 30.1 %collective-permute-start.17 = (bf16[128,2048]{1,0:T(8,128)(2,1)S(1)}, bf16[128,2048]{1,0:T(8,128)(2,1)}, u32[]{:S(2)}, u32[]{:S(2)}) collective-permute-start(bf16[128,2048]{1,0:T(8,128)(2,1)S(1)} %bitcast.327), channel_id=1, source_target_pairs={{0,4},{2,6},{4,0},{6,2},{8,12},{10,14},{12,8},{14,10},{16,20},{18,... | collective-permute-start | bytes 1572872 | tf_op jit(solution)/shard_map/ppermute | solution.py:89
  160.9 36.7 %collective-permute-start.20 = (bf16[128,2048]{1,0:T(8,128)(2,1)}, bf16[128,2048]{1,0:T(8,128)(2,1)S(1)}, u32[]{:S(2)}, u32[]{:S(2)}) collective-permute-start(bf16[128,2048]{1,0:T(8,128)(2,1)} %collective-permute-done.14), channel_id=1, source_target_pairs={{0,2},{2,0},{4,6},{6,4},{8,10},{10,8},{12,14},{14,12},{16,18},{18,... | collective-permute-start | bytes 1572872 | tf_op jit(solution)/shard_map/ppermute | solution.py:89
  161.4 36.1 %collective-permute-start.21 = (bf16[128,2048]{1,0:T(8,128)(2,1)}, bf16[128,2048]{1,0:T(8,128)(2,1)S(1)}, u32[]{:S(2)}, u32[]{:S(2)}) collective-permute-start(bf16[128,2048]{1,0:T(8,128)(2,1)} %collective-permute-done.14), channel_id=1, source_target_pairs={{0,4},{2,6},{4,0},{6,2},{8,12},{10,14},{12,8},{14,10},{16,20},{18,... | collective-permute-start | bytes 1572872 | tf_op jit(solution)/shard_map/ppermute | solution.py:89
  197.7 37.7 %collective-permute-start.22 = (bf16[2,128,2048]{2,1,0:T(8,128)(2,1)S(1)}, bf16[2,128,2048]{2,1,0:T(8,128)(2,1)}, u32[]{:S(2)}, u32[]{:S(2)}) collective-permute-start(bf16[2,128,2048]{2,1,0:T(8,128)(2,1)S(1)} %pad_maximum_fusion.5.refs_0_.refs_1_), channel_id=1, source_target_pairs={{0,2},{2,0},{4,6},{6,4},{8,10},{10,8},{12,14},{14,12},{16,18},{18,... | collective-permute-start | bytes 3145736 | tf_op jit(solution)/shard_map/ppermute | solution.py:89
  198.4 37.0 %collective-permute-start.23 = (bf16[2,128,2048]{2,1,0:T(8,128)(2,1)S(1)}, bf16[2,128,2048]{2,1,0:T(8,128)(2,1)}, u32[]{:S(2)}, u32[]{:S(2)}) collective-permute-start(bf16[2,128,2048]{2,1,0:T(8,128)(2,1)S(1)} %pad_maximum_fusion.5.refs_0_.refs_1_), channel_id=1, source_target_pairs={{0,4},{2,6},{4,0},{6,2},{8,12},{10,14},{12,8},{14,10},{16,20},{18,... | collective-permute-start | bytes 3145736 | tf_op jit(solution)/shard_map/ppermute | solution.py:89
  283.0 57.1 %collective-permute-start.36 = (bf16[704,2048]{1,0:T(8,128)(2,1)}, bf16[704,2048]{1,0:T(8,128)(2,1)}, u32[]{:S(2)}, u32[]{:S(2)}) collective-permute-start(bf16[704,2048]{1,0:T(8,128)(2,1)} %bitcast.270), channel_id=1, source_target_pairs={{0,1},{1,0},{2,3},{3,2},{4,5},{5,4},{6,7},{7,6},{8,9},{9,8},{10,11... | collective-permute-start | bytes 8650760 | tf_op jit(solution)/shard_map/ppermute | solution.py:190
  286.5 53.6 %collective-permute-start.37 = (bf16[704,2048]{1,0:T(8,128)(2,1)}, bf16[704,2048]{1,0:T(8,128)(2,1)}, u32[]{:S(2)}, u32[]{:S(2)}) collective-permute-start(bf16[704,2048]{1,0:T(8,128)(2,1)} %bitcast.275), channel_id=1, source_target_pairs={{0,1},{1,0},{2,3},{3,2},{4,5},{5,4},{6,7},{7,6},{8,9},{9,8},{10,11... | collective-permute-start | bytes 8650760 | tf_op jit(solution)/shard_map/ppermute | solution.py:190
  286.5 53.6 %collective-permute-start.38 = (bf16[704,2048]{1,0:T(8,128)(2,1)}, bf16[704,2048]{1,0:T(8,128)(2,1)}, u32[]{:S(2)}, u32[]{:S(2)}) collective-permute-start(bf16[704,2048]{1,0:T(8,128)(2,1)} %bitcast.280), channel_id=1, source_target_pairs={{0,1},{1,0},{2,3},{3,2},{4,5},{5,4},{6,7},{7,6},{8,9},{9,8},{10,11... | collective-permute-start | bytes 8650760 | tf_op jit(solution)/shard_map/ppermute | solution.py:190
  310.6 342.6 %all-gather.8.cloned.1.call-start = ((), (), s32[]{:S(2)}) async-start(), calls=%async_computation.13 | async-start | bytes 12976128 | tf_op jit(solution)/shard_map/all_gather | solution.py:834
  336.2 33.6 %collective-permute-start.41 = (bf16[2,128,2048]{2,1,0:T(8,128)(2,1)S(1)}, bf16[2,128,2048]{2,1,0:T(8,128)(2,1)S(1)}, u32[]{:S(2)}, u32[]{:S(2)}) collective-permute-start(bf16[2,128,2048]{2,1,0:T(8,128)(2,1)S(1)} %pad_maximum_fusion.6.refs_0_.refs_1_), channel_id=1, source_target_pairs={{0,2},{2,0},{4,6},{6,4},{8,10},{10,8},{12,14},{14,12},{16,18},{18,... | collective-permute-start | bytes 3145736 | tf_op jit(solution)/shard_map/ppermute | solution.py:89
  337.7 32.1 %collective-permute-start.42 = (bf16[2,128,2048]{2,1,0:T(8,128)(2,1)S(1)}, bf16[2,128,2048]{2,1,0:T(8,128)(2,1)}, u32[]{:S(2)}, u32[]{:S(2)}) collective-permute-start(bf16[2,128,2048]{2,1,0:T(8,128)(2,1)S(1)} %pad_maximum_fusion.6.refs_0_.refs_1_), channel_id=1, source_target_pairs={{0,4},{2,6},{4,0},{6,2},{8,12},{10,14},{12,8},{14,10},{16,20},{18,... | collective-permute-start | bytes 3145736 | tf_op jit(solution)/shard_map/ppermute | solution.py:89
  369.8 57.0 %collective-permute-start.43 = (bf16[2,128,2048]{2,1,0:T(8,128)(2,1)}, bf16[2,128,2048]{2,1,0:T(8,128)(2,1)}, u32[]{:S(2)}, u32[]{:S(2)}) collective-permute-start(bf16[2,128,2048]{2,1,0:T(8,128)(2,1)} %get-tuple-element.386), channel_id=1, source_target_pairs={{0,2},{2,0},{4,6},{6,4},{8,10},{10,8},{12,14},{14,12},{16,18},{18,... | collective-permute-start | bytes 3145736 | tf_op jit(solution)/shard_map/ppermute | solution.py:89
  370.5 56.4 %collective-permute-start.44 = (bf16[2,128,2048]{2,1,0:T(8,128)(2,1)}, bf16[2,128,2048]{2,1,0:T(8,128)(2,1)}, u32[]{:S(2)}, u32[]{:S(2)}) collective-permute-start(bf16[2,128,2048]{2,1,0:T(8,128)(2,1)} %get-tuple-element.387), channel_id=1, source_target_pairs={{0,4},{2,6},{4,0},{6,2},{8,12},{10,14},{12,8},{14,10},{16,20},{18,... | collective-permute-start | bytes 3145736 | tf_op jit(solution)/shard_map/ppermute | solution.py:89
  371.0 55.9 %collective-permute-start.45 = (bf16[2,128,2048]{2,1,0:T(8,128)(2,1)}, bf16[2,128,2048]{2,1,0:T(8,128)(2,1)}, u32[]{:S(2)}, u32[]{:S(2)}) collective-permute-start(bf16[2,128,2048]{2,1,0:T(8,128)(2,1)} %get-tuple-element.388), channel_id=1, source_target_pairs={{0,6},{2,4},{4,2},{6,0},{8,14},{10,12},{12,10},{14,8},{16,22},{18,... | collective-permute-start | bytes 3145736 | tf_op jit(solution)/shard_map/ppermute | solution.py:89
  374.5 50.8 %collective-permute-start.46 = (bf16[128,2048]{1,0:T(8,128)(2,1)S(1)}, bf16[128,2048]{1,0:T(8,128)(2,1)S(1)}, u32[]{:S(2)}, u32[]{:S(2)}) collective-permute-start(bf16[128,2048]{1,0:T(8,128)(2,1)S(1)} %slice_bitcast_fusion.9), channel_id=1, source_target_pairs={{0,2},{2,0},{4,6},{6,4},{8,10},{10,8},{12,14},{14,12},{16,18},{18,... | collective-permute-start | bytes 1572872 | tf_op jit(solution)/shard_map/ppermute | solution.py:89
  375.9 50.2 %collective-permute-start.47 = (bf16[128,2048]{1,0:T(8,128)(2,1)}, bf16[128,2048]{1,0:T(8,128)(2,1)S(1)}, u32[]{:S(2)}, u32[]{:S(2)}) collective-permute-start(bf16[128,2048]{1,0:T(8,128)(2,1)} %slice_bitcast_fusion.8), channel_id=1, source_target_pairs={{0,4},{2,6},{4,0},{6,2},{8,12},{10,14},{12,8},{14,10},{16,20},{18,... | collective-permute-start | bytes 1572872 | tf_op jit(solution)/shard_map/ppermute | solution.py:89
  426.9 33.5 %collective-permute-start.48 = (bf16[2,128,2048]{2,1,0:T(8,128)(2,1)}, bf16[2,128,2048]{2,1,0:T(8,128)(2,1)S(1)}, u32[]{:S(2)}, u32[]{:S(2)}) collective-permute-start(bf16[2,128,2048]{2,1,0:T(8,128)(2,1)} %get-tuple-element.453), channel_id=1, source_target_pairs={{0,2},{2,0},{4,6},{6,4},{8,10},{10,8},{12,14},{14,12},{16,18},{18,... | collective-permute-start | bytes 3145736 | tf_op jit(solution)/shard_map/ppermute | solution.py:89
  427.4 37.1 %collective-permute-start.49 = (bf16[2,128,2048]{2,1,0:T(8,128)(2,1)}, bf16[2,128,2048]{2,1,0:T(8,128)(2,1)S(1)}, u32[]{:S(2)}, u32[]{:S(2)}) collective-permute-start(bf16[2,128,2048]{2,1,0:T(8,128)(2,1)} %get-tuple-element.454), channel_id=1, source_target_pairs={{0,4},{2,6},{4,0},{6,2},{8,12},{10,14},{12,8},{14,10},{16,20},{18,... | collective-permute-start | bytes 3145736 | tf_op jit(solution)/shard_map/ppermute | solution.py:89
  429.1 61.2 %collective-permute-start.50 = (bf16[2,128,2048]{2,1,0:T(8,128)(2,1)}, bf16[2,128,2048]{2,1,0:T(8,128)(2,1)}, u32[]{:S(2)}, u32[]{:S(2)}) collective-permute-start(bf16[2,128,2048]{2,1,0:T(8,128)(2,1)} %get-tuple-element.455), channel_id=1, source_target_pairs={{0,6},{2,4},{4,2},{6,0},{8,14},{10,12},{12,10},{14,8},{16,22},{18,... | collective-permute-start | bytes 3145736 | tf_op jit(solution)/shard_map/ppermute | solution.py:89
  490.3 45.1 %collective-permute-start.51 = (bf16[2,128,2048]{2,1,0:T(8,128)(2,1)}, bf16[2,128,2048]{2,1,0:T(8,128)(2,1)S(1)}, u32[]{:S(2)}, u32[]{:S(2)}) collective-permute-start(bf16[2,128,2048]{2,1,0:T(8,128)(2,1)} %get-tuple-element.486), channel_id=1, source_target_pairs={{0,2},{2,0},{4,6},{6,4},{8,10},{10,8},{12,14},{14,12},{16,18},{18,... | collective-permute-start | bytes 3145736 | tf_op jit(solution)/shard_map/ppermute | solution.py:89
  490.7 45.3 %collective-permute-start.52 = (bf16[2,128,2048]{2,1,0:T(8,128)(2,1)}, bf16[2,128,2048]{2,1,0:T(8,128)(2,1)}, u32[]{:S(2)}, u32[]{:S(2)}) collective-permute-start(bf16[2,128,2048]{2,1,0:T(8,128)(2,1)} %get-tuple-element.487), channel_id=1, source_target_pairs={{0,4},{2,6},{4,0},{6,2},{8,12},{10,14},{12,8},{14,10},{16,20},{18,... | collective-permute-start | bytes 3145736 | tf_op jit(solution)/shard_map/ppermute | solution.py:89
  490.7 68.0 %collective-permute-start.53 = (bf16[2,128,2048]{2,1,0:T(8,128)(2,1)}, bf16[2,128,2048]{2,1,0:T(8,128)(2,1)}, u32[]{:S(2)}, u32[]{:S(2)}) collective-permute-start(bf16[2,128,2048]{2,1,0:T(8,128)(2,1)} %get-tuple-element.488), channel_id=1, source_target_pairs={{0,6},{2,4},{4,2},{6,0},{8,14},{10,12},{12,10},{14,8},{16,22},{18,... | collective-permute-start | bytes 3145736 | tf_op jit(solution)/shard_map/ppermute | solution.py:89
  558.6 53.5 %collective-permute-start.54 = (bf16[2,128,2048]{2,1,0:T(8,128)(2,1)}, bf16[2,128,2048]{2,1,0:T(8,128)(2,1)}, u32[]{:S(2)}, u32[]{:S(2)}) collective-permute-start(bf16[2,128,2048]{2,1,0:T(8,128)(2,1)} %get-tuple-element.501), channel_id=1, source_target_pairs={{0,2},{2,0},{4,6},{6,4},{8,10},{10,8},{12,14},{14,12},{16,18},{18,... | collective-permute-start | bytes 3145736 | tf_op jit(solution)/shard_map/ppermute | solution.py:89
  558.6 53.5 %collective-permute-start.55 = (bf16[2,128,2048]{2,1,0:T(8,128)(2,1)}, bf16[2,128,2048]{2,1,0:T(8,128)(2,1)}, u32[]{:S(2)}, u32[]{:S(2)}) collective-permute-start(bf16[2,128,2048]{2,1,0:T(8,128)(2,1)} %get-tuple-element.502), channel_id=1, source_target_pairs={{0,4},{2,6},{4,0},{6,2},{8,12},{10,14},{12,8},{14,10},{16,20},{18,... | collective-permute-start | bytes 3145736 | tf_op jit(solution)/shard_map/ppermute | solution.py:89
  558.7 53.4 %collective-permute-start.56 = (bf16[2,128,2048]{2,1,0:T(8,128)(2,1)}, bf16[2,128,2048]{2,1,0:T(8,128)(2,1)}, u32[]{:S(2)}, u32[]{:S(2)}) collective-permute-start(bf16[2,128,2048]{2,1,0:T(8,128)(2,1)} %get-tuple-element.503), channel_id=1, source_target_pairs={{0,6},{2,4},{4,2},{6,0},{8,14},{10,12},{12,10},{14,8},{16,22},{18,... | collective-permute-start | bytes 3145736 | tf_op jit(solution)/shard_map/ppermute | solution.py:89
  562.1 50.0 %all-to-all-start.4 = ((f32[16,1,128]{2,1,0:T(1,128)}), f32[16,1,128]{2,1,0:T(1,128)S(1)}, u32[]{:S(2)}, u32[]{:S(2)}) async-start(f32[16,1,128]{2,1,0:T(1,128)} %get-tuple-element.512), calls=%async_computation.4 | async-start | bytes 16384 | tf_op jit(solution)/shard_map/all_to_all | solution.py:215
  571.9 131.8 %collective-permute-start.61 = (bf16[128,2048]{1,0:T(8,128)(2,1)}, bf16[128,2048]{1,0:T(8,128)(2,1)}, u32[]{:S(2)}, u32[]{:S(2)}) collective-permute-start(bf16[128,2048]{1,0:T(8,128)(2,1)} %get-tuple-element.717), channel_id=1, source_target_pairs={{0,16},{2,18},{4,20},{6,22},{8,24},{10,26},{12,28},{14,30},{16,0},... | collective-permute-start | bytes 1572872 | tf_op jit(solution)/shard_map/ppermute | solution.py:89
  574.3 129.5 %collective-permute-start.62 = (bf16[128,2048]{1,0:T(8,128)(2,1)}, bf16[128,2048]{1,0:T(8,128)(2,1)}, u32[]{:S(2)}, u32[]{:S(2)}) collective-permute-start(bf16[128,2048]{1,0:T(8,128)(2,1)} %get-tuple-element.716), channel_id=1, source_target_pairs={{0,24},{2,26},{4,28},{6,30},{8,16},{10,18},{12,20},{14,22},{16,8},... | collective-permute-start | bytes 1572872 | tf_op jit(solution)/shard_map/ppermute | solution.py:89
  618.0 34.4 %collective-permute-start.59 = (bf16[128,2048]{1,0:T(8,128)(2,1)S(1)}, bf16[128,2048]{1,0:T(8,128)(2,1)S(1)}, u32[]{:S(2)}, u32[]{:S(2)}) collective-permute-start(bf16[128,2048]{1,0:T(8,128)(2,1)S(1)} %get-tuple-element.718), channel_id=1, source_target_pairs={{0,24},{2,26},{4,28},{6,30},{8,16},{10,18},{12,20},{14,22},{16,8},... | collective-permute-start | bytes 1572872 | tf_op jit(solution)/shard_map/ppermute | solution.py:89
  620.5 32.7 %collective-permute-start.57 = (bf16[128,2048]{1,0:T(8,128)(2,1)S(1)}, bf16[128,2048]{1,0:T(8,128)(2,1)}, u32[]{:S(2)}, u32[]{:S(2)}) collective-permute-start(bf16[128,2048]{1,0:T(8,128)(2,1)S(1)} %fusion.27), channel_id=1, source_target_pairs={{0,8},{2,10},{4,12},{6,14},{8,0},{10,2},{12,4},{14,6},{16,24},{18,... | collective-permute-start | bytes 1572872 | tf_op jit(solution)/shard_map/ppermute | solution.py:89
  673.3 45.6 %collective-permute-start.65 = (bf16[704,2048]{1,0:T(8,128)(2,1)}, bf16[704,2048]{1,0:T(8,128)(2,1)}, u32[]{:S(2)}, u32[]{:S(2)}) collective-permute-start(bf16[704,2048]{1,0:T(8,128)(2,1)} %convolution_convert_fusion.1), channel_id=1, source_target_pairs={{0,1},{1,0},{2,3},{3,2},{4,5},{5,4},{6,7},{7,6},{8,9},{9,8},{10,11... | collective-permute-start | bytes 8650760 | tf_op jit(solution)/shard_map/ppermute | solution.py:190
  674.4 29.4 %collective-permute-start.60 = (bf16[128,2048]{1,0:T(8,128)(2,1)}, bf16[128,2048]{1,0:T(8,128)(2,1)}, u32[]{:S(2)}, u32[]{:S(2)}) collective-permute-start(bf16[128,2048]{1,0:T(8,128)(2,1)} %fusion.28), channel_id=1, source_target_pairs={{0,8},{2,10},{4,12},{6,14},{8,0},{10,2},{12,4},{14,6},{16,24},{18,... | collective-permute-start | bytes 1572872 | tf_op jit(solution)/shard_map/ppermute | solution.py:89
  674.8 51.6 %collective-permute-start.64 = (bf16[704,2048]{1,0:T(8,128)(2,1)}, bf16[704,2048]{1,0:T(8,128)(2,1)}, u32[]{:S(2)}, u32[]{:S(2)}) collective-permute-start(bf16[704,2048]{1,0:T(8,128)(2,1)} %convolution_convert_fusion.2), channel_id=1, source_target_pairs={{0,1},{1,0},{2,3},{3,2},{4,5},{5,4},{6,7},{7,6},{8,9},{9,8},{10,11... | collective-permute-start | bytes 8650760 | tf_op jit(solution)/shard_map/ppermute | solution.py:190
  708.1 56.4 %all-to-all-start.6 = ((bf16[16,128,576]{1,2,0:T(8,128)(2,1)}), bf16[16,128,576]{1,2,0:T(8,128)(2,1)}, u32[]{:S(2)}, u32[]{:S(2)}) async-start(bf16[16,128,576]{1,2,0:T(8,128)(2,1)} %copy.316), calls=%async_computation.6 | async-start | bytes 4718592 | tf_op jit(solution)/shard_map/all_to_all | solution.py:215
  713.9 226.7 %reduce-scatter.2.cloned.1.call-start = ((), (), s32[]{:S(2)}) async-start(), calls=%async_computation.14 | async-start | bytes 4456448 | tf_op jit(solution)/shard_map/reduce_scatter | solution.py:869
  718.4 70.0 %collective-permute-start.68 = (bf16[1024,2048]{1,0:T(8,128)(2,1)}, bf16[1024,2048]{1,0:T(8,128)(2,1)}, u32[]{:S(2)}, u32[]{:S(2)}) collective-permute-start(bf16[1024,2048]{1,0:T(8,128)(2,1)} %convolution_convert_fusion), channel_id=1, source_target_pairs={{0,1},{1,0},{2,3},{3,2},{4,5},{5,4},{6,7},{7,6},{8,9},{9,8},{10,11... | collective-permute-start | bytes 12582920 | tf_op jit(solution)/shard_map/ppermute | solution.py:190
  803.1 50.4 %all-to-all-start.7 = ((bf16[16,64,608]{2,1,0:T(8,128)(2,1)}), bf16[16,64,608]{2,1,0:T(8,128)(2,1)}, u32[]{:S(2)}, u32[]{:S(2)}) async-start(bf16[16,64,608]{2,1,0:T(8,128)(2,1)} %fusion.3), calls=%async_computation.7 | async-start | bytes 2621440 | tf_op jit(solution)/shard_map/all_to_all | solution.py:215
  829.1 35.3 %collective-permute-start.66 = (bf16[16,64,640]{2,1,0:T(8,128)(2,1)}, bf16[16,64,640]{2,1,0:T(8,128)(2,1)}, u32[]{:S(2)}, u32[]{:S(2)}) collective-permute-start(bf16[16,64,640]{2,1,0:T(8,128)(2,1)} %select_bitcast_fusion), channel_id=1, source_target_pairs={{0,1},{1,0},{2,3},{3,2},{4,5},{5,4},{6,7},{7,6},{8,9},{9,8},{10,11... | collective-permute-start | bytes 3932168 | tf_op jit(solution)/shard_map/ppermute | solution.py:190
  853.5 34.2 %all-to-all-start.8 = ((bf16[16,128,192]{1,2,0:T(8,128)(2,1)}), bf16[16,128,192]{1,2,0:T(8,128)(2,1)S(1)}, u32[]{:S(2)}, u32[]{:S(2)}) async-start(bf16[16,128,192]{1,2,0:T(8,128)(2,1)} %copy.324), calls=%async_computation.8 | async-start | bytes 1572864 | tf_op jit(solution)/shard_map/all_to_all | solution.py:215
  863.5 30.4 %collective-permute-start.69 = (bf16[88,2048]{1,0:T(8,128)(2,1)}, bf16[88,2048]{1,0:T(8,128)(2,1)}, u32[]{:S(2)}, u32[]{:S(2)}) collective-permute-start(bf16[88,2048]{1,0:T(8,128)(2,1)} %select_convert_fusion.1), channel_id=1, source_target_pairs={{0,1},{1,0},{2,3},{3,2},{4,5},{5,4},{6,7},{7,6},{8,9},{9,8},{10,11... | collective-permute-start | bytes 1081352 | tf_op jit(solution)/shard_map/ppermute | solution.py:190
  887.7 44.0 %all-to-all-start.9 = ((bf16[16,64,640]{2,1,0:T(8,128)(2,1)}), bf16[16,64,640]{2,1,0:T(8,128)(2,1)}, u32[]{:S(2)}, u32[]{:S(2)}) async-start(bf16[16,64,640]{2,1,0:T(8,128)(2,1)} %fusion.2), calls=%async_computation.9 | async-start | bytes 2621440 | tf_op jit(solution)/shard_map/all_to_all | solution.py:215
  (127 other events, 2122.0 us)
Sparse Core Ops, SparseCore 0:
  13.0 81.2 all-gather.3
  97.2 105.2 all-gather.5
  427.0 137.8 all-gather.7
  794.0 132.8 reduce-scatter.1
